TPU v7x, 32 devices: a whole 2x2x4 slice. The times are simulated.
32 devices in a mesh: grp: 2 (over y), row: 4 (over z), col: 4 (over x, core).
Axes of the slice: x: 2, y: 2, z: 4, core: 2. Of those that a mesh axis runs over, the one named last changes fastest.
Arguments:
- pair: float32 [80, 40, 128], P(('grp', 'row'), 'col'), parts along dimension 0, may hold values from -6 to 6
- pair_mask: int32 [80, 40], P(('grp', 'row'), 'col'), parts along dimension 0, may hold values 0 or 1
- out_proj: float32 [128, 512], replicated, may hold values from -0.5 to 0.5
- out_gate: float32 [128, 128], replicated, may hold values from -0.5 to 0.5
- out_final: float32 [128, 128], replicated, may hold values from -0.5 to 0.5
- in_proj: float32 [128, 512], replicated, may hold values from -0.5 to 0.5
- in_gate: float32 [128, 128], replicated, may hold values from -0.5 to 0.5
- in_final: float32 [128, 128], replicated, may hold values from -0.5 to 0.5
Outputs:
- new_pair: float32 [80, 40, 128], P(('grp', 'row'), 'col'), parts along dimension 0
There are 2 independent parts, one for each index of `grp`. A program takes and returns all parts, laid end to end along the dimension named above; an argument that names none is the same for every part. Nothing has to cross between parts.
All inputs are finite; a program needn't handle non-finite values. No bound on the sum of `pair_mask` on one device may be relied on, other than what follows from the above.
Results may differ from a plain program's by a relative error of at most 0.0075.
Values may be sent and summed in bfloat16 or wider, within the bound.
No kernel may reach another device: no remote copies, remote signals or barrier semaphores. Data moves between devices by JAX's collectives and lax.ppermute only.
A program may use at most 64 MiB of HBM per device.

v0:
```python
import jax
import jax.numpy as jnp
from jax import lax
from jax.sharding import PartitionSpec as P


def layer_norm(value):
    mean = jnp.mean(value, axis=-1, keepdims=True)
    centred = value - mean
    variance = jnp.mean(centred * centred, axis=-1, keepdims=True)
    return centred * lax.rsqrt(variance + 1e-05)


def project(pair, pair_mask, proj_weight, gate_weight):
    normed = layer_norm(pair)
    proj = jnp.einsum("ijc,cd->ijd", normed, proj_weight, precision=lax.Precision.HIGHEST)
    hidden = proj_weight.shape[1] // 4
    valid = pair_mask.astype(jnp.float32)[:, :, None]
    left = jax.nn.sigmoid(proj[..., :hidden]) * proj[..., hidden : 2 * hidden] * valid
    right = jax.nn.sigmoid(proj[..., 2 * hidden : 3 * hidden]) * proj[..., 3 * hidden :] * valid
    gate = jax.nn.sigmoid(
        jnp.einsum("ijc,cd->ijd", normed, gate_weight, precision=lax.Precision.HIGHEST)
    )
    left = jnp.transpose(left.astype(jnp.bfloat16), (2, 0, 1))
    right = jnp.transpose(right.astype(jnp.bfloat16), (2, 0, 1))
    return (left, right, gate)


def finish(pair, summed, gate, final_weight):
    normed = layer_norm(jnp.transpose(summed, (1, 2, 0)))
    return pair + gate * jnp.einsum(
        "ijh,hc->ijc", normed, final_weight, precision=lax.Precision.HIGHEST
    )


def body(pair, pair_mask, out_proj, out_gate, out_final, in_proj, in_gate, in_final):
    left, right, gate = project(pair, pair_mask, out_proj, out_gate)
    outer_terms = jnp.einsum(
        "hik,hjk->hij",
        left,
        lax.all_gather(right, "row", axis=1, tiled=True),
        preferred_element_type=jnp.float32,
    )
    outer = lax.psum_scatter(
        outer_terms.astype(jnp.bfloat16), "col", scatter_dimension=2, tiled=True
    ).astype(jnp.float32)
    middle = finish(pair, outer, gate, out_final)
    left2, right2, gate2 = project(middle, pair_mask, in_proj, in_gate)
    inner_terms = jnp.einsum(
        "hki,hkj->hij",
        lax.all_gather(left2, "col", axis=2, tiled=True),
        right2,
        preferred_element_type=jnp.float32,
    )
    inner = lax.psum_scatter(
        inner_terms.astype(jnp.bfloat16), "row", scatter_dimension=1, tiled=True
    ).astype(jnp.float32)
    return finish(middle, inner, gate2, in_final)


def solution(mesh):
    return jax.shard_map(
        body,
        mesh=mesh,
        in_specs=(
            P(("grp", "row"), "col", None),
            P(("grp", "row"), "col"),
            P(),
            P(),
            P(),
            P(),
            P(),
            P(),
        ),
        out_specs=P(("grp", "row"), "col", None),
        check_vma=False,
    )
```

profile of v0, /device:TPU:0, one launch (start us, length us, event | category | flops | bytes accessed | tf_op | source)
XLA Modules:
  0.0 93.6 jit_solution(14190614982025493989)
XLA Ops:
  6.5 0.0 copy-start
  6.5 0.0 reduce-scatter.3.cloned.1.call-start
  6.5 1.0 %reduce_sum.72 = f32[10,10]{1,0:T(8,128)S(1)} reduce(f32[10,10,128]{2,1,0:T(8,128)} %param.8, f32[]{:T(128)} %constant.13.clone.1), dimensions={2}, to_apply=%region_0.0 | reduce | flops 12700 | bytes 51604 | tf_op jit(solution)/shard_map/reduce_sum | solution.py:8
  7.6 1.1 %multiply_reduce_fusion.1 = f32[10,10]{1,0:T(8,128)S(1)} fusion(f32[10,10,128]{2,1,0:T(8,128)} %param.8, f32[10,10]{1,0:T(8,128)S(1)} %broadcast_multiply_fusion.3), kind=kLoop, calls=%fused_computation.58 | loop fusion | flops 38300 | bytes 52000 | tf_op jit(solution)/shard_map/reduce_sum | solution.py:10
  8.7 0.7 convert_element_type.24
  9.4 0.0 copy-done
  9.4 1.3 %fusion.10 = f32[10,10,512]{2,1,0:T(8,128)S(1)} fusion(f32[128,512]{1,0:T(8,128)S(1)} %copy-done, f32[10,10,128]{2,1,0:T(8,128)} %param.8, f32[10,10]{1,0:T(8,128)S(1)} %add_rsqrt_fusion.3, f32[10,10]{1,0:T(8,128)S(1)} %broadcast_multiply_fusion.3), kind=kOutput, calls=%fused_computation.16 | convolution fusion | flops 78668800 | bytes 518944 | tf_op jit(solution)/shard_map/ijc,cd->ijd/dot_general | solution.py:16
  10.7 0.1 fusion.63
  10.8 15.1 %all_gather.6 = bf16[128,40,10]{0,2,1:T(8,128)(2,1)S(1)} all-gather(bf16[128,10,10]{0,2,1:T(8,128)(2,1)S(1)} %get-tuple-element.7), channel_id=1, replica_groups=mesh['grp'=2,'row'=4,'col'=4] {'row'}, dimensions={1}, use_global_device_ids=true | all-gather | bytes 128000 | tf_op jit(solution)/shard_map/all_gather | solution.py:41
  26.0 0.7 copy.40
  26.7 0.5 copy.39
  27.1 0.0 copy-start.1
  27.1 0.0 copy-start.5
  27.2 0.8 convolution_convert_fusion.1
  27.9 0.0 copy-start.2
  28.0 1.2 %copy.41 = bf16[128,10,40]{0,1,2:T(8,128)(2,1)} copy(bf16[128,10,40]{2,1,0:T(8,128)(2,1)S(1)} %convolution_convert_fusion.1) | data formatting | bytes 204800 | tf_op jit(solution)/shard_map/convert_element_type | solution.py:45
  29.1 0.0 reduce-scatter.3.cloned.1.call-update
  29.2 0.0 reduce-scatter.5.cloned.1.call-start
  29.2 0.0 copy-done.1
  29.2 0.0 copy-done.5
  29.2 0.3 fusion.7
  29.5 20.9 %reduce-scatter.3.cloned.1.call-done = bf16[128,10,10]{0,1,2:T(8,128)(2,1)} async-done(((bf16[128,10,40]{0,1,2:T(8,128)(2,1)}), bf16[128,10,10]{0,1,2:T(8,128)(2,1)}) %reduce-scatter.3.cloned.1.call-update) | async-done | bytes 25616 | tf_op jit(solution)/shard_map/reduce_scatter | solution.py:44
  50.5 0.9 bitcast_reduce_fusion.1
  51.3 0.1 copy.42
  51.4 0.1 copy.43
  51.5 1.0 %fusion.38 = f32[10,10]{0,1:T(8,128)S(1)} fusion(bf16[128,10,10]{0,1,2:T(8,128)(2,1)} %reduce-scatter.3.cloned.1.call-done, f32[10,10]{0,1:T(8,128)S(1)} %copy.43), kind=kLoop, calls=%fused_computation.55 | loop fusion | flops 51100 | bytes 26400 | tf_op jit(solution)/shard_map/reduce_sum | solution.py:10
  52.5 0.1 copy.44
  52.6 0.1 copy.45
  52.7 0.9 fusion.36
  53.6 0.0 copy-done.3
  53.6 0.3 fusion.66
  53.9 0.2 multiply_reduce_fusion
  54.1 0.0 copy-done.2
  54.1 0.5 fusion.8
  54.6 0.1 fusion.65
  54.7 5.5 %all_gather.7 = bf16[128,10,40]{0,1,2:T(8,128)(2,1)S(1)} all-gather(bf16[128,10,10]{0,1,2:T(8,128)(2,1)S(1)} %copy.47), channel_id=1, replica_groups=mesh['grp'=2,'row'=4,'col'=4] {'col'}, dimensions={2}, use_global_device_ids=true | all-gather | bytes 128000 | tf_op jit(solution)/shard_map/all_gather | solution.py:51
  60.2 0.7 copy.48
  60.9 0.5 copy.49
  61.4 0.8 convolution_convert_fusion
  62.2 0.0 copy-start.6
  62.2 0.0 copy-start.4
  62.2 1.4 %copy.50 = bf16[128,40,10]{0,2,1:T(8,128)(2,1)} copy(bf16[128,40,10]{2,1,0:T(8,128)(2,1)S(1)} %convolution_convert_fusion) | data formatting | bytes 204800 | tf_op jit(solution)/shard_map/convert_element_type | solution.py:56
  63.7 0.0 reduce-scatter.5.cloned.1.call-update
  63.7 0.3 fusion.3
  64.0 19.2 %reduce-scatter.5.cloned.1.call-done = bf16[128,10,10]{0,2,1:T(8,128)(2,1)} async-done(((bf16[128,40,10]{0,2,1:T(8,128)(2,1)}), bf16[128,10,10]{0,2,1:T(8,128)(2,1)}) %reduce-scatter.5.cloned.1.call-update) | async-done | bytes 25616 | tf_op jit(solution)/shard_map/reduce_scatter | solution.py:55
  83.2 0.9 bitcast_reduce_fusion
  84.0 1.0 %fusion.34 = f32[10,10]{1,0:T(8,128)S(1)} fusion(bf16[128,10,10]{0,2,1:T(8,128)(2,1)} %reduce-scatter.5.cloned.1.call-done, f32[10,10]{1,0:T(8,128)S(1)} %broadcast_multiply_fusion), kind=kLoop, calls=%fused_computation.50 | loop fusion | flops 51100 | bytes 26400 | tf_op jit(solution)/shard_map/reduce_sum | solution.py:10
  85.0 1.7 %fusion = f32[10,10,128]{2,1,0:T(8,128)} fusion(f32[10,10,128]{2,1,0:T(8,128)S(1)} %get-tuple-element.10, f32[10,10,128]{2,1,0:T(8,128)S(1)} %fusion.3, bf16[128,10,10]{0,2,1:T(8,128)(2,1)} %reduce-scatter.5.cloned.1.call-done, f32[128,128]{1,0:T(8,128)S(1)} %copy-done.4, f32[10,10]{1,0:T(8,128)S(1)} %add_rsqrt_fusion, f32[10,10]{1,0:T(8,128)S(1)} %broadcast_multiply_fusion), kind=kOutput, calls=%fused_computation.3 | convolution fusion | flops 19724800 | bytes 245536 | tf_op jit(solution)/shard_map/ijh,hc->ijc/dot_general | solution.py:31
  (12 shorter events, 0.1 us)
Async XLA Ops:
  6.5 2.8 %copy-start = (f32[128,512]{1,0:T(8,128)S(1)}, f32[128,512]{1,0:T(8,128)}, u32[]{:S(2)}) copy-start(f32[128,512]{1,0:T(8,128)} %param.10) | copy-start | bytes 786436
  6.5 43.9 %reduce-scatter.3.cloned.1.call-start = ((), (), s32[]{:S(2)}) async-start(), calls=%async_computation.2 | async-start | bytes 204800 | tf_op jit(solution)/shard_map/reduce_scatter | solution.py:44
  27.1 2.1 %copy-start.1 = (f32[10,10,128]{2,1,0:T(8,128)S(1)}, f32[10,10,128]{2,1,0:T(8,128)}, u32[]{:S(2)}) copy-start(f32[10,10,128]{2,1,0:T(8,128)} %param.8) | copy-start | bytes 153604
  27.1 2.1 %copy-start.5 = (f32[128,128]{1,0:T(8,128)S(1)}, f32[128,128]{1,0:T(8,128)}, u32[]{:S(2)}) copy-start(f32[128,128]{1,0:T(8,128)} %param.11) | copy-start | bytes 196612
  27.9 25.7 %copy-start.3 = (f32[128,128]{1,0:T(8,128)S(1)}, f32[128,128]{1,0:T(8,128)}, u32[]{:S(2)}) copy-start(f32[128,128]{1,0:T(8,128)} %param.12) | copy-start | bytes 196612
  27.9 26.2 %copy-start.2 = (f32[128,512]{1,0:T(8,128)S(1)}, f32[128,512]{1,0:T(8,128)}, u32[]{:S(2)}) copy-start(f32[128,512]{1,0:T(8,128)} %param.13) | copy-start | bytes 786436
  29.2 54.0 %reduce-scatter.5.cloned.1.call-start = ((), (), s32[]{:S(2)}) async-start(), calls=%async_computation.3 | async-start | bytes 204800 | tf_op jit(solution)/shard_map/reduce_scatter | solution.py:55
  62.2 1.5 %copy-start.6 = (f32[128,128]{1,0:T(8,128)S(1)}, f32[128,128]{1,0:T(8,128)}, u32[]{:S(2)}) copy-start(f32[128,128]{1,0:T(8,128)} %param.14) | copy-start | bytes 196612
  62.2 22.8 %copy-start.4 = (f32[128,128]{1,0:T(8,128)S(1)}, f32[128,128]{1,0:T(8,128)}, u32[]{:S(2)}) copy-start(f32[128,128]{1,0:T(8,128)} %param.15) | copy-start | bytes 196612
Sparse Core Ops, SparseCore 0:
  29.3 21.1 reduce-scatter.2
  63.8 19.2 reduce-scatter.4
where the time goes:
time: 94.2 us; the launch traced here: 93.6 us
  waiting for transfers between devices  40.1 us (43%)
  blocking collectives  20.7 us (22%)
  between operations  13.7 us (15%)
  other arithmetic  7.72 us (8%)
  matrix products  5.98 us (6%)
  local copies, waits for them, and re-layouts  5.35 us (6%)
    reduce_scatter x1, waiting for transfers between devices, body(): lax.psum_scatter(outer_terms.astype(jnp.bfloat16), 'col', scatter_dimensi...  20.9 us
    reduce_scatter x1, waiting for transfers between devices, body(): lax.psum_scatter(inner_terms.astype(jnp.bfloat16), 'row', scatter_dimensi...  19.2 us
    all_gather x1, blocking collectives, body(): lax.all_gather(right, 'row', axis=1, tiled=True)  15.1 us
    all_gather x1, blocking collectives, body(): lax.all_gather(left2, 'col', axis=2, tiled=True)  5.52 us
    reduce_sum x4, other arithmetic, layer_norm(): variance = jnp.mean(centred * centred, axis=-1, keepdims=True)  3.14 us
    reduce_sum x3, other arithmetic, layer_norm(): mean = jnp.mean(value, axis=-1, keepdims=True)  2.76 us
    dot_general x2, matrix products, finish(): jnp.einsum('ijh,hc->ijc', normed, final_weight, precision=lax.Precision.H...  1.99 us
  transfers between devices with their start and end apart: 2, of which 2 were waited for; matrix products, arithmetic and copies ran while one was open for 1% of the time, Pallas kernels for 0%

commit v1 on v0

--- a/solution.py
+++ b/solution.py
@@ -1,7 +1,17 @@
 import jax
 import jax.numpy as jnp
 from jax import lax
+from jax.experimental import pallas as pl
+from jax.experimental.pallas import tpu as pltpu
 from jax.sharding import PartitionSpec as P
+
+MASKED = 64.0
+SPLIT = 4
+SIDE = 10
+MAIN = 8
+REST = SIDE - MAIN
+ROWS = 112
+WIDTH = SIDE * SPLIT
 
 
 def layer_norm(value):
@@ -33,7 +43,7 @@
     )
 
 
-def body(pair, pair_mask, out_proj, out_gate, out_final, in_proj, in_gate, in_final):
+def split_plan(pair, pair_mask, out_proj, out_gate, out_final, in_proj, in_gate, in_final):
     left, right, gate = project(pair, pair_mask, out_proj, out_gate)
     outer_terms = jnp.einsum(
         "hik,hjk->hij",
@@ -58,7 +68,212 @@
     return finish(middle, inner, gate2, in_final)
 
 
+def sigmoid(value):
+    return 0.5 * jnp.tanh(0.5 * value) + 0.5
+
+
+def dot(value, weight):
+    return jnp.dot(value.astype(jnp.bfloat16), weight, preferred_element_type=jnp.float32)
+
+
+def scaled(centred):
+    return centred * lax.rsqrt(jnp.mean(centred * centred, axis=-1, keepdims=True) + 1e-05)
+
+
+def rest_rows(k):
+    return 80 + 16 * k
+
+
+def pack_kernel(pair_ref, mask_ref, tile_ref, own_ref, send_ref):
+    own_ref[...] = jnp.zeros(own_ref.shape, own_ref.dtype)
+    send_ref[...] = jnp.zeros(send_ref.shape, send_ref.dtype)
+    valid = mask_ref[...]
+    for k in range(SIDE):
+        rows = pair_ref[:, k, :]
+        centred = rows - jnp.mean(rows, axis=-1, keepdims=True)
+        sent = jnp.where(valid[:, k : k + 1] > 0, centred, MASKED)
+        own_ref[pl.ds(MAIN * k, MAIN), :] = rows[:MAIN]
+        send_ref[pl.ds(MAIN * k, MAIN), :] = sent[:MAIN]
+        for e in range(REST):
+            own_ref[pl.ds(rest_rows(e) + k, 1), :] = rows[MAIN + e : MAIN + e + 1]
+            send_ref[pl.ds(rest_rows(e) + k, 1), :] = sent[MAIN + e : MAIN + e + 1]
+    tile_ref[...] = send_ref[...].astype(tile_ref.dtype)
+
+
+def to_lines(target, base, tile, slot, slots, line):
+    for k in range(SIDE):
+        target[pl.ds(base + line * k + MAIN * slot, MAIN), :] = tile[MAIN * k : MAIN * (k + 1)]
+    for e in range(REST):
+        target[pl.ds(base + MAIN * slots + REST * slot + e, SIDE, stride=line), :] = tile[
+            rest_rows(e) : rest_rows(e) + SIDE
+        ]
+
+
+def update_kernel(
+    near_ref, far_ref, own_ref, out_proj_ref, out_gate_ref, out_final_ref, in_proj_ref, in_gate_ref, in_final_ref,
+    result_ref,
+    lines_ref, right_lines_ref, left_ref, right_ref, outer_ref, mid_ref, pieces_ref, flat_ref,
+):
+    bf16 = jnp.bfloat16
+    row, col = lax.axis_index("row"), lax.axis_index("col")
+    other = jnp.bitwise_xor(row, col)
+    length = SIDE * WIDTH
+    right_line = 24
+    own = own_ref[...]
+    own_centred = own - jnp.mean(own, axis=-1, keepdims=True)
+
+    out_proj = out_proj_ref[...].astype(bf16)
+    for part in range(SPLIT):
+        source, place = (near_ref, far_ref)[part % 2], SPLIT * (part // 2)
+        for slot in range(SPLIT):
+            to_lines(lines_ref, part * length, source[place + slot].astype(jnp.float32), slot, SPLIT, WIDTH)
+        to_lines(right_lines_ref, 0, source[place].astype(jnp.float32), 0, 2, right_line)
+        to_lines(right_lines_ref, 0, source[place + other].astype(jnp.float32), 1, 2, right_line)
+        raw = lines_ref[pl.ds(part * length, length), :]
+        valid = raw < 0.5 * MASKED
+        normed = scaled(jnp.where(valid, raw, 0.0))
+        proj = dot(normed, out_proj[:, :256])
+        left_ref[pl.ds(part * length, length), :] = sigmoid(proj[:, :128]) * proj[:, 128:]
+        raw = right_lines_ref[...]
+        normed = scaled(jnp.where(raw < 0.5 * MASKED, raw, 0.0))
+        proj = dot(normed, out_proj[:, 256:])
+        right_ref[pl.ds(part * SIDE * right_line, SIDE * right_line), :] = sigmoid(proj[:, :128]) * proj[:, 128:]
+
+    group = 4
+
+    def outer_step(g, carry):
+        def add(k, sums):
+            rows = left_ref[pl.ds(pl.multiple_of(k * WIDTH, 8), WIDTH), :]
+            new = []
+            for jj in range(group):
+                one = right_ref[pl.ds(k * right_line + g * group + jj, 1), :]
+                new.append(sums[jj] + rows * jnp.broadcast_to(one, rows.shape))
+            return tuple(new)
+
+        sums = lax.fori_loop(
+            0, WIDTH, add, tuple(jnp.zeros((WIDTH, 128), jnp.float32) for _ in range(group)), unroll=4
+        )
+        for jj in range(group):
+            outer_ref[pl.ds(pl.multiple_of((g * group + jj) * WIDTH, 8), WIDTH), :] = sums[jj]
+        return carry
+
+    lax.fori_loop(0, 2 * SIDE // group, outer_step, 0)
+
+    out_gate = out_gate_ref[...].astype(bf16)
+    out_final = out_final_ref[...].astype(bf16)
+    in_proj = in_proj_ref[...].astype(bf16)
+    for block in range(2):
+        start = pl.multiple_of(other * length, 8) if block == 1 else 0
+        raw = lines_ref[pl.ds(start, length), :]
+        valid = raw < 0.5 * MASKED
+        centred = jnp.where(valid, raw, 0.0)
+        if block == 0:
+            mid_ref[pl.ds(0, length), :] = centred
+            for k in range(SIDE):
+                mid_ref[pl.ds(WIDTH * k, MAIN), :] = own_centred[MAIN * k : MAIN * (k + 1)]
+            for e in range(REST):
+                mid_ref[pl.ds(MAIN * SPLIT + e, SIDE, stride=WIDTH), :] = own_centred[rest_rows(e) : rest_rows(e) + SIDE]
+            centred = mid_ref[pl.ds(0, length), :]
+        gate = sigmoid(dot(scaled(centred), out_gate))
+        from_slot = 1 - block
+        summed = jnp.concatenate(
+            [outer_ref[pl.ds(from_slot * MAIN * WIDTH, MAIN * WIDTH), :],
+             outer_ref[pl.ds((2 * MAIN + REST * from_slot) * WIDTH, REST * WIDTH), :]], axis=0)
+        change = gate * dot(layer_norm(summed), out_final)
+        mid = centred + change
+        normed = layer_norm(mid)
+        proj = dot(normed, in_proj[:, 256:] if block == 0 else in_proj[:, :256])
+        value = jnp.where(valid, sigmoid(proj[:, :128]) * proj[:, 128:], 0.0)
+        if block == 0:
+            right_ref[pl.ds(0, length), :] = value
+            mid_ref[pl.ds(0, length), :] = change
+            mid_ref[pl.ds(length, length), :] = normed
+        else:
+            left_ref[pl.ds(0, length), :] = value
+
+    def inner_step(j, carry):
+        right = right_ref[pl.ds(pl.multiple_of(j * WIDTH, 8), WIDTH), :]
+        for i in range(SIDE):
+            product = left_ref[pl.ds(i * WIDTH, WIDTH), :] * right
+            folded = product[:8]
+            for t in range(1, WIDTH // 8):
+                folded = folded + product[8 * t : 8 * (t + 1)]
+            at = MAIN * j + i if i < MAIN else rest_rows(i - MAIN) + j
+            pieces_ref[pl.ds(pl.multiple_of(8 * at, 8), 8), :] = folded
+        return carry
+
+    lax.fori_loop(0, SIDE, inner_step, 0)
+    inner = pieces_ref[pl.ds(0, ROWS, stride=8), :]
+    for t in range(1, 8):
+        inner = inner + pieces_ref[pl.ds(t, ROWS, stride=8), :]
+
+    def own_rows(base):
+        for k in range(SIDE):
+            flat_ref[pl.ds(MAIN * k, MAIN), :] = mid_ref[pl.ds(base + WIDTH * k, MAIN), :]
+        for e in range(REST):
+            flat_ref[pl.ds(rest_rows(e), SIDE), :] = mid_ref[pl.ds(base + MAIN * SPLIT + e, SIDE, stride=WIDTH), :]
+        return flat_ref[...]
+
+    mid = own + own_rows(0)
+    gate = sigmoid(dot(own_rows(length), in_gate_ref[...].astype(bf16)))
+    result = mid + gate * dot(layer_norm(inner), in_final_ref[...].astype(bf16))
+    for k in range(SIDE):
+        result_ref[pl.ds(0, MAIN), k, :] = result[MAIN * k : MAIN * (k + 1)]
+        for e in range(REST):
+            result_ref[MAIN + e, pl.ds(k, 1), :] = result[rest_rows(e) + k : rest_rows(e) + k + 1]
+
+
+def swapped(value, rows, cols):
+    pairs = [
+        (r * SPLIT + c, (r ^ rows) * SPLIT + (c ^ cols)) for r in range(SPLIT) for c in range(SPLIT)
+    ]
+    return lax.ppermute(value, ("row", "col"), pairs)
+
+
+def in_vmem(value):
+    return pltpu.with_memory_space_constraint(value, pltpu.VMEM)
+
+
+def compact_plan(pair, pair_mask, out_proj, out_gate, out_final, in_proj, in_gate, in_final):
+    f32 = jnp.float32
+    tile, own = pl.pallas_call(
+        pack_kernel,
+        out_shape=(pltpu.VMEM((ROWS, 128), jnp.bfloat16), pltpu.VMEM((ROWS, 128), f32)),
+        scratch_shapes=[pltpu.VMEM((ROWS, 128), f32)],
+        name="pack",
+    )(pair, pair_mask)
+    along_row = [swapped(tile, s, 0) for s in (3, 2, 1)]
+    column = jnp.stack([tile] + along_row[::-1])
+    near = jnp.concatenate([column, swapped(column, 0, 2)])
+    far = swapped(near, 0, 1)
+    length = SIDE * WIDTH
+    return pl.pallas_call(
+        update_kernel,
+        out_shape=jax.ShapeDtypeStruct(pair.shape, f32),
+        scratch_shapes=[
+            pltpu.VMEM((SPLIT * length, 128), f32),
+            pltpu.VMEM((SIDE * 24, 128), f32),
+            pltpu.VMEM((SPLIT * length, 128), f32),
+            pltpu.VMEM((SPLIT * SIDE * 24, 128), f32),
+            pltpu.VMEM((2 * length, 128), f32),
+            pltpu.VMEM((2 * length, 128), f32),
+            pltpu.VMEM((8 * ROWS, 128), f32),
+            pltpu.VMEM((ROWS, 128), f32),
+        ],
+        compiler_params=pltpu.CompilerParams(vmem_limit_bytes=32 << 20),
+        name="update",
+    )(in_vmem(near), in_vmem(far), in_vmem(own), *map(in_vmem, (out_proj, out_gate, out_final, in_proj, in_gate, in_final)))
+
+
 def solution(mesh):
+    def body(pair, *rest):
+        compact = (
+            mesh.shape["row"] == mesh.shape["col"] == SPLIT
+            and pair.shape == (SIDE, SIDE, 128)
+            and rest[1].shape == (128, 512)
+        )
+        return (compact_plan if compact else split_plan)(pair, *rest)
+
     return jax.shard_map(
         body,
         mesh=mesh,

time: 94.2 us -> 23.7 us (0.25)
  waiting for transfers between devices: 40.1 us -> 10.4 us
  blocking collectives: 20.7 us -> 0 us
  between operations: 13.7 us -> 0.08 us
  other arithmetic: 7.72 us -> 0.02 us
  starting transfers between devices: 0.04 us -> 7.31 us
  matrix products: 5.98 us -> 0 us
  Pallas kernels: 0 us -> 5.74 us
  local copies, waits for them, and re-layouts: 5.35 us -> 0.07 us
    reduce_scatter x2 -> x0, waiting for transfers between devices: 40.1 us -> none  [the longest x1 20.9 us: body(): lax.psum_scatter(outer_terms.astype(jnp.bfloat16), 'col', scatter_dimensi...]
    all_gather x2 -> x0, blocking collectives: 20.7 us -> none  [the longest x1 15.1 us: body(): lax.all_gather(right, 'row', axis=1, tiled=True)]
    ppermute x0 -> x5, waiting for transfers between devices: none -> 10.4 us  [swapped(): return lax.ppermute(value, ('row', 'col'), pairs)]
    ppermute x0 -> x5, starting transfers between devices: none -> 7.31 us  [swapped(): return lax.ppermute(value, ('row', 'col'), pairs)]
    dot_general x8 -> x0, matrix products: 5.98 us -> none  [the longest x2 1.99 us: finish(): jnp.einsum('ijh,hc->ijc', normed, final_weight, precision=lax.Precision.H...]
    reduce_sum x7 -> x0, other arithmetic: 5.9 us -> none  [the longest x4 3.14 us: layer_norm(): variance = jnp.mean(centred * centred, axis=-1, keepdims=True)]
    pallas_call x0 -> x2, Pallas kernels: none -> 5.74 us  [the longest x1 4.48 us: compact_plan(): pl.pallas_call(update_kernel, out_shape=jax.ShapeDtypeStruct(pair.shape,...]
    convert_element_type x2 -> x0, local copies, waits for them, and re-layouts: 2.61 us -> none  [the longest x1 1.44 us: body(): inner_terms.astype(jnp.bfloat16)]
  transfers between devices with their start and end apart: 2 -> 5, of which waited for: 2 -> 4; matrix products, arithmetic and copies ran while one was open for 1% -> 0% of each run, Pallas kernels for 0% -> 0%
where the time goes in v1:
time: 23.7 us; the launch traced here: 23.6 us
  waiting for transfers between devices  10.4 us (44%)
  starting transfers between devices  7.31 us (31%)
  Pallas kernels  5.74 us (24%)
    ppermute x5, waiting for transfers between devices, swapped(): return lax.ppermute(value, ('row', 'col'), pairs)  10.4 us
    ppermute x5, starting transfers between devices, swapped(): return lax.ppermute(value, ('row', 'col'), pairs)  7.31 us
    pallas_call x1, Pallas kernels, compact_plan(): pl.pallas_call(update_kernel, out_shape=jax.ShapeDtypeStruct(pair.shape,...  4.48 us
    pallas_call x1, Pallas kernels, compact_plan(): pl.pallas_call(pack_kernel, out_shape=(pltpu.VMEM((ROWS, 128), jnp.bfloat...  1.26 us
  transfers between devices with their start and end apart: 5, of which 4 were waited for; matrix products, arithmetic and copies ran while one was open for 0% of the time, Pallas kernels for 0%

profile of v1, /device:TPU:0, one launch (start us, length us, event | category | flops | bytes accessed | tf_op | source)
XLA Modules:
  0.0 23.6 jit_solution(11140805879632268919)
XLA Ops:
  0.0 0.0 copy-start.4
  0.0 0.0 copy-start.5
  0.0 1.3 %pack.1 = (bf16[112,128]{1,0:T(8,128)(2,1)S(1)}, f32[112,128]{1,0:T(8,128)S(1)}) custom-call(f32[10,10,128]{2,1,0:T(8,128)} %pair_ref.1, s32[10,10]{1,0:T(8,128)} %mask_ref.1), custom_call_target="tpu_custom_call" | custom-call | tf_op jit(solution)/shard_map/pack/pallas_call | solution.py:239
  1.3 3.1 %collective-permute-start = (bf16[112,128]{1,0:T(8,128)(2,1)S(1)}, bf16[112,128]{1,0:T(8,128)(2,1)S(1)}, u32[]{:S(2)}, u32[]{:S(2)}) collective-permute-start(bf16[112,128]{1,0:T(8,128)(2,1)S(1)} %get-tuple-element.7), channel_id=1, source_target_pairs={{0,4},{1,5},{2,6},{3,7},{4,0},{5,1},{6,2},{7,3},{8,12},{9,13},{10,... | collective-permute-start | bytes 86024 | tf_op jit(solution)/shard_map/ppermute | solution.py:230
  4.4 2.6 %collective-permute-start.1 = (bf16[112,128]{1,0:T(8,128)(2,1)S(1)}, bf16[112,128]{1,0:T(8,128)(2,1)S(1)}, u32[]{:S(2)}, u32[]{:S(2)}) collective-permute-start(bf16[112,128]{1,0:T(8,128)(2,1)S(1)} %get-tuple-element.7), channel_id=1, source_target_pairs={{0,8},{1,9},{2,10},{3,11},{4,12},{5,13},{6,14},{7,15},{8,0},{9,1},... | collective-permute-start | bytes 86024 | tf_op jit(solution)/shard_map/ppermute | solution.py:230
  6.9 0.0 collective-permute-start.2
  7.0 0.0 copy-start.3
  7.0 0.0 collective-permute-done
  7.0 2.6 %collective-permute-done.1 = bf16[112,128]{1,0:T(8,128)(2,1)S(1)} collective-permute-done((bf16[112,128]{1,0:T(8,128)(2,1)S(1)}, bf16[112,128]{1,0:T(8,128)(2,1)S(1)}, u32[]{:S(2)}, u32[]{:S(2)}) %collective-permute-start.1) | collective-permute-done | bytes 28704 | tf_op jit(solution)/shard_map/ppermute | solution.py:230
  9.6 3.0 %collective-permute-done.2 = bf16[112,128]{1,0:T(8,128)(2,1)S(1)} collective-permute-done((bf16[112,128]{1,0:T(8,128)(2,1)S(1)}, bf16[112,128]{1,0:T(8,128)(2,1)S(1)}, u32[]{:S(2)}, u32[]{:S(2)}) %collective-permute-start.2) | collective-permute-done | bytes 28704 | tf_op jit(solution)/shard_map/ppermute | solution.py:230
  12.6 0.0 copy-start
  12.6 0.0 copy-start.1
  12.6 1.6 %collective-permute-start.3 = (bf16[4,112,128]{2,1,0:T(8,128)(2,1)S(1)}, bf16[4,112,128]{2,1,0:T(8,128)(2,1)S(1)}, u32[]{:S(2)}, u32[]{:S(2)}) collective-permute-start(bf16[4,112,128]{2,1,0:T(8,128)(2,1)S(1)} %pad_maximum_fusion), channel_id=1, source_target_pairs={{0,2},{1,3},{2,0},{3,1},{4,6},{5,7},{6,4},{7,5},{8,10},{9,11},{10,... | collective-permute-start | bytes 344072 | tf_op jit(solution)/shard_map/ppermute | solution.py:230
  14.2 0.0 copy-start.2
  14.2 3.3 %collective-permute-done.3 = bf16[4,112,128]{2,1,0:T(8,128)(2,1)S(1)} collective-permute-done((bf16[4,112,128]{2,1,0:T(8,128)(2,1)S(1)}, bf16[4,112,128]{2,1,0:T(8,128)(2,1)S(1)}, u32[]{:S(2)}, u32[]{:S(2)}) %collective-permute-start.3) | collective-permute-done | bytes 114720 | tf_op jit(solution)/shard_map/ppermute | solution.py:230
  17.5 0.1 collective-permute-start.4
  17.6 1.5 %collective-permute-done.4.far_ref = bf16[8,112,128]{2,1,0:T(8,128)(2,1)S(1)} collective-permute-done((bf16[8,112,128]{2,1,0:T(8,128)(2,1)S(1)}, bf16[8,112,128]{2,1,0:T(8,128)(2,1)S(1)}, u32[]{:S(2)}, u32[]{:S(2)}) %collective-permute-start.4) | collective-permute-done | bytes 229408 | tf_op jit(solution)/shard_map/ppermute | solution.py:230
  19.1 0.0 copy-done.4
  19.1 0.0 copy-done.5
  19.1 0.0 copy-done.3
  19.1 0.0 copy-done
  19.1 0.0 copy-done.1
  19.1 0.0 copy-done.2
  19.1 4.5 %update.1 = f32[10,10,128]{2,1,0:T(8,128)} custom-call(bf16[8,112,128]{2,1,0:T(8,128)(2,1)S(1)} %constant_dynamic-update-slice_fusion.near_ref, bf16[8,112,128]{2,1,0:T(8,128)(2,1)S(1)} %collective-permute-done.4.far_ref, f32[112,128]{1,0:T(8,128)S(1)} %get-tuple-element.8.own_ref, f32[128,512]{1,0:T(8,128)S(1)} %copy-done, f32[128,128]{1,0:T(8,128)S(1)} %copy-done.2, ...), custom_call_target="tpu_custom_call" | custom-call | tf_op jit(solution)/shard_map/update/pallas_call | solution.py:250
  (6 shorter events, 0.1 us)
Async XLA Ops:
  0.0 19.1 %copy-start.4 = (f32[128,128]{1,0:T(8,128)S(1)}, f32[128,128]{1,0:T(8,128)}, u32[]{:S(2)}) copy-start(f32[128,128]{1,0:T(8,128)} %in_gate_ref.1) | copy-start | bytes 196612
  0.0 19.1 %copy-start.5 = (f32[128,128]{1,0:T(8,128)S(1)}, f32[128,128]{1,0:T(8,128)}, u32[]{:S(2)}) copy-start(f32[128,128]{1,0:T(8,128)} %in_final_ref.1) | copy-start | bytes 196612
  1.3 5.7 %collective-permute-start = (bf16[112,128]{1,0:T(8,128)(2,1)S(1)}, bf16[112,128]{1,0:T(8,128)(2,1)S(1)}, u32[]{:S(2)}, u32[]{:S(2)}) collective-permute-start(bf16[112,128]{1,0:T(8,128)(2,1)S(1)} %get-tuple-element.7), channel_id=1, source_target_pairs={{0,4},{1,5},{2,6},{3,7},{4,0},{5,1},{6,2},{7,3},{8,12},{9,13},{10,... | collective-permute-start | bytes 86024 | tf_op jit(solution)/shard_map/ppermute | solution.py:230
  4.4 5.2 %collective-permute-start.1 = (bf16[112,128]{1,0:T(8,128)(2,1)S(1)}, bf16[112,128]{1,0:T(8,128)(2,1)S(1)}, u32[]{:S(2)}, u32[]{:S(2)}) collective-permute-start(bf16[112,128]{1,0:T(8,128)(2,1)S(1)} %get-tuple-element.7), channel_id=1, source_target_pairs={{0,8},{1,9},{2,10},{3,11},{4,12},{5,13},{6,14},{7,15},{8,0},{9,1},... | collective-permute-start | bytes 86024 | tf_op jit(solution)/shard_map/ppermute | solution.py:230
  6.9 5.7 %collective-permute-start.2 = (bf16[112,128]{1,0:T(8,128)(2,1)S(1)}, bf16[112,128]{1,0:T(8,128)(2,1)S(1)}, u32[]{:S(2)}, u32[]{:S(2)}) collective-permute-start(bf16[112,128]{1,0:T(8,128)(2,1)S(1)} %get-tuple-element.7), channel_id=1, source_target_pairs={{0,12},{1,13},{2,14},{3,15},{4,8},{5,9},{6,10},{7,11},{8,4},{9,5},... | collective-permute-start | bytes 86024 | tf_op jit(solution)/shard_map/ppermute | solution.py:230
  7.0 12.1 %copy-start.3 = (f32[128,128]{1,0:T(8,128)S(1)}, f32[128,128]{1,0:T(8,128)}, u32[]{:S(2)}) copy-start(f32[128,128]{1,0:T(8,128)} %out_final_ref.1) | copy-start | bytes 196612
  12.6 6.5 %copy-start = (f32[128,512]{1,0:T(8,128)S(1)}, f32[128,512]{1,0:T(8,128)}, u32[]{:S(2)}) copy-start(f32[128,512]{1,0:T(8,128)} %out_proj_ref.1) | copy-start | bytes 786436
  12.6 6.5 %copy-start.1 = (f32[128,512]{1,0:T(8,128)S(1)}, f32[128,512]{1,0:T(8,128)}, u32[]{:S(2)}) copy-start(f32[128,512]{1,0:T(8,128)} %in_proj_ref.1) | copy-start | bytes 786436
  12.6 4.9 %collective-permute-start.3 = (bf16[4,112,128]{2,1,0:T(8,128)(2,1)S(1)}, bf16[4,112,128]{2,1,0:T(8,128)(2,1)S(1)}, u32[]{:S(2)}, u32[]{:S(2)}) collective-permute-start(bf16[4,112,128]{2,1,0:T(8,128)(2,1)S(1)} %pad_maximum_fusion), channel_id=1, source_target_pairs={{0,2},{1,3},{2,0},{3,1},{4,6},{5,7},{6,4},{7,5},{8,10},{9,11},{10,... | collective-permute-start | bytes 344072 | tf_op jit(solution)/shard_map/ppermute | solution.py:230
  14.2 4.9 %copy-start.2 = (f32[128,128]{1,0:T(8,128)S(1)}, f32[128,128]{1,0:T(8,128)}, u32[]{:S(2)}) copy-start(f32[128,128]{1,0:T(8,128)} %out_gate_ref.1) | copy-start | bytes 196612
  17.5 1.6 %collective-permute-start.4 = (bf16[8,112,128]{2,1,0:T(8,128)(2,1)S(1)}, bf16[8,112,128]{2,1,0:T(8,128)(2,1)S(1)}, u32[]{:S(2)}, u32[]{:S(2)}) collective-permute-start(bf16[8,112,128]{2,1,0:T(8,128)(2,1)S(1)} %constant_dynamic-update-slice_fusion.near_ref), channel_id=1, source_target_pairs={{0,1},{1,0},{2,3},{3,2},{4,5},{5,4},{6,7},{7,6},{8,9},{9,8},{10,11... | collective-permute-start | bytes 688136 | tf_op jit(solution)/shard_map/ppermute | solution.py:230

commit v2 on v1

--- a/solution.py
+++ b/solution.py
@@ -109,87 +109,120 @@
         ]
 
 
-def update_kernel(
-    near_ref, far_ref, own_ref, out_proj_ref, out_gate_ref, out_final_ref, in_proj_ref, in_gate_ref, in_final_ref,
+RIGHT_LINE = 24
+LENGTH = SIDE * WIDTH
+GROUP = 4
+
+
+def add_terms(tiles, other, out_proj, first, outer_ref, lines_ref, right_lines_ref, left_ref, right_ref):
+    for slot in range(SPLIT):
+        to_lines(lines_ref, 0, tiles[slot].astype(jnp.float32), slot, SPLIT, WIDTH)
+    to_lines(right_lines_ref, 0, tiles[0].astype(jnp.float32), 0, 2, RIGHT_LINE)
+    to_lines(right_lines_ref, 0, tiles[other].astype(jnp.float32), 1, 2, RIGHT_LINE)
+    for raw_ref, weight, value_ref in (
+        (lines_ref, out_proj[:, :256], left_ref),
+        (right_lines_ref, out_proj[:, 256:], right_ref),
+    ):
+        raw = raw_ref[...]
+        proj = dot(scaled(jnp.where(raw < 0.5 * MASKED, raw, 0.0)), weight)
+        value_ref[...] = sigmoid(proj[:, :128]) * proj[:, 128:]
+
+    def step(g, carry):
+        at = [pl.ds(pl.multiple_of((g * GROUP + t) * WIDTH, 8), WIDTH) for t in range(GROUP)]
+        sums = [jnp.zeros((WIDTH, 128), jnp.float32) if first else outer_ref[at[t], :] for t in range(GROUP)]
+        for k in range(SIDE):
+            rows = left_ref[pl.ds(k * WIDTH, WIDTH), :]
+            for t in range(GROUP):
+                one = right_ref[pl.ds(k * RIGHT_LINE + g * GROUP + t, 1), :]
+                sums[t] = sums[t] + rows * jnp.broadcast_to(one, rows.shape)
+        for t in range(GROUP):
+            outer_ref[at[t], :] = sums[t]
+        return carry
+
+    lax.fori_loop(0, 2 * SIDE // GROUP, step, 0)
+
+
+def split_lines(raw):
+    valid = raw < 0.5 * MASKED
+    return jnp.where(valid, raw, 0.0), valid
+
+
+def other_slot():
+    before = lax.rem(lax.axis_index("row") - lax.axis_index("col") + SPLIT, SPLIT)
+    place = jnp.int32(0)
+    for number, step in enumerate(STEPS):
+        place = jnp.where(before == step, number + 1, place)
+    return place
+
+
+def other_part():
+    return jnp.bitwise_xor(lax.axis_index("row"), lax.axis_index("col"))
+
+
+def first_kernel(
+    tiles, own_ref, out_proj_ref, out_gate_ref, outer_ref, centred_ref, gate_ref, valid_ref, *scratch
+):
+    lines_ref = scratch[0]
+    add_terms(tiles, other_slot(), out_proj_ref[...].astype(jnp.bfloat16), True, outer_ref, *scratch)
+    centred, valid = split_lines(lines_ref[...])
+    centred_ref[...] = centred
+    valid_ref[...] = jnp.where(valid, 1.0, 0.0)
+    own = own_ref[...]
+    own = own - jnp.mean(own, axis=-1, keepdims=True)
+    to_lines(centred_ref, 0, own, 0, SPLIT, WIDTH)
+    gate_ref[...] = sigmoid(dot(scaled(centred_ref[...]), out_gate_ref[...].astype(jnp.bfloat16)))
+
+
+def next_kernel(tiles, out_proj_ref, before_ref, outer_ref, *scratch):
+    outer_ref[...] = before_ref[...]
+    add_terms(tiles, other_slot(), out_proj_ref[...].astype(jnp.bfloat16), False, outer_ref, *scratch)
+
+
+def last_kernel(
+    part0, part1, part2, part3, before_ref, centred0_ref, gate0_ref, valid0_ref, own_ref,
+    out_proj_ref, out_gate_ref, out_final_ref, in_proj_ref, in_gate_ref, in_final_ref,
     result_ref,
     lines_ref, right_lines_ref, left_ref, right_ref, outer_ref, mid_ref, pieces_ref, flat_ref,
 ):
     bf16 = jnp.bfloat16
-    row, col = lax.axis_index("row"), lax.axis_index("col")
-    other = jnp.bitwise_xor(row, col)
-    length = SIDE * WIDTH
-    right_line = 24
-    own = own_ref[...]
-    own_centred = own - jnp.mean(own, axis=-1, keepdims=True)
-
-    out_proj = out_proj_ref[...].astype(bf16)
-    for part in range(SPLIT):
-        source, place = (near_ref, far_ref)[part % 2], SPLIT * (part // 2)
-        for slot in range(SPLIT):
-            to_lines(lines_ref, part * length, source[place + slot].astype(jnp.float32), slot, SPLIT, WIDTH)
-        to_lines(right_lines_ref, 0, source[place].astype(jnp.float32), 0, 2, right_line)
-        to_lines(right_lines_ref, 0, source[place + other].astype(jnp.float32), 1, 2, right_line)
-        raw = lines_ref[pl.ds(part * length, length), :]
-        valid = raw < 0.5 * MASKED
-        normed = scaled(jnp.where(valid, raw, 0.0))
-        proj = dot(normed, out_proj[:, :256])
-        left_ref[pl.ds(part * length, length), :] = sigmoid(proj[:, :128]) * proj[:, 128:]
-        raw = right_lines_ref[...]
-        normed = scaled(jnp.where(raw < 0.5 * MASKED, raw, 0.0))
-        proj = dot(normed, out_proj[:, 256:])
-        right_ref[pl.ds(part * SIDE * right_line, SIDE * right_line), :] = sigmoid(proj[:, :128]) * proj[:, 128:]
-
-    group = 4
-
-    def outer_step(g, carry):
-        def add(k, sums):
-            rows = left_ref[pl.ds(pl.multiple_of(k * WIDTH, 8), WIDTH), :]
-            new = []
-            for jj in range(group):
-                one = right_ref[pl.ds(k * right_line + g * group + jj, 1), :]
-                new.append(sums[jj] + rows * jnp.broadcast_to(one, rows.shape))
-            return tuple(new)
-
-        sums = lax.fori_loop(
-            0, WIDTH, add, tuple(jnp.zeros((WIDTH, 128), jnp.float32) for _ in range(group)), unroll=4
-        )
-        for jj in range(group):
-            outer_ref[pl.ds(pl.multiple_of((g * group + jj) * WIDTH, 8), WIDTH), :] = sums[jj]
-        return carry
-
-    lax.fori_loop(0, 2 * SIDE // group, outer_step, 0)
-
-    out_gate = out_gate_ref[...].astype(bf16)
+    other = other_slot()
+    outer_ref[...] = before_ref[...]
+    add_terms(
+        part3, other, out_proj_ref[...].astype(bf16), False, outer_ref,
+        lines_ref, right_lines_ref, left_ref, right_ref.at[pl.ds(0, SIDE * RIGHT_LINE)],
+    )
+    for number, tiles in enumerate((part0, part1, part2, part3)):
+        @pl.when(other_part() == number)
+        def _():
+            for slot in range(SPLIT):
+                to_lines(lines_ref, 0, tiles[slot].astype(jnp.float32), slot, SPLIT, WIDTH)
+
     out_final = out_final_ref[...].astype(bf16)
     in_proj = in_proj_ref[...].astype(bf16)
     for block in range(2):
-        start = pl.multiple_of(other * length, 8) if block == 1 else 0
-        raw = lines_ref[pl.ds(start, length), :]
-        valid = raw < 0.5 * MASKED
-        centred = jnp.where(valid, raw, 0.0)
         if block == 0:
-            mid_ref[pl.ds(0, length), :] = centred
-            for k in range(SIDE):
-                mid_ref[pl.ds(WIDTH * k, MAIN), :] = own_centred[MAIN * k : MAIN * (k + 1)]
-            for e in range(REST):
-                mid_ref[pl.ds(MAIN * SPLIT + e, SIDE, stride=WIDTH), :] = own_centred[rest_rows(e) : rest_rows(e) + SIDE]
-            centred = mid_ref[pl.ds(0, length), :]
-        gate = sigmoid(dot(scaled(centred), out_gate))
-        from_slot = 1 - block
+            centred, gate, valid = centred0_ref[...], gate0_ref[...], valid0_ref[...] > 0.5
+        else:
+            centred, valid = split_lines(lines_ref[...])
+            gate = sigmoid(dot(scaled(centred), out_gate_ref[...].astype(bf16)))
+        slot = 1 - block
         summed = jnp.concatenate(
-            [outer_ref[pl.ds(from_slot * MAIN * WIDTH, MAIN * WIDTH), :],
-             outer_ref[pl.ds((2 * MAIN + REST * from_slot) * WIDTH, REST * WIDTH), :]], axis=0)
+            [
+                outer_ref[pl.ds(slot * MAIN * WIDTH, MAIN * WIDTH), :],
+                outer_ref[pl.ds((2 * MAIN + REST * slot) * WIDTH, REST * WIDTH), :],
+            ],
+            axis=0,
+        )
         change = gate * dot(layer_norm(summed), out_final)
-        mid = centred + change
-        normed = layer_norm(mid)
+        normed = layer_norm(centred + change)
         proj = dot(normed, in_proj[:, 256:] if block == 0 else in_proj[:, :256])
         value = jnp.where(valid, sigmoid(proj[:, :128]) * proj[:, 128:], 0.0)
         if block == 0:
-            right_ref[pl.ds(0, length), :] = value
-            mid_ref[pl.ds(0, length), :] = change
-            mid_ref[pl.ds(length, length), :] = normed
+            right_ref[...] = value
+            mid_ref[pl.ds(0, LENGTH), :] = change
+            mid_ref[pl.ds(LENGTH, LENGTH), :] = normed
         else:
-            left_ref[pl.ds(0, length), :] = value
+            left_ref[...] = value
 
     def inner_step(j, carry):
         right = right_ref[pl.ds(pl.multiple_of(j * WIDTH, 8), WIDTH), :]
@@ -214,8 +247,8 @@
             flat_ref[pl.ds(rest_rows(e), SIDE), :] = mid_ref[pl.ds(base + MAIN * SPLIT + e, SIDE, stride=WIDTH), :]
         return flat_ref[...]
 
-    mid = own + own_rows(0)
-    gate = sigmoid(dot(own_rows(length), in_gate_ref[...].astype(bf16)))
+    mid = own_ref[...] + own_rows(0)
+    gate = sigmoid(dot(own_rows(LENGTH), in_gate_ref[...].astype(bf16)))
     result = mid + gate * dot(layer_norm(inner), in_final_ref[...].astype(bf16))
     for k in range(SIDE):
         result_ref[pl.ds(0, MAIN), k, :] = result[MAIN * k : MAIN * (k + 1)]
@@ -230,39 +263,64 @@
     return lax.ppermute(value, ("row", "col"), pairs)
 
 
+STEPS = (1, 3, 2)
+
+
+def shifted(value, step):
+    pairs = [
+        (r * SPLIT + c, (r + step) % SPLIT * SPLIT + c) for r in range(SPLIT) for c in range(SPLIT)
+    ]
+    return lax.ppermute(value, ("row", "col"), pairs)
+
+
 def in_vmem(value):
     return pltpu.with_memory_space_constraint(value, pltpu.VMEM)
 
 
-def compact_plan(pair, pair_mask, out_proj, out_gate, out_final, in_proj, in_gate, in_final):
+def call(kernel, name, cycles, out, scratch, *operands, grant=32 << 20):
+    return pl.pallas_call(
+        kernel,
+        out_shape=out,
+        scratch_shapes=[pltpu.VMEM(shape, jnp.float32) for shape in scratch],
+        cost_estimate=pl.CostEstimate(flops=cycles, bytes_accessed=0, transcendentals=0),
+        compiler_params=pltpu.CompilerParams(vmem_limit_bytes=grant),
+        name=name,
+    )(*operands)
+
+
+def compact_plan(pair, pair_mask, *weights):
     f32 = jnp.float32
-    tile, own = pl.pallas_call(
-        pack_kernel,
-        out_shape=(pltpu.VMEM((ROWS, 128), jnp.bfloat16), pltpu.VMEM((ROWS, 128), f32)),
-        scratch_shapes=[pltpu.VMEM((ROWS, 128), f32)],
-        name="pack",
-    )(pair, pair_mask)
-    along_row = [swapped(tile, s, 0) for s in (3, 2, 1)]
-    column = jnp.stack([tile] + along_row[::-1])
-    near = jnp.concatenate([column, swapped(column, 0, 2)])
-    far = swapped(near, 0, 1)
-    length = SIDE * WIDTH
-    return pl.pallas_call(
-        update_kernel,
-        out_shape=jax.ShapeDtypeStruct(pair.shape, f32),
-        scratch_shapes=[
-            pltpu.VMEM((SPLIT * length, 128), f32),
-            pltpu.VMEM((SIDE * 24, 128), f32),
-            pltpu.VMEM((SPLIT * length, 128), f32),
-            pltpu.VMEM((SPLIT * SIDE * 24, 128), f32),
-            pltpu.VMEM((2 * length, 128), f32),
-            pltpu.VMEM((2 * length, 128), f32),
-            pltpu.VMEM((8 * ROWS, 128), f32),
-            pltpu.VMEM((ROWS, 128), f32),
-        ],
-        compiler_params=pltpu.CompilerParams(vmem_limit_bytes=32 << 20),
-        name="update",
-    )(in_vmem(near), in_vmem(far), in_vmem(own), *map(in_vmem, (out_proj, out_gate, out_final, in_proj, in_gate, in_final)))
+    out_proj, out_gate, out_final, in_proj, in_gate, in_final = map(in_vmem, weights)
+    tile, own = call(
+        pack_kernel, "pack", 1000, (pltpu.VMEM((ROWS, 128), jnp.bfloat16), pltpu.VMEM((ROWS, 128), f32)),
+        [(ROWS, 128)], pair, pair_mask, grant=None,
+    )
+    around = [tile] + [shifted(tile, step) for step in STEPS]
+    early = jnp.stack(around[:2])
+    swapped_early = swapped(early, 0, 2)
+    two, three, _ = lax.optimization_barrier((around[2], around[3], early))
+    late = jnp.stack([two, three])
+    part0 = jnp.concatenate([early, late])
+    part2 = jnp.concatenate([swapped_early, swapped(late, 0, 2)])
+    lines = pltpu.VMEM((LENGTH, 128), f32)
+    sums = pltpu.VMEM((2 * LENGTH, 128), f32)
+    work = [(LENGTH, 128), (SIDE * RIGHT_LINE, 128), (LENGTH, 128), (SIDE * RIGHT_LINE, 128)]
+    cost = 1 << 10
+    outer, centred0, gate0, valid0 = call(
+        first_kernel, "first", cost, (sums, lines, lines, lines), work, in_vmem(part0), in_vmem(own), out_proj, out_gate
+    )
+    part2, outer = lax.optimization_barrier((part2, outer))
+    part1 = swapped(part0, 0, 1)
+    outer = call(next_kernel, "second", cost, sums, work, in_vmem(part1), out_proj, in_vmem(outer))
+    part3 = swapped(part2, 0, 1)
+    outer = call(next_kernel, "third", cost, sums, work, in_vmem(part2), out_proj, in_vmem(outer))
+    part3, outer = lax.optimization_barrier((part3, outer))
+    return call(
+        last_kernel, "last", cost, jax.ShapeDtypeStruct(pair.shape, f32),
+        work[:3] + [(LENGTH, 128), (2 * LENGTH, 128), (2 * LENGTH, 128), (8 * ROWS, 128), (ROWS, 128)],
+        *map(in_vmem, (part0, part1, part2, part3, outer, centred0, gate0, valid0, own)),
+        out_proj, out_gate, out_final, in_proj, in_gate, in_final,
+    )
 
 
 def solution(mesh):

time: 23.7 us -> 20.1 us (0.85)
  waiting for transfers between devices: 10.4 us -> 2.26 us
  starting transfers between devices: 7.31 us -> 10.4 us
  Pallas kernels: 5.74 us -> 6.79 us
    ppermute x5 -> x4, waiting for transfers between devices: 10.4 us -> 1.48 us  [swapped(): return lax.ppermute(value, ('row', 'col'), pairs)]
    ppermute x0 -> x3, starting transfers between devices: none -> 7.01 us  [shifted(): return lax.ppermute(value, ('row', 'col'), pairs)]
    ppermute x5 -> x4, starting transfers between devices: 7.31 us -> 3.43 us  [swapped(): return lax.ppermute(value, ('row', 'col'), pairs)]
    pallas_call x2 -> x5, Pallas kernels: 5.74 us -> 6.79 us  [call(): pl.pallas_call(kernel, out_shape=out, scratch_shapes=[pltpu.VMEM(shape, j...]
    ppermute x0 -> x3, waiting for transfers between devices: none -> 0.78 us  [shifted(): return lax.ppermute(value, ('row', 'col'), pairs)]
  transfers between devices with their start and end apart: 5 -> 7, of which waited for: 4 -> 2; matrix products, arithmetic and copies ran while one was open for 0% -> 0% of each run, Pallas kernels for 0% -> 12%
where the time goes in v2:
time: 20.1 us; the launch traced here: 19.9 us
  starting transfers between devices  10.4 us (52%)
  Pallas kernels  6.79 us (34%)
  waiting for transfers between devices  2.26 us (11%)
  local copies, waits for them, and re-layouts  0.27 us (1%)
    ppermute x3, starting transfers between devices, shifted(): return lax.ppermute(value, ('row', 'col'), pairs)  7.01 us
    pallas_call x5, Pallas kernels, call(): pl.pallas_call(kernel, out_shape=out, scratch_shapes=[pltpu.VMEM(shape, j...  6.79 us
    ppermute x4, starting transfers between devices, swapped(): return lax.ppermute(value, ('row', 'col'), pairs)  3.43 us
    ppermute x4, waiting for transfers between devices, swapped(): return lax.ppermute(value, ('row', 'col'), pairs)  1.48 us
    ppermute x3, waiting for transfers between devices, shifted(): return lax.ppermute(value, ('row', 'col'), pairs)  0.78 us
  transfers between devices with their start and end apart: 7, of which 2 were waited for; matrix products, arithmetic and copies ran while one was open for 0% of the time, Pallas kernels for 12%

profile of v2, /device:TPU:0, one launch (start us, length us, event | category | flops | bytes accessed | tf_op | source)
XLA Modules:
  0.0 19.9 jit_solution(17505428008690431201)
XLA Ops:
  0.0 0.0 copy-start
  0.0 1.3 %pack.1 = (bf16[112,128]{1,0:T(8,128)(2,1)S(1)}, f32[112,128]{1,0:T(8,128)S(1)}) custom-call(f32[10,10,128]{2,1,0:T(8,128)} %pair_ref.1, s32[10,10]{1,0:T(8,128)} %mask_ref.1), custom_call_target="tpu_custom_call" | custom-call | flops 1000 | tf_op jit(solution)/shard_map/pack/pallas_call | solution.py:281
  1.3 3.1 %collective-permute-start = (bf16[112,128]{1,0:T(8,128)(2,1)S(1)}, bf16[112,128]{1,0:T(8,128)(2,1)S(1)}, u32[]{:S(2)}, u32[]{:S(2)}) collective-permute-start(bf16[112,128]{1,0:T(8,128)(2,1)S(1)} %get-tuple-element.17), channel_id=1, source_target_pairs={{0,4},{1,5},{2,6},{3,7},{4,8},{5,9},{6,10},{7,11},{8,12},{9,13},{1... | collective-permute-start | bytes 86024 | tf_op jit(solution)/shard_map/ppermute | solution.py:273
  4.4 2.6 %collective-permute-start.2 = (bf16[112,128]{1,0:T(8,128)(2,1)S(1)}, bf16[112,128]{1,0:T(8,128)(2,1)S(1)}, u32[]{:S(2)}, u32[]{:S(2)}) collective-permute-start(bf16[112,128]{1,0:T(8,128)(2,1)S(1)} %get-tuple-element.17), channel_id=1, source_target_pairs={{0,8},{1,9},{2,10},{3,11},{4,12},{5,13},{6,14},{7,15},{8,0},{9,1},... | collective-permute-start | bytes 86024 | tf_op jit(solution)/shard_map/ppermute | solution.py:273
  6.9 1.3 %collective-permute-start.1 = (bf16[112,128]{1,0:T(8,128)(2,1)S(1)}, bf16[112,128]{1,0:T(8,128)(2,1)S(1)}, u32[]{:S(2)}, u32[]{:S(2)}) collective-permute-start(bf16[112,128]{1,0:T(8,128)(2,1)S(1)} %get-tuple-element.17), channel_id=1, source_target_pairs={{0,12},{1,13},{2,14},{3,15},{4,0},{5,1},{6,2},{7,3},{8,4},{9,5},{1... | collective-permute-start | bytes 86024 | tf_op jit(solution)/shard_map/ppermute | solution.py:273
  8.3 0.0 collective-permute-done
  8.3 1.7 %collective-permute-start.4 = (bf16[2,112,128]{2,1,0:T(8,128)(2,1)S(1)}, bf16[2,112,128]{2,1,0:T(8,128)(2,1)S(1)}, u32[]{:S(2)}, u32[]{:S(2)}) collective-permute-start(bf16[2,112,128]{2,1,0:T(8,128)(2,1)S(1)} %pad_maximum_fusion.2), channel_id=1, source_target_pairs={{0,2},{1,3},{2,0},{3,1},{4,6},{5,7},{6,4},{7,5},{8,10},{9,11},{10,... | collective-permute-start | bytes 172040 | tf_op jit(solution)/shard_map/ppermute | solution.py:263
  10.0 0.0 collective-permute-done.2
  10.0 0.8 %collective-permute-done.1 = bf16[112,128]{1,0:T(8,128)(2,1)S(1)} collective-permute-done((bf16[112,128]{1,0:T(8,128)(2,1)S(1)}, bf16[112,128]{1,0:T(8,128)(2,1)S(1)}, u32[]{:S(2)}, u32[]{:S(2)}) %collective-permute-start.1) | collective-permute-done | bytes 28704 | tf_op jit(solution)/shard_map/ppermute | solution.py:273
  10.8 0.0 copy-start.2
  10.8 1.6 %collective-permute-start.5 = (bf16[2,112,128]{2,1,0:T(8,128)(2,1)S(1)}, bf16[2,112,128]{2,1,0:T(8,128)(2,1)S(1)}, u32[]{:S(2)}, u32[]{:S(2)}) collective-permute-start(bf16[2,112,128]{2,1,0:T(8,128)(2,1)S(1)} %pad_maximum_fusion.3), channel_id=1, source_target_pairs={{0,2},{1,3},{2,0},{3,1},{4,6},{5,7},{6,4},{7,5},{8,10},{9,11},{10,... | collective-permute-start | bytes 172040 | tf_op jit(solution)/shard_map/ppermute | solution.py:263
  12.4 0.1 collective-permute-start.3
  12.5 0.0 copy-done
  12.5 0.0 copy-done.2
  12.5 1.1 %first.1 = (f32[800,128]{1,0:T(8,128)S(1)}, f32[400,128]{1,0:T(8,128)S(1)}, f32[400,128]{1,0:T(8,128)S(1)}, f32[400,128]{1,0:T(8,128)S(1)}) custom-call(bf16[4,112,128]{2,1,0:T(8,128)(2,1)S(1)} %pad_maximum_fusion.tiles.part0, f32[112,128]{1,0:T(8,128)S(1)} %get-tuple-element.20.own_ref, f32[128,512]{1,0:T(8,128)S(1)} %copy-done, f32[128,128]{1,0:T(8,128)S(1)} %copy-done.2), custom_call_target="tpu_custom_call" | custom-call | flops 1024 | tf_op jit(solution)/shard_map/first/pallas_call | solution.py:281
  13.6 1.5 %collective-permute-done.5 = bf16[2,112,128]{2,1,0:T(8,128)(2,1)S(1)} collective-permute-done((bf16[2,112,128]{2,1,0:T(8,128)(2,1)S(1)}, bf16[2,112,128]{2,1,0:T(8,128)(2,1)S(1)}, u32[]{:S(2)}, u32[]{:S(2)}) %collective-permute-start.5) | collective-permute-done | bytes 57376 | tf_op jit(solution)/shard_map/ppermute | solution.py:263
  15.1 0.0 collective-permute-done.4
  15.1 0.1 collective-permute-start.6
  15.2 0.0 collective-permute-done.3.tiles.part1
  15.2 0.7 %second.1.before_ref = f32[800,128]{1,0:T(8,128)S(1)} custom-call(bf16[4,112,128]{2,1,0:T(8,128)(2,1)S(1)} %collective-permute-done.3.tiles.part1, f32[128,512]{1,0:T(8,128)S(1)} %copy-done, f32[800,128]{1,0:T(8,128)S(1)} %get-tuple-element.23.before_ref), custom_call_target="tpu_custom_call" | custom-call | flops 1024 | tf_op jit(solution)/shard_map/second/pallas_call | solution.py:281
  15.9 0.0 copy-start.1
  15.9 0.0 copy-start.3
  15.9 0.0 copy-start.4
  15.9 0.0 copy-start.5
  15.9 0.7 %third.1.before_ref = f32[800,128]{1,0:T(8,128)S(1)} custom-call(bf16[4,112,128]{2,1,0:T(8,128)(2,1)S(1)} %pad_maximum_fusion.1.tiles.part2, f32[128,512]{1,0:T(8,128)S(1)} %copy-done, f32[800,128]{1,0:T(8,128)S(1)} %second.1.before_ref), custom_call_target="tpu_custom_call" | custom-call | flops 1024 | tf_op jit(solution)/shard_map/third/pallas_call | solution.py:281
  16.6 0.0 collective-permute-done.6.part3
  16.6 0.2 %copy-done.1 = f32[128,512]{1,0:T(8,128)S(1)} copy-done((f32[128,512]{1,0:T(8,128)S(1)}, f32[128,512]{1,0:T(8,128)}, u32[]{:S(2)}) %copy-start.1) | copy-done | bytes 262168
  16.8 0.0 copy-done.3
  16.8 0.0 copy-done.4
  16.8 0.0 copy-done.5
  16.8 3.1 %last.1 = f32[10,10,128]{2,1,0:T(8,128)} custom-call(bf16[4,112,128]{2,1,0:T(8,128)(2,1)S(1)} %pad_maximum_fusion.tiles.part0, bf16[4,112,128]{2,1,0:T(8,128)(2,1)S(1)} %collective-permute-done.3.tiles.part1, bf16[4,112,128]{2,1,0:T(8,128)(2,1)S(1)} %pad_maximum_fusion.1.tiles.part2, bf16[4,112,128]{2,1,0:T(8,128)(2,1)S(1)} %collective-permute-done.6.part3, ...), custom_call_target="tpu_custom_call" | custom-call | flops 1024 | tf_op jit(solution)/shard_map/last/pallas_call | solution.py:281
  (4 shorter events, 0.0 us)
Async XLA Ops:
  0.0 12.5 %copy-start = (f32[128,512]{1,0:T(8,128)S(1)}, f32[128,512]{1,0:T(8,128)}, u32[]{:S(2)}) copy-start(f32[128,512]{1,0:T(8,128)} %out_proj_ref.7) | copy-start | bytes 786436
  1.3 7.0 %collective-permute-start = (bf16[112,128]{1,0:T(8,128)(2,1)S(1)}, bf16[112,128]{1,0:T(8,128)(2,1)S(1)}, u32[]{:S(2)}, u32[]{:S(2)}) collective-permute-start(bf16[112,128]{1,0:T(8,128)(2,1)S(1)} %get-tuple-element.17), channel_id=1, source_target_pairs={{0,4},{1,5},{2,6},{3,7},{4,8},{5,9},{6,10},{7,11},{8,12},{9,13},{1... | collective-permute-start | bytes 86024 | tf_op jit(solution)/shard_map/ppermute | solution.py:273
  4.4 5.7 %collective-permute-start.2 = (bf16[112,128]{1,0:T(8,128)(2,1)S(1)}, bf16[112,128]{1,0:T(8,128)(2,1)S(1)}, u32[]{:S(2)}, u32[]{:S(2)}) collective-permute-start(bf16[112,128]{1,0:T(8,128)(2,1)S(1)} %get-tuple-element.17), channel_id=1, source_target_pairs={{0,8},{1,9},{2,10},{3,11},{4,12},{5,13},{6,14},{7,15},{8,0},{9,1},... | collective-permute-start | bytes 86024 | tf_op jit(solution)/shard_map/ppermute | solution.py:273
  6.9 3.9 %collective-permute-start.1 = (bf16[112,128]{1,0:T(8,128)(2,1)S(1)}, bf16[112,128]{1,0:T(8,128)(2,1)S(1)}, u32[]{:S(2)}, u32[]{:S(2)}) collective-permute-start(bf16[112,128]{1,0:T(8,128)(2,1)S(1)} %get-tuple-element.17), channel_id=1, source_target_pairs={{0,12},{1,13},{2,14},{3,15},{4,0},{5,1},{6,2},{7,3},{8,4},{9,5},{1... | collective-permute-start | bytes 86024 | tf_op jit(solution)/shard_map/ppermute | solution.py:273
  8.3 6.8 %collective-permute-start.4 = (bf16[2,112,128]{2,1,0:T(8,128)(2,1)S(1)}, bf16[2,112,128]{2,1,0:T(8,128)(2,1)S(1)}, u32[]{:S(2)}, u32[]{:S(2)}) collective-permute-start(bf16[2,112,128]{2,1,0:T(8,128)(2,1)S(1)} %pad_maximum_fusion.2), channel_id=1, source_target_pairs={{0,2},{1,3},{2,0},{3,1},{4,6},{5,7},{6,4},{7,5},{8,10},{9,11},{10,... | collective-permute-start | bytes 172040 | tf_op jit(solution)/shard_map/ppermute | solution.py:263
  10.8 1.7 %copy-start.2 = (f32[128,128]{1,0:T(8,128)S(1)}, f32[128,128]{1,0:T(8,128)}, u32[]{:S(2)}) copy-start(f32[128,128]{1,0:T(8,128)} %out_gate_ref.3) | copy-start | bytes 196612
  10.8 4.2 %collective-permute-start.5 = (bf16[2,112,128]{2,1,0:T(8,128)(2,1)S(1)}, bf16[2,112,128]{2,1,0:T(8,128)(2,1)S(1)}, u32[]{:S(2)}, u32[]{:S(2)}) collective-permute-start(bf16[2,112,128]{2,1,0:T(8,128)(2,1)S(1)} %pad_maximum_fusion.3), channel_id=1, source_target_pairs={{0,2},{1,3},{2,0},{3,1},{4,6},{5,7},{6,4},{7,5},{8,10},{9,11},{10,... | collective-permute-start | bytes 172040 | tf_op jit(solution)/shard_map/ppermute | solution.py:263
  12.4 2.8 %collective-permute-start.3 = (bf16[4,112,128]{2,1,0:T(8,128)(2,1)S(1)}, bf16[4,112,128]{2,1,0:T(8,128)(2,1)S(1)}, u32[]{:S(2)}, u32[]{:S(2)}) collective-permute-start(bf16[4,112,128]{2,1,0:T(8,128)(2,1)S(1)} %pad_maximum_fusion.tiles.part0), channel_id=1, source_target_pairs={{0,1},{1,0},{2,3},{3,2},{4,5},{5,4},{6,7},{7,6},{8,9},{9,8},{10,11... | collective-permute-start | bytes 344072 | tf_op jit(solution)/shard_map/ppermute | solution.py:263
  15.1 1.5 %collective-permute-start.6 = (bf16[4,112,128]{2,1,0:T(8,128)(2,1)S(1)}, bf16[4,112,128]{2,1,0:T(8,128)(2,1)S(1)}, u32[]{:S(2)}, u32[]{:S(2)}) collective-permute-start(bf16[4,112,128]{2,1,0:T(8,128)(2,1)S(1)} %pad_maximum_fusion.1.tiles.part2), channel_id=1, source_target_pairs={{0,1},{1,0},{2,3},{3,2},{4,5},{5,4},{6,7},{7,6},{8,9},{9,8},{10,11... | collective-permute-start | bytes 344072 | tf_op jit(solution)/shard_map/ppermute | solution.py:263
  15.9 1.0 %copy-start.1 = (f32[128,512]{1,0:T(8,128)S(1)}, f32[128,512]{1,0:T(8,128)}, u32[]{:S(2)}) copy-start(f32[128,512]{1,0:T(8,128)} %in_proj_ref.1) | copy-start | bytes 786436
  15.9 0.9 %copy-start.3 = (f32[128,128]{1,0:T(8,128)S(1)}, f32[128,128]{1,0:T(8,128)}, u32[]{:S(2)}) copy-start(f32[128,128]{1,0:T(8,128)} %out_final_ref.1) | copy-start | bytes 196612
  15.9 0.9 %copy-start.4 = (f32[128,128]{1,0:T(8,128)S(1)}, f32[128,128]{1,0:T(8,128)}, u32[]{:S(2)}) copy-start(f32[128,128]{1,0:T(8,128)} %in_gate_ref.1) | copy-start | bytes 196612
  15.9 0.9 %copy-start.5 = (f32[128,128]{1,0:T(8,128)S(1)}, f32[128,128]{1,0:T(8,128)}, u32[]{:S(2)}) copy-start(f32[128,128]{1,0:T(8,128)} %in_final_ref.1) | copy-start | bytes 196612

commit v3 on v2

--- a/solution.py
+++ b/solution.py
@@ -100,6 +100,17 @@
     tile_ref[...] = send_ref[...].astype(tile_ref.dtype)
 
 
+OUT_PROJ, OUT_GATE, OUT_FINAL, IN_PROJ, IN_GATE, IN_FINAL, WEIGHTS = 0, 512, 640, 768, 1280, 1408, 1536
+
+
+def weights_kernel(*refs):
+    start = 0
+    for weight_ref in refs[:-1]:
+        width = weight_ref.shape[1]
+        refs[-1][:, pl.ds(start, width)] = weight_ref[...].astype(refs[-1].dtype)
+        start += width
+
+
 def to_lines(target, base, tile, slot, slots, line):
     for k in range(SIDE):
         target[pl.ds(base + line * k + MAIN * slot, MAIN), :] = tile[MAIN * k : MAIN * (k + 1)]
@@ -114,32 +125,29 @@
 GROUP = 4
 
 
-def add_terms(tiles, other, out_proj, first, outer_ref, lines_ref, right_lines_ref, left_ref, right_ref):
+def add_terms(tiles, other, weights_ref, before_ref, outer_ref, lines_ref, right_lines_ref, left_ref, right_ref):
     for slot in range(SPLIT):
         to_lines(lines_ref, 0, tiles[slot].astype(jnp.float32), slot, SPLIT, WIDTH)
     to_lines(right_lines_ref, 0, tiles[0].astype(jnp.float32), 0, 2, RIGHT_LINE)
     to_lines(right_lines_ref, 0, tiles[other].astype(jnp.float32), 1, 2, RIGHT_LINE)
-    for raw_ref, weight, value_ref in (
-        (lines_ref, out_proj[:, :256], left_ref),
-        (right_lines_ref, out_proj[:, 256:], right_ref),
-    ):
-        raw = raw_ref[...]
-        proj = dot(scaled(jnp.where(raw < 0.5 * MASKED, raw, 0.0)), weight)
-        value_ref[...] = sigmoid(proj[:, :128]) * proj[:, 128:]
-
-    def step(g, carry):
-        at = [pl.ds(pl.multiple_of((g * GROUP + t) * WIDTH, 8), WIDTH) for t in range(GROUP)]
-        sums = [jnp.zeros((WIDTH, 128), jnp.float32) if first else outer_ref[at[t], :] for t in range(GROUP)]
+    raw = jnp.concatenate([lines_ref[...], right_lines_ref[...]], axis=0)
+    normed = scaled(split_lines(raw)[0])
+    proj = dot(normed[:LENGTH], weights_ref[:, pl.ds(OUT_PROJ, 256)])
+    left_ref[...] = sigmoid(proj[:, :128]) * proj[:, 128:]
+    proj = dot(normed[LENGTH:], weights_ref[:, pl.ds(OUT_PROJ + 256, 256)])
+    right_ref[...] = sigmoid(proj[:, :128]) * proj[:, 128:]
+
+    for g in range(2 * SIDE // GROUP):
+        at = [pl.ds((g * GROUP + t) * WIDTH, WIDTH) for t in range(GROUP)]
+        sums = [None if before_ref is None else before_ref[at[t], :] for t in range(GROUP)]
         for k in range(SIDE):
             rows = left_ref[pl.ds(k * WIDTH, WIDTH), :]
             for t in range(GROUP):
                 one = right_ref[pl.ds(k * RIGHT_LINE + g * GROUP + t, 1), :]
-                sums[t] = sums[t] + rows * jnp.broadcast_to(one, rows.shape)
+                term = rows * jnp.broadcast_to(one, rows.shape)
+                sums[t] = term if sums[t] is None else sums[t] + term
         for t in range(GROUP):
             outer_ref[at[t], :] = sums[t]
-        return carry
-
-    lax.fori_loop(0, 2 * SIDE // GROUP, step, 0)
 
 
 def split_lines(raw):
@@ -160,96 +168,83 @@
 
 
 def first_kernel(
-    tiles, own_ref, out_proj_ref, out_gate_ref, outer_ref, centred_ref, gate_ref, valid_ref, *scratch
+    tiles, own_ref, weights_ref, outer_ref, centred_ref, gate_ref, valid_ref, *scratch
 ):
     lines_ref = scratch[0]
-    add_terms(tiles, other_slot(), out_proj_ref[...].astype(jnp.bfloat16), True, outer_ref, *scratch)
+    add_terms(tiles, other_slot(), weights_ref, None, outer_ref, *scratch)
     centred, valid = split_lines(lines_ref[...])
     centred_ref[...] = centred
     valid_ref[...] = jnp.where(valid, 1.0, 0.0)
     own = own_ref[...]
     own = own - jnp.mean(own, axis=-1, keepdims=True)
     to_lines(centred_ref, 0, own, 0, SPLIT, WIDTH)
-    gate_ref[...] = sigmoid(dot(scaled(centred_ref[...]), out_gate_ref[...].astype(jnp.bfloat16)))
-
-
-def next_kernel(tiles, out_proj_ref, before_ref, outer_ref, *scratch):
-    outer_ref[...] = before_ref[...]
-    add_terms(tiles, other_slot(), out_proj_ref[...].astype(jnp.bfloat16), False, outer_ref, *scratch)
+    gate_ref[...] = sigmoid(dot(scaled(centred_ref[...]), weights_ref[:, pl.ds(OUT_GATE, 128)]))
+
+
+def next_kernel(tiles, weights_ref, before_ref, outer_ref, *scratch):
+    add_terms(tiles, other_slot(), weights_ref, before_ref, outer_ref, *scratch)
 
 
 def last_kernel(
     part0, part1, part2, part3, before_ref, centred0_ref, gate0_ref, valid0_ref, own_ref,
-    out_proj_ref, out_gate_ref, out_final_ref, in_proj_ref, in_gate_ref, in_final_ref,
+    weights_ref,
     result_ref,
-    lines_ref, right_lines_ref, left_ref, right_ref, outer_ref, mid_ref, pieces_ref, flat_ref,
+    lines_ref, right_lines_ref, left_ref, right_ref, outer_ref, block_ref, left2_ref, right2_ref, mid_ref, normed_ref,
+    pieces_ref, flat_ref, flat2_ref,
 ):
-    bf16 = jnp.bfloat16
-    other = other_slot()
-    outer_ref[...] = before_ref[...]
-    add_terms(
-        part3, other, out_proj_ref[...].astype(bf16), False, outer_ref,
-        lines_ref, right_lines_ref, left_ref, right_ref.at[pl.ds(0, SIDE * RIGHT_LINE)],
-    )
     for number, tiles in enumerate((part0, part1, part2, part3)):
         @pl.when(other_part() == number)
         def _():
             for slot in range(SPLIT):
-                to_lines(lines_ref, 0, tiles[slot].astype(jnp.float32), slot, SPLIT, WIDTH)
-
-    out_final = out_final_ref[...].astype(bf16)
-    in_proj = in_proj_ref[...].astype(bf16)
-    for block in range(2):
-        if block == 0:
-            centred, gate, valid = centred0_ref[...], gate0_ref[...], valid0_ref[...] > 0.5
-        else:
-            centred, valid = split_lines(lines_ref[...])
-            gate = sigmoid(dot(scaled(centred), out_gate_ref[...].astype(bf16)))
-        slot = 1 - block
-        summed = jnp.concatenate(
-            [
-                outer_ref[pl.ds(slot * MAIN * WIDTH, MAIN * WIDTH), :],
-                outer_ref[pl.ds((2 * MAIN + REST * slot) * WIDTH, REST * WIDTH), :],
-            ],
-            axis=0,
-        )
-        change = gate * dot(layer_norm(summed), out_final)
-        normed = layer_norm(centred + change)
-        proj = dot(normed, in_proj[:, 256:] if block == 0 else in_proj[:, :256])
-        value = jnp.where(valid, sigmoid(proj[:, :128]) * proj[:, 128:], 0.0)
-        if block == 0:
-            right_ref[...] = value
-            mid_ref[pl.ds(0, LENGTH), :] = change
-            mid_ref[pl.ds(LENGTH, LENGTH), :] = normed
-        else:
-            left_ref[...] = value
-
-    def inner_step(j, carry):
-        right = right_ref[pl.ds(pl.multiple_of(j * WIDTH, 8), WIDTH), :]
+                to_lines(block_ref, 0, tiles[slot].astype(jnp.float32), slot, SPLIT, WIDTH)
+
+    add_terms(
+        part3, other_slot(), weights_ref, before_ref, outer_ref,
+        lines_ref, right_lines_ref, left_ref, right_ref,
+    )
+
+    def sums_of(slot):
+        return [
+            outer_ref[pl.ds(slot * MAIN * WIDTH, MAIN * WIDTH), :],
+            outer_ref[pl.ds((2 * MAIN + REST * slot) * WIDTH, REST * WIDTH), :],
+        ]
+
+    centred1, valid1 = split_lines(block_ref[...])
+    gate1 = sigmoid(dot(scaled(centred1), weights_ref[:, pl.ds(OUT_GATE, 128)]))
+    gate = jnp.concatenate([gate0_ref[...], gate1], axis=0)
+    centred = jnp.concatenate([centred0_ref[...], centred1], axis=0)
+    change = gate * dot(layer_norm(jnp.concatenate(sums_of(1) + sums_of(0), axis=0)), weights_ref[:, pl.ds(OUT_FINAL, 128)])
+    normed = layer_norm(centred + change)
+    mid_ref[...] = change[:LENGTH]
+    normed_ref[...] = normed[:LENGTH]
+    proj = dot(normed[:LENGTH], weights_ref[:, pl.ds(IN_PROJ + 256, 256)])
+    right2_ref[...] = jnp.where(valid0_ref[...] > 0.5, sigmoid(proj[:, :128]) * proj[:, 128:], 0.0)
+    proj = dot(normed[LENGTH:], weights_ref[:, pl.ds(IN_PROJ, 256)])
+    left2_ref[...] = jnp.where(valid1, sigmoid(proj[:, :128]) * proj[:, 128:], 0.0)
+
+    for j in range(SIDE):
+        right = right2_ref[pl.ds(j * WIDTH, WIDTH), :]
         for i in range(SIDE):
-            product = left_ref[pl.ds(i * WIDTH, WIDTH), :] * right
+            product = left2_ref[pl.ds(i * WIDTH, WIDTH), :] * right
             folded = product[:8]
             for t in range(1, WIDTH // 8):
                 folded = folded + product[8 * t : 8 * (t + 1)]
             at = MAIN * j + i if i < MAIN else rest_rows(i - MAIN) + j
-            pieces_ref[pl.ds(pl.multiple_of(8 * at, 8), 8), :] = folded
-        return carry
-
-    lax.fori_loop(0, SIDE, inner_step, 0)
+            pieces_ref[pl.ds(8 * at, 8), :] = folded
     inner = pieces_ref[pl.ds(0, ROWS, stride=8), :]
     for t in range(1, 8):
         inner = inner + pieces_ref[pl.ds(t, ROWS, stride=8), :]
 
-    def own_rows(base):
+    def own_rows(source_ref, flat_ref):
         for k in range(SIDE):
-            flat_ref[pl.ds(MAIN * k, MAIN), :] = mid_ref[pl.ds(base + WIDTH * k, MAIN), :]
+            flat_ref[pl.ds(MAIN * k, MAIN), :] = source_ref[pl.ds(WIDTH * k, MAIN), :]
         for e in range(REST):
-            flat_ref[pl.ds(rest_rows(e), SIDE), :] = mid_ref[pl.ds(base + MAIN * SPLIT + e, SIDE, stride=WIDTH), :]
+            flat_ref[pl.ds(rest_rows(e), SIDE), :] = source_ref[pl.ds(MAIN * SPLIT + e, SIDE, stride=WIDTH), :]
         return flat_ref[...]
 
-    mid = own_ref[...] + own_rows(0)
-    gate = sigmoid(dot(own_rows(LENGTH), in_gate_ref[...].astype(bf16)))
-    result = mid + gate * dot(layer_norm(inner), in_final_ref[...].astype(bf16))
+    mid = own_ref[...] + own_rows(mid_ref, flat_ref)
+    gate = sigmoid(dot(own_rows(normed_ref, flat2_ref), weights_ref[:, pl.ds(IN_GATE, 128)]))
+    result = mid + gate * dot(layer_norm(inner), weights_ref[:, pl.ds(IN_FINAL, 128)])
     for k in range(SIDE):
         result_ref[pl.ds(0, MAIN), k, :] = result[MAIN * k : MAIN * (k + 1)]
         for e in range(REST):
@@ -263,7 +258,7 @@
     return lax.ppermute(value, ("row", "col"), pairs)
 
 
-STEPS = (1, 3, 2)
+STEPS = (2, 1, 3)
 
 
 def shifted(value, step):
@@ -290,16 +285,19 @@
 
 def compact_plan(pair, pair_mask, *weights):
     f32 = jnp.float32
-    out_proj, out_gate, out_final, in_proj, in_gate, in_final = map(in_vmem, weights)
     tile, own = call(
         pack_kernel, "pack", 1000, (pltpu.VMEM((ROWS, 128), jnp.bfloat16), pltpu.VMEM((ROWS, 128), f32)),
         [(ROWS, 128)], pair, pair_mask, grant=None,
     )
+    weights = call(
+        weights_kernel, "weights", 1000, pltpu.VMEM((128, WEIGHTS), jnp.bfloat16), [], *weights, grant=None
+    )
     around = [tile] + [shifted(tile, step) for step in STEPS]
-    early = jnp.stack(around[:2])
+    early, weights = lax.optimization_barrier((jnp.stack(around[:3]), weights))
+    weights = in_vmem(weights)
     swapped_early = swapped(early, 0, 2)
-    two, three, _ = lax.optimization_barrier((around[2], around[3], early))
-    late = jnp.stack([two, three])
+    last, _ = lax.optimization_barrier((around[3], early))
+    late = last[None]
     part0 = jnp.concatenate([early, late])
     part2 = jnp.concatenate([swapped_early, swapped(late, 0, 2)])
     lines = pltpu.VMEM((LENGTH, 128), f32)
@@ -307,19 +305,19 @@
     work = [(LENGTH, 128), (SIDE * RIGHT_LINE, 128), (LENGTH, 128), (SIDE * RIGHT_LINE, 128)]
     cost = 1 << 10
     outer, centred0, gate0, valid0 = call(
-        first_kernel, "first", cost, (sums, lines, lines, lines), work, in_vmem(part0), in_vmem(own), out_proj, out_gate
+        first_kernel, "first", cost, (sums, lines, lines, lines), work, in_vmem(part0), in_vmem(own), weights
     )
     part2, outer = lax.optimization_barrier((part2, outer))
     part1 = swapped(part0, 0, 1)
-    outer = call(next_kernel, "second", cost, sums, work, in_vmem(part1), out_proj, in_vmem(outer))
+    outer = call(next_kernel, "second", cost, sums, work, in_vmem(part1), weights, in_vmem(outer))
     part3 = swapped(part2, 0, 1)
-    outer = call(next_kernel, "third", cost, sums, work, in_vmem(part2), out_proj, in_vmem(outer))
+    outer = call(next_kernel, "third", cost, sums, work, in_vmem(part2), weights, in_vmem(outer))
     part3, outer = lax.optimization_barrier((part3, outer))
     return call(
         last_kernel, "last", cost, jax.ShapeDtypeStruct(pair.shape, f32),
-        work[:3] + [(LENGTH, 128), (2 * LENGTH, 128), (2 * LENGTH, 128), (8 * ROWS, 128), (ROWS, 128)],
+        work + [(2 * LENGTH, 128)] + 5 * [(LENGTH, 128)] + [(8 * ROWS, 128), (ROWS, 128), (ROWS, 128)],
         *map(in_vmem, (part0, part1, part2, part3, outer, centred0, gate0, valid0, own)),
-        out_proj, out_gate, out_final, in_proj, in_gate, in_final,
+        weights,
     )
 
 

time: 20.1 us -> 18.8 us (0.935)
  waiting for transfers between devices: 2.26 us -> 1.77 us
  starting transfers between devices: 10.4 us -> 10 us
  local copies, waits for them, and re-layouts: 0.27 us -> 0 us
    ppermute x3, waiting for transfers between devices: 0.78 us -> 0.01 us  [shifted(): return lax.ppermute(value, ('row', 'col'), pairs)]
    ppermute x4, starting transfers between devices: 3.43 us -> 2.99 us  [swapped(): return lax.ppermute(value, ('row', 'col'), pairs)]
    ppermute x4, waiting for transfers between devices: 1.48 us -> 1.76 us  [swapped(): return lax.ppermute(value, ('row', 'col'), pairs)]
    unnamed x12 -> x0, local copies, waits for them, and re-layouts: 0.27 us -> none
    pallas_call x5 -> x6, Pallas kernels: 6.79 us -> 6.72 us  [call(): pl.pallas_call(kernel, out_shape=out, scratch_shapes=[pltpu.VMEM(shape, j...]
  transfers between devices with their start and end apart: 7 -> 7, of which waited for: 2 -> 1; matrix products, arithmetic and copies ran while one was open for 0% -> 0% of each run, Pallas kernels for 12% -> 17%
where the time goes in v3:
time: 18.8 us; the launch traced here: 18.6 us
  starting transfers between devices  10 us (53%)
  Pallas kernels  6.72 us (36%)
  waiting for transfers between devices  1.77 us (9%)
    ppermute x3, starting transfers between devices, shifted(): return lax.ppermute(value, ('row', 'col'), pairs)  7.01 us
    pallas_call x6, Pallas kernels, call(): pl.pallas_call(kernel, out_shape=out, scratch_shapes=[pltpu.VMEM(shape, j...  6.72 us
    ppermute x4, starting transfers between devices, swapped(): return lax.ppermute(value, ('row', 'col'), pairs)  2.99 us
    ppermute x4, waiting for transfers between devices, swapped(): return lax.ppermute(value, ('row', 'col'), pairs)  1.76 us
  transfers between devices with their start and end apart: 7, of which 1 were waited for; matrix products, arithmetic and copies ran while one was open for 0% of the time, Pallas kernels for 17%

profile of v3, /device:TPU:0, one launch (start us, length us, event | category | flops | bytes accessed | tf_op | source)
XLA Modules:
  0.0 18.6 jit_solution(13881618441567130440)
XLA Ops:
  0.0 1.2 %pack.1 = (bf16[112,128]{1,0:T(8,128)(2,1)S(1)}, f32[112,128]{1,0:T(8,128)S(1)}) custom-call(f32[10,10,128]{2,1,0:T(8,128)} %pair_ref.1, s32[10,10]{1,0:T(8,128)} %mask_ref.1), custom_call_target="tpu_custom_call" | custom-call | flops 1000 | tf_op jit(solution)/shard_map/pack/pallas_call | solution.py:276
  1.2 3.1 %collective-permute-start.1 = (bf16[112,128]{1,0:T(8,128)(2,1)S(1)}, bf16[112,128]{1,0:T(8,128)(2,1)S(1)}, u32[]{:S(2)}, u32[]{:S(2)}) collective-permute-start(bf16[112,128]{1,0:T(8,128)(2,1)S(1)} %get-tuple-element.18), channel_id=1, source_target_pairs={{0,4},{1,5},{2,6},{3,7},{4,8},{5,9},{6,10},{7,11},{8,12},{9,13},{1... | collective-permute-start | bytes 86024 | tf_op jit(solution)/shard_map/ppermute | solution.py:268
  4.3 2.6 %collective-permute-start = (bf16[112,128]{1,0:T(8,128)(2,1)S(1)}, bf16[112,128]{1,0:T(8,128)(2,1)S(1)}, u32[]{:S(2)}, u32[]{:S(2)}) collective-permute-start(bf16[112,128]{1,0:T(8,128)(2,1)S(1)} %get-tuple-element.18), channel_id=1, source_target_pairs={{0,8},{1,9},{2,10},{3,11},{4,12},{5,13},{6,14},{7,15},{8,0},{9,1},... | collective-permute-start | bytes 86024 | tf_op jit(solution)/shard_map/ppermute | solution.py:268
  6.9 1.3 %collective-permute-start.2 = (bf16[112,128]{1,0:T(8,128)(2,1)S(1)}, bf16[112,128]{1,0:T(8,128)(2,1)S(1)}, u32[]{:S(2)}, u32[]{:S(2)}) collective-permute-start(bf16[112,128]{1,0:T(8,128)(2,1)S(1)} %get-tuple-element.18), channel_id=1, source_target_pairs={{0,12},{1,13},{2,14},{3,15},{4,0},{5,1},{6,2},{7,3},{8,4},{9,5},{1... | collective-permute-start | bytes 86024 | tf_op jit(solution)/shard_map/ppermute | solution.py:268
  8.2 1.1 %weights.1.weights_ref = bf16[128,1536]{1,0:T(8,128)(2,1)S(1)} custom-call(f32[128,512]{1,0:T(8,128)} %refs_0_.1, f32[128,128]{1,0:T(8,128)} %refs_1_.1, f32[128,128]{1,0:T(8,128)} %refs_2_.1, f32[128,512]{1,0:T(8,128)} %refs_3_.1, f32[128,128]{1,0:T(8,128)} %refs_4_.1, f32[128,128]{1,0:T(8,128)} %refs_5_.1), custom_call_target="tpu_custom_call" | custom-call | flops 1000 | tf_op jit(solution)/shard_map/weights/pallas_call | solution.py:276
  9.4 0.0 collective-permute-done.1
  9.4 0.0 collective-permute-done
  9.4 1.6 %collective-permute-start.4 = (bf16[3,112,128]{2,1,0:T(8,128)(2,1)S(1)}, bf16[3,112,128]{2,1,0:T(8,128)(2,1)S(1)}, u32[]{:S(2)}, u32[]{:S(2)}) collective-permute-start(bf16[3,112,128]{2,1,0:T(8,128)(2,1)S(1)} %pad_maximum_fusion.2), channel_id=1, source_target_pairs={{0,2},{1,3},{2,0},{3,1},{4,6},{5,7},{6,4},{7,5},{8,10},{9,11},{10,... | collective-permute-start | bytes 258056 | tf_op jit(solution)/shard_map/ppermute | solution.py:258
  11.0 0.0 collective-permute-done.2
  11.0 1.3 %collective-permute-start.5 = (bf16[1,112,128]{2,1,0:T(8,128)(2,1)S(1)}, bf16[1,112,128]{2,1,0:T(8,128)(2,1)S(1)}, u32[]{:S(2)}, u32[]{:S(2)}) collective-permute-start(bf16[1,112,128]{2,1,0:T(8,128)(2,1)S(1)} %bitcast.5), channel_id=1, source_target_pairs={{0,2},{1,3},{2,0},{3,1},{4,6},{5,7},{6,4},{7,5},{8,10},{9,11},{10,... | collective-permute-start | bytes 86024 | tf_op jit(solution)/shard_map/ppermute | solution.py:258
  12.3 0.1 collective-permute-start.3
  12.4 0.7 %first.1 = (f32[800,128]{1,0:T(8,128)S(1)}, f32[400,128]{1,0:T(8,128)S(1)}, f32[400,128]{1,0:T(8,128)S(1)}, f32[400,128]{1,0:T(8,128)S(1)}) custom-call(bf16[4,112,128]{2,1,0:T(8,128)(2,1)S(1)} %pad_maximum_fusion.tiles.part0, f32[112,128]{1,0:T(8,128)S(1)} %get-tuple-element.21.own_ref, bf16[128,1536]{1,0:T(8,128)(2,1)S(1)} %weights.1.weights_ref), custom_call_target="tpu_custom_call" | custom-call | flops 1024 | tf_op jit(solution)/shard_map/first/pallas_call | solution.py:276
  13.1 1.7 %collective-permute-done.5 = bf16[1,112,128]{2,1,0:T(8,128)(2,1)S(1)} collective-permute-done((bf16[1,112,128]{2,1,0:T(8,128)(2,1)S(1)}, bf16[1,112,128]{2,1,0:T(8,128)(2,1)S(1)}, u32[]{:S(2)}, u32[]{:S(2)}) %collective-permute-start.5) | collective-permute-done | bytes 28704 | tf_op jit(solution)/shard_map/ppermute | solution.py:258
  14.8 0.0 collective-permute-done.4
  14.9 0.1 collective-permute-start.6
  14.9 0.0 collective-permute-done.3.tiles.part1
  14.9 0.6 %second.1.before_ref = f32[800,128]{1,0:T(8,128)S(1)} custom-call(bf16[4,112,128]{2,1,0:T(8,128)(2,1)S(1)} %collective-permute-done.3.tiles.part1, bf16[128,1536]{1,0:T(8,128)(2,1)S(1)} %weights.1.weights_ref, f32[800,128]{1,0:T(8,128)S(1)} %get-tuple-element.25.before_ref), custom_call_target="tpu_custom_call" | custom-call | flops 1024 | tf_op jit(solution)/shard_map/second/pallas_call | solution.py:276
  15.6 0.6 %third.1.before_ref = f32[800,128]{1,0:T(8,128)S(1)} custom-call(bf16[4,112,128]{2,1,0:T(8,128)(2,1)S(1)} %pad_maximum_fusion.1.tiles.part2, bf16[128,1536]{1,0:T(8,128)(2,1)S(1)} %weights.1.weights_ref, f32[800,128]{1,0:T(8,128)S(1)} %second.1.before_ref), custom_call_target="tpu_custom_call" | custom-call | flops 1024 | tf_op jit(solution)/shard_map/third/pallas_call | solution.py:276
  16.2 0.0 collective-permute-done.6.part3
  16.2 2.4 %last.1 = f32[10,10,128]{2,1,0:T(8,128)} custom-call(bf16[4,112,128]{2,1,0:T(8,128)(2,1)S(1)} %pad_maximum_fusion.tiles.part0, bf16[4,112,128]{2,1,0:T(8,128)(2,1)S(1)} %collective-permute-done.3.tiles.part1, bf16[4,112,128]{2,1,0:T(8,128)(2,1)S(1)} %pad_maximum_fusion.1.tiles.part2, bf16[4,112,128]{2,1,0:T(8,128)(2,1)S(1)} %collective-permute-done.6.part3, ...), custom_call_target="tpu_custom_call" | custom-call | flops 1024 | tf_op jit(solution)/shard_map/last/pallas_call | solution.py:276
  (3 shorter events, 0.0 us)
Async XLA Ops:
  1.2 8.1 %collective-permute-start.1 = (bf16[112,128]{1,0:T(8,128)(2,1)S(1)}, bf16[112,128]{1,0:T(8,128)(2,1)S(1)}, u32[]{:S(2)}, u32[]{:S(2)}) collective-permute-start(bf16[112,128]{1,0:T(8,128)(2,1)S(1)} %get-tuple-element.18), channel_id=1, source_target_pairs={{0,4},{1,5},{2,6},{3,7},{4,8},{5,9},{6,10},{7,11},{8,12},{9,13},{1... | collective-permute-start | bytes 86024 | tf_op jit(solution)/shard_map/ppermute | solution.py:268
  4.3 5.1 %collective-permute-start = (bf16[112,128]{1,0:T(8,128)(2,1)S(1)}, bf16[112,128]{1,0:T(8,128)(2,1)S(1)}, u32[]{:S(2)}, u32[]{:S(2)}) collective-permute-start(bf16[112,128]{1,0:T(8,128)(2,1)S(1)} %get-tuple-element.18), channel_id=1, source_target_pairs={{0,8},{1,9},{2,10},{3,11},{4,12},{5,13},{6,14},{7,15},{8,0},{9,1},... | collective-permute-start | bytes 86024 | tf_op jit(solution)/shard_map/ppermute | solution.py:268
  6.9 4.1 %collective-permute-start.2 = (bf16[112,128]{1,0:T(8,128)(2,1)S(1)}, bf16[112,128]{1,0:T(8,128)(2,1)S(1)}, u32[]{:S(2)}, u32[]{:S(2)}) collective-permute-start(bf16[112,128]{1,0:T(8,128)(2,1)S(1)} %get-tuple-element.18), channel_id=1, source_target_pairs={{0,12},{1,13},{2,14},{3,15},{4,0},{5,1},{6,2},{7,3},{8,4},{9,5},{1... | collective-permute-start | bytes 86024 | tf_op jit(solution)/shard_map/ppermute | solution.py:268
  9.4 5.4 %collective-permute-start.4 = (bf16[3,112,128]{2,1,0:T(8,128)(2,1)S(1)}, bf16[3,112,128]{2,1,0:T(8,128)(2,1)S(1)}, u32[]{:S(2)}, u32[]{:S(2)}) collective-permute-start(bf16[3,112,128]{2,1,0:T(8,128)(2,1)S(1)} %pad_maximum_fusion.2), channel_id=1, source_target_pairs={{0,2},{1,3},{2,0},{3,1},{4,6},{5,7},{6,4},{7,5},{8,10},{9,11},{10,... | collective-permute-start | bytes 258056 | tf_op jit(solution)/shard_map/ppermute | solution.py:258
  11.0 3.9 %collective-permute-start.5 = (bf16[1,112,128]{2,1,0:T(8,128)(2,1)S(1)}, bf16[1,112,128]{2,1,0:T(8,128)(2,1)S(1)}, u32[]{:S(2)}, u32[]{:S(2)}) collective-permute-start(bf16[1,112,128]{2,1,0:T(8,128)(2,1)S(1)} %bitcast.5), channel_id=1, source_target_pairs={{0,2},{1,3},{2,0},{3,1},{4,6},{5,7},{6,4},{7,5},{8,10},{9,11},{10,... | collective-permute-start | bytes 86024 | tf_op jit(solution)/shard_map/ppermute | solution.py:258
  12.3 2.7 %collective-permute-start.3 = (bf16[4,112,128]{2,1,0:T(8,128)(2,1)S(1)}, bf16[4,112,128]{2,1,0:T(8,128)(2,1)S(1)}, u32[]{:S(2)}, u32[]{:S(2)}) collective-permute-start(bf16[4,112,128]{2,1,0:T(8,128)(2,1)S(1)} %pad_maximum_fusion.tiles.part0), channel_id=1, source_target_pairs={{0,1},{1,0},{2,3},{3,2},{4,5},{5,4},{6,7},{7,6},{8,9},{9,8},{10,11... | collective-permute-start | bytes 344072 | tf_op jit(solution)/shard_map/ppermute | solution.py:258
  14.9 1.4 %collective-permute-start.6 = (bf16[4,112,128]{2,1,0:T(8,128)(2,1)S(1)}, bf16[4,112,128]{2,1,0:T(8,128)(2,1)S(1)}, u32[]{:S(2)}, u32[]{:S(2)}) collective-permute-start(bf16[4,112,128]{2,1,0:T(8,128)(2,1)S(1)} %pad_maximum_fusion.1.tiles.part2), channel_id=1, source_target_pairs={{0,1},{1,0},{2,3},{3,2},{4,5},{5,4},{6,7},{7,6},{8,9},{9,8},{10,11... | collective-permute-start | bytes 344072 | tf_op jit(solution)/shard_map/ppermute | solution.py:258

commit v4 on v3

--- a/solution.py
+++ b/solution.py
@@ -84,20 +84,28 @@
     return 80 + 16 * k
 
 
-def pack_kernel(pair_ref, mask_ref, tile_ref, own_ref, send_ref):
-    own_ref[...] = jnp.zeros(own_ref.shape, own_ref.dtype)
-    send_ref[...] = jnp.zeros(send_ref.shape, send_ref.dtype)
-    valid = mask_ref[...]
+def pack_kernel(pair_ref, mask_ref, tile_ref, own_ref, valid_ref, pair_vmem, mask_vmem, sems):
+    pair_copy = pltpu.make_async_copy(pair_ref, pair_vmem, sems.at[0])
+    mask_copy = pltpu.make_async_copy(mask_ref, mask_vmem, sems.at[1])
+    pair_copy.start()
+    mask_copy.start()
+    rest = pl.ds(MAIN * SIDE, ROWS - MAIN * SIDE)
+    own_ref[rest, :] = jnp.zeros((ROWS - MAIN * SIDE, 128), own_ref.dtype)
+    valid_ref[rest, :] = jnp.zeros((ROWS - MAIN * SIDE, 128), valid_ref.dtype)
+    mask_copy.wait()
+    valid = mask_vmem[...].astype(jnp.float32)
     for k in range(SIDE):
-        rows = pair_ref[:, k, :]
-        centred = rows - jnp.mean(rows, axis=-1, keepdims=True)
-        sent = jnp.where(valid[:, k : k + 1] > 0, centred, MASKED)
-        own_ref[pl.ds(MAIN * k, MAIN), :] = rows[:MAIN]
-        send_ref[pl.ds(MAIN * k, MAIN), :] = sent[:MAIN]
+        column = jnp.broadcast_to(valid[:, k : k + 1], (SIDE, 128))
+        valid_ref[pl.ds(MAIN * k, MAIN), :] = column[:MAIN]
         for e in range(REST):
-            own_ref[pl.ds(rest_rows(e) + k, 1), :] = rows[MAIN + e : MAIN + e + 1]
-            send_ref[pl.ds(rest_rows(e) + k, 1), :] = sent[MAIN + e : MAIN + e + 1]
-    tile_ref[...] = send_ref[...].astype(tile_ref.dtype)
+            valid_ref[pl.ds(rest_rows(e) + k, 1), :] = column[MAIN + e : MAIN + e + 1]
+    pair_copy.wait()
+    for i in range(SIDE):
+        at = pl.ds(i, SIDE, stride=MAIN) if i < MAIN else pl.ds(rest_rows(i - MAIN), SIDE)
+        own_ref[at, :] = pair_vmem[i]
+    own = own_ref[...]
+    centred = own - jnp.mean(own, axis=-1, keepdims=True)
+    tile_ref[...] = jnp.where(valid_ref[...] > 0.5, centred, MASKED).astype(tile_ref.dtype)
 
 
 OUT_PROJ, OUT_GATE, OUT_FINAL, IN_PROJ, IN_GATE, IN_FINAL, WEIGHTS = 0, 512, 640, 768, 1280, 1408, 1536
@@ -125,16 +133,16 @@
 GROUP = 4
 
 
-def add_terms(tiles, other, weights_ref, before_ref, outer_ref, lines_ref, right_lines_ref, left_ref, right_ref):
+def add_terms(tiles, other, proj_weight, before_ref, outer_ref, lines_ref, right_lines_ref, left_ref, right_ref):
     for slot in range(SPLIT):
         to_lines(lines_ref, 0, tiles[slot].astype(jnp.float32), slot, SPLIT, WIDTH)
     to_lines(right_lines_ref, 0, tiles[0].astype(jnp.float32), 0, 2, RIGHT_LINE)
     to_lines(right_lines_ref, 0, tiles[other].astype(jnp.float32), 1, 2, RIGHT_LINE)
     raw = jnp.concatenate([lines_ref[...], right_lines_ref[...]], axis=0)
     normed = scaled(split_lines(raw)[0])
-    proj = dot(normed[:LENGTH], weights_ref[:, pl.ds(OUT_PROJ, 256)])
+    proj = dot(normed[:LENGTH], proj_weight[:, :256])
     left_ref[...] = sigmoid(proj[:, :128]) * proj[:, 128:]
-    proj = dot(normed[LENGTH:], weights_ref[:, pl.ds(OUT_PROJ + 256, 256)])
+    proj = dot(normed[LENGTH:], proj_weight[:, 256:])
     right_ref[...] = sigmoid(proj[:, :128]) * proj[:, 128:]
 
     for g in range(2 * SIDE // GROUP):
@@ -167,11 +175,19 @@
     return jnp.bitwise_xor(lax.axis_index("row"), lax.axis_index("col"))
 
 
-def first_kernel(
-    tiles, own_ref, weights_ref, outer_ref, centred_ref, gate_ref, valid_ref, *scratch
-):
-    lines_ref = scratch[0]
-    add_terms(tiles, other_slot(), weights_ref, None, outer_ref, *scratch)
+def first_kernel(tiles, out_proj_ref, outer_ref, *scratch):
+    add_terms(tiles, other_slot(), out_proj_ref[...].astype(jnp.bfloat16), None, outer_ref, *scratch)
+
+
+def next_kernel(tiles, weights_ref, before_ref, outer_ref, *scratch):
+    add_terms(tiles, other_slot(), weights_ref[:, pl.ds(OUT_PROJ, 512)], before_ref, outer_ref, *scratch)
+
+
+def gate_kernel(tiles, own_tiles, own_ref, weights_ref, before_ref, outer_ref, centred_ref, gate_ref, valid_ref, *scratch):
+    add_terms(tiles, other_slot(), weights_ref[:, pl.ds(OUT_PROJ, 512)], before_ref, outer_ref, *scratch[:-1])
+    lines_ref = scratch[-1]
+    for slot in range(SPLIT):
+        to_lines(lines_ref, 0, own_tiles[slot].astype(jnp.float32), slot, SPLIT, WIDTH)
     centred, valid = split_lines(lines_ref[...])
     centred_ref[...] = centred
     valid_ref[...] = jnp.where(valid, 1.0, 0.0)
@@ -179,10 +195,6 @@
     own = own - jnp.mean(own, axis=-1, keepdims=True)
     to_lines(centred_ref, 0, own, 0, SPLIT, WIDTH)
     gate_ref[...] = sigmoid(dot(scaled(centred_ref[...]), weights_ref[:, pl.ds(OUT_GATE, 128)]))
-
-
-def next_kernel(tiles, weights_ref, before_ref, outer_ref, *scratch):
-    add_terms(tiles, other_slot(), weights_ref, before_ref, outer_ref, *scratch)
 
 
 def last_kernel(
@@ -199,7 +211,7 @@
                 to_lines(block_ref, 0, tiles[slot].astype(jnp.float32), slot, SPLIT, WIDTH)
 
     add_terms(
-        part3, other_slot(), weights_ref, before_ref, outer_ref,
+        part3, other_slot(), weights_ref[:, pl.ds(OUT_PROJ, 512)], before_ref, outer_ref,
         lines_ref, right_lines_ref, left_ref, right_ref,
     )
 
@@ -258,12 +270,12 @@
     return lax.ppermute(value, ("row", "col"), pairs)
 
 
-STEPS = (2, 1, 3)
-
-
-def shifted(value, step):
+STEPS = (1, 2, 3)
+
+
+def shifted(value, step, cols=0):
     pairs = [
-        (r * SPLIT + c, (r + step) % SPLIT * SPLIT + c) for r in range(SPLIT) for c in range(SPLIT)
+        (r * SPLIT + c, (r + step) % SPLIT * SPLIT + (c ^ cols)) for r in range(SPLIT) for c in range(SPLIT)
     ]
     return lax.ppermute(value, ("row", "col"), pairs)
 
@@ -272,14 +284,15 @@
     return pltpu.with_memory_space_constraint(value, pltpu.VMEM)
 
 
-def call(kernel, name, cycles, out, scratch, *operands, grant=32 << 20):
+def call(kernel, name, cycles, out, scratch, *operands, grant=32 << 20, **more):
     return pl.pallas_call(
         kernel,
         out_shape=out,
-        scratch_shapes=[pltpu.VMEM(shape, jnp.float32) for shape in scratch],
+        scratch_shapes=[pltpu.VMEM(one, jnp.float32) if isinstance(one, tuple) else one for one in scratch],
         cost_estimate=pl.CostEstimate(flops=cycles, bytes_accessed=0, transcendentals=0),
         compiler_params=pltpu.CompilerParams(vmem_limit_bytes=grant),
         name=name,
+        **more,
     )(*operands)
 
 
@@ -287,29 +300,32 @@
     f32 = jnp.float32
     tile, own = call(
         pack_kernel, "pack", 1000, (pltpu.VMEM((ROWS, 128), jnp.bfloat16), pltpu.VMEM((ROWS, 128), f32)),
-        [(ROWS, 128)], pair, pair_mask, grant=None,
-    )
-    weights = call(
-        weights_kernel, "weights", 1000, pltpu.VMEM((128, WEIGHTS), jnp.bfloat16), [], *weights, grant=None
+        [(ROWS, 128), pair.shape, pltpu.VMEM(pair_mask.shape, jnp.int32), pltpu.SemaphoreType.DMA((2,))],
+        pair, pair_mask, grant=None, in_specs=2 * [pl.BlockSpec(memory_space=pl.ANY)],
     )
     around = [tile] + [shifted(tile, step) for step in STEPS]
-    early, weights = lax.optimization_barrier((jnp.stack(around[:3]), weights))
-    weights = in_vmem(weights)
+    aslant = shifted(tile, STEPS[2], 2)
+    early = jnp.stack(around[:3])
     swapped_early = swapped(early, 0, 2)
-    last, _ = lax.optimization_barrier((around[3], early))
-    late = last[None]
-    part0 = jnp.concatenate([early, late])
-    part2 = jnp.concatenate([swapped_early, swapped(late, 0, 2)])
+    late, _ = lax.optimization_barrier((around[3], early))
+    part0 = jnp.concatenate([early, late[None]])
     lines = pltpu.VMEM((LENGTH, 128), f32)
     sums = pltpu.VMEM((2 * LENGTH, 128), f32)
     work = [(LENGTH, 128), (SIDE * RIGHT_LINE, 128), (LENGTH, 128), (SIDE * RIGHT_LINE, 128)]
     cost = 1 << 10
+    outer = call(first_kernel, "first", cost, sums, work, in_vmem(part0), in_vmem(weights[0]))
+    outer, *weights = lax.optimization_barrier((outer, *weights))
+    weights = call(
+        weights_kernel, "weights", 1000, pltpu.VMEM((128, WEIGHTS), jnp.bfloat16), [], *weights, grant=None
+    )
+    aslant, swapped_early, outer, weights = lax.optimization_barrier((aslant, swapped_early, outer, weights))
+    part2 = jnp.concatenate([swapped_early, aslant[None]])
+    weights = in_vmem(weights)
+    part1 = swapped(part0, 0, 1)
     outer, centred0, gate0, valid0 = call(
-        first_kernel, "first", cost, (sums, lines, lines, lines), work, in_vmem(part0), in_vmem(own), weights
-    )
-    part2, outer = lax.optimization_barrier((part2, outer))
-    part1 = swapped(part0, 0, 1)
-    outer = call(next_kernel, "second", cost, sums, work, in_vmem(part1), weights, in_vmem(outer))
+        gate_kernel, "second", cost, (sums, lines, lines, lines), work + [(LENGTH, 128)],
+        *map(in_vmem, (part1, part0, own)), weights, in_vmem(outer),
+    )
     part3 = swapped(part2, 0, 1)
     outer = call(next_kernel, "third", cost, sums, work, in_vmem(part2), weights, in_vmem(outer))
     part3, outer = lax.optimization_barrier((part3, outer))

time: 18.8 us -> 18.1 us (0.963)
  waiting for transfers between devices: 1.77 us -> 1.39 us
  Pallas kernels: 6.72 us -> 6.48 us
    ppermute x4 -> x3, starting transfers between devices: 2.99 us -> 1.45 us  [swapped(): return lax.ppermute(value, ('row', 'col'), pairs)]
    ppermute x3 -> x4, starting transfers between devices: 7.01 us -> 8.39 us  [shifted(): return lax.ppermute(value, ('row', 'col'), pairs)]
    ppermute x4 -> x3, waiting for transfers between devices: 1.76 us -> 1.19 us  [swapped(): return lax.ppermute(value, ('row', 'col'), pairs)]
    pallas_call x6, Pallas kernels: 6.72 us -> 6.48 us  [call(): pl.pallas_call(kernel, out_shape=out, scratch_shapes=[pltpu.VMEM(one, jnp...]
    ppermute x3 -> x4, waiting for transfers between devices: 0.01 us -> 0.21 us  [shifted(): return lax.ppermute(value, ('row', 'col'), pairs)]
  transfers between devices with their start and end apart: 7 -> 7, of which waited for: 1 -> 2; matrix products, arithmetic and copies ran while one was open for 0% -> 0% of each run, Pallas kernels for 17% -> 17%
where the time goes in v4:
time: 18.1 us; the launch traced here: 17.9 us
  starting transfers between devices  9.84 us (54%)
  Pallas kernels  6.48 us (36%)
  waiting for transfers between devices  1.39 us (8%)
    ppermute x4, starting transfers between devices, shifted(): return lax.ppermute(value, ('row', 'col'), pairs)  8.39 us
    pallas_call x6, Pallas kernels, call(): pl.pallas_call(kernel, out_shape=out, scratch_shapes=[pltpu.VMEM(one, jnp...  6.48 us
    ppermute x3, starting transfers between devices, swapped(): return lax.ppermute(value, ('row', 'col'), pairs)  1.45 us
    ppermute x3, waiting for transfers between devices, swapped(): return lax.ppermute(value, ('row', 'col'), pairs)  1.19 us
  transfers between devices with their start and end apart: 7, of which 2 were waited for; matrix products, arithmetic and copies ran while one was open for 0% of the time, Pallas kernels for 17%

profile of v4, /device:TPU:0, one launch (start us, length us, event | category | flops | bytes accessed | tf_op | source)
XLA Modules:
  0.0 17.9 jit_solution(12851434031069421792)
XLA Ops:
  0.0 0.0 copy-start
  0.0 1.0 %pack.1 = (bf16[112,128]{1,0:T(8,128)(2,1)S(1)}, f32[112,128]{1,0:T(8,128)S(1)}) custom-call(f32[10,10,128]{2,1,0:T(8,128)} %pair_ref.1, s32[10,10]{1,0:T(8,128)} %mask_ref.1), custom_call_target="tpu_custom_call" | custom-call | flops 1000 | tf_op jit(solution)/shard_map/pack/pallas_call | solution.py:288
  1.0 3.1 %collective-permute-start = (bf16[112,128]{1,0:T(8,128)(2,1)S(1)}, bf16[112,128]{1,0:T(8,128)(2,1)S(1)}, u32[]{:S(2)}, u32[]{:S(2)}) collective-permute-start(bf16[112,128]{1,0:T(8,128)(2,1)S(1)} %get-tuple-element.25), channel_id=1, source_target_pairs={{0,4},{1,5},{2,6},{3,7},{4,8},{5,9},{6,10},{7,11},{8,12},{9,13},{1... | collective-permute-start | bytes 86024 | tf_op jit(solution)/shard_map/ppermute | solution.py:280
  4.1 2.6 %collective-permute-start.1 = (bf16[112,128]{1,0:T(8,128)(2,1)S(1)}, bf16[112,128]{1,0:T(8,128)(2,1)S(1)}, u32[]{:S(2)}, u32[]{:S(2)}) collective-permute-start(bf16[112,128]{1,0:T(8,128)(2,1)S(1)} %get-tuple-element.25), channel_id=1, source_target_pairs={{0,8},{1,9},{2,10},{3,11},{4,12},{5,13},{6,14},{7,15},{8,0},{9,1},... | collective-permute-start | bytes 86024 | tf_op jit(solution)/shard_map/ppermute | solution.py:280
  6.7 1.3 %collective-permute-start.2 = (bf16[112,128]{1,0:T(8,128)(2,1)S(1)}, bf16[112,128]{1,0:T(8,128)(2,1)S(1)}, u32[]{:S(2)}, u32[]{:S(2)}) collective-permute-start(bf16[112,128]{1,0:T(8,128)(2,1)S(1)} %get-tuple-element.25), channel_id=1, source_target_pairs={{0,12},{1,13},{2,14},{3,15},{4,0},{5,1},{6,2},{7,3},{8,4},{9,5},{1... | collective-permute-start | bytes 86024 | tf_op jit(solution)/shard_map/ppermute | solution.py:280
  8.0 1.4 %collective-permute-start.4 = (bf16[112,128]{1,0:T(8,128)(2,1)S(1)}, bf16[112,128]{1,0:T(8,128)(2,1)S(1)}, u32[]{:S(2)}, u32[]{:S(2)}) collective-permute-start(bf16[112,128]{1,0:T(8,128)(2,1)S(1)} %get-tuple-element.25), channel_id=1, source_target_pairs={{0,14},{1,15},{2,12},{3,13},{4,2},{5,3},{6,0},{7,1},{8,6},{9,7},{1... | collective-permute-start | bytes 86024 | tf_op jit(solution)/shard_map/ppermute | solution.py:280
  9.4 0.0 collective-permute-done
  9.4 0.0 collective-permute-done.1
  9.4 1.3 %collective-permute-start.5 = (bf16[3,112,128]{2,1,0:T(8,128)(2,1)S(1)}, bf16[3,112,128]{2,1,0:T(8,128)(2,1)S(1)}, u32[]{:S(2)}, u32[]{:S(2)}) collective-permute-start(bf16[3,112,128]{2,1,0:T(8,128)(2,1)S(1)} %pad_maximum_fusion.2), channel_id=1, source_target_pairs={{0,2},{1,3},{2,0},{3,1},{4,6},{5,7},{6,4},{7,5},{8,10},{9,11},{10,... | collective-permute-start | bytes 258056 | tf_op jit(solution)/shard_map/ppermute | solution.py:270
  10.7 0.0 collective-permute-done.2
  10.7 0.1 collective-permute-start.3
  10.8 0.0 copy-done
  10.8 0.6 %first.1.before_ref = f32[800,128]{1,0:T(8,128)S(1)} custom-call(bf16[4,112,128]{2,1,0:T(8,128)(2,1)S(1)} %pad_maximum_fusion.tiles.own_tiles.part0, f32[128,512]{1,0:T(8,128)S(1)} %copy-done), custom_call_target="tpu_custom_call" | custom-call | flops 1024 | tf_op jit(solution)/shard_map/first/pallas_call | solution.py:288
  11.4 1.1 %weights.1.weights_ref = bf16[128,1536]{1,0:T(8,128)(2,1)S(1)} custom-call(f32[128,512]{1,0:T(8,128)} %refs_0_, f32[128,128]{1,0:T(8,128)} %refs_1_, f32[128,128]{1,0:T(8,128)} %refs_2_, f32[128,512]{1,0:T(8,128)} %refs_3_, f32[128,128]{1,0:T(8,128)} %refs_4_, f32[128,128]{1,0:T(8,128)} %refs_5_), custom_call_target="tpu_custom_call" | custom-call | flops 1000 | tf_op jit(solution)/shard_map/weights/pallas_call | solution.py:288
  12.6 0.2 %collective-permute-done.4 = bf16[112,128]{1,0:T(8,128)(2,1)S(1)} collective-permute-done((bf16[112,128]{1,0:T(8,128)(2,1)S(1)}, bf16[112,128]{1,0:T(8,128)(2,1)S(1)}, u32[]{:S(2)}, u32[]{:S(2)}) %collective-permute-start.4) | collective-permute-done | bytes 28704 | tf_op jit(solution)/shard_map/ppermute | solution.py:280
  12.8 1.2 %collective-permute-done.5 = bf16[3,112,128]{2,1,0:T(8,128)(2,1)S(1)} collective-permute-done((bf16[3,112,128]{2,1,0:T(8,128)(2,1)S(1)}, bf16[3,112,128]{2,1,0:T(8,128)(2,1)S(1)}, u32[]{:S(2)}, u32[]{:S(2)}) %collective-permute-start.5) | collective-permute-done | bytes 86048 | tf_op jit(solution)/shard_map/ppermute | solution.py:270
  14.0 0.1 collective-permute-start.6
  14.0 0.0 collective-permute-done.3.tiles.part1
  14.1 0.7 %second.1 = (f32[800,128]{1,0:T(8,128)S(1)}, f32[400,128]{1,0:T(8,128)S(1)}, f32[400,128]{1,0:T(8,128)S(1)}, f32[400,128]{1,0:T(8,128)S(1)}) custom-call(bf16[4,112,128]{2,1,0:T(8,128)(2,1)S(1)} %collective-permute-done.3.tiles.part1, bf16[4,112,128]{2,1,0:T(8,128)(2,1)S(1)} %pad_maximum_fusion.tiles.own_tiles.part0, ...), custom_call_target="tpu_custom_call" | custom-call | flops 1024 | tf_op jit(solution)/shard_map/second/pallas_call | solution.py:288
  14.8 0.6 %third.1.before_ref = f32[800,128]{1,0:T(8,128)S(1)} custom-call(bf16[4,112,128]{2,1,0:T(8,128)(2,1)S(1)} %pad_maximum_fusion.1.tiles.part2, bf16[128,1536]{1,0:T(8,128)(2,1)S(1)} %weights.1.weights_ref, f32[800,128]{1,0:T(8,128)S(1)} %get-tuple-element.39.before_ref), custom_call_target="tpu_custom_call" | custom-call | flops 1024 | tf_op jit(solution)/shard_map/third/pallas_call | solution.py:288
  15.5 0.0 collective-permute-done.6.part3
  15.5 2.4 %last.1 = f32[10,10,128]{2,1,0:T(8,128)} custom-call(bf16[4,112,128]{2,1,0:T(8,128)(2,1)S(1)} %pad_maximum_fusion.tiles.own_tiles.part0, bf16[4,112,128]{2,1,0:T(8,128)(2,1)S(1)} %collective-permute-done.3.tiles.part1, bf16[4,112,128]{2,1,0:T(8,128)(2,1)S(1)} %pad_maximum_fusion.1.tiles.part2, bf16[4,112,128]{2,1,0:T(8,128)(2,1)S(1)} %collective-permute-done.6.part3, ...), custom_call_target="tpu_custom_call" | custom-call | flops 1024 | tf_op jit(solution)/shard_map/last/pallas_call | solution.py:288
  (3 shorter events, 0.0 us)
Async XLA Ops:
  0.0 10.8 %copy-start = (f32[128,512]{1,0:T(8,128)S(1)}, f32[128,512]{1,0:T(8,128)}, u32[]{:S(2)}) copy-start(f32[128,512]{1,0:T(8,128)} %refs_0_) | copy-start | bytes 786436
  1.0 8.4 %collective-permute-start = (bf16[112,128]{1,0:T(8,128)(2,1)S(1)}, bf16[112,128]{1,0:T(8,128)(2,1)S(1)}, u32[]{:S(2)}, u32[]{:S(2)}) collective-permute-start(bf16[112,128]{1,0:T(8,128)(2,1)S(1)} %get-tuple-element.25), channel_id=1, source_target_pairs={{0,4},{1,5},{2,6},{3,7},{4,8},{5,9},{6,10},{7,11},{8,12},{9,13},{1... | collective-permute-start | bytes 86024 | tf_op jit(solution)/shard_map/ppermute | solution.py:280
  4.1 5.3 %collective-permute-start.1 = (bf16[112,128]{1,0:T(8,128)(2,1)S(1)}, bf16[112,128]{1,0:T(8,128)(2,1)S(1)}, u32[]{:S(2)}, u32[]{:S(2)}) collective-permute-start(bf16[112,128]{1,0:T(8,128)(2,1)S(1)} %get-tuple-element.25), channel_id=1, source_target_pairs={{0,8},{1,9},{2,10},{3,11},{4,12},{5,13},{6,14},{7,15},{8,0},{9,1},... | collective-permute-start | bytes 86024 | tf_op jit(solution)/shard_map/ppermute | solution.py:280
  6.7 4.1 %collective-permute-start.2 = (bf16[112,128]{1,0:T(8,128)(2,1)S(1)}, bf16[112,128]{1,0:T(8,128)(2,1)S(1)}, u32[]{:S(2)}, u32[]{:S(2)}) collective-permute-start(bf16[112,128]{1,0:T(8,128)(2,1)S(1)} %get-tuple-element.25), channel_id=1, source_target_pairs={{0,12},{1,13},{2,14},{3,15},{4,0},{5,1},{6,2},{7,3},{8,4},{9,5},{1... | collective-permute-start | bytes 86024 | tf_op jit(solution)/shard_map/ppermute | solution.py:280
  8.0 4.8 %collective-permute-start.4 = (bf16[112,128]{1,0:T(8,128)(2,1)S(1)}, bf16[112,128]{1,0:T(8,128)(2,1)S(1)}, u32[]{:S(2)}, u32[]{:S(2)}) collective-permute-start(bf16[112,128]{1,0:T(8,128)(2,1)S(1)} %get-tuple-element.25), channel_id=1, source_target_pairs={{0,14},{1,15},{2,12},{3,13},{4,2},{5,3},{6,0},{7,1},{8,6},{9,7},{1... | collective-permute-start | bytes 86024 | tf_op jit(solution)/shard_map/ppermute | solution.py:280
  9.4 4.6 %collective-permute-start.5 = (bf16[3,112,128]{2,1,0:T(8,128)(2,1)S(1)}, bf16[3,112,128]{2,1,0:T(8,128)(2,1)S(1)}, u32[]{:S(2)}, u32[]{:S(2)}) collective-permute-start(bf16[3,112,128]{2,1,0:T(8,128)(2,1)S(1)} %pad_maximum_fusion.2), channel_id=1, source_target_pairs={{0,2},{1,3},{2,0},{3,1},{4,6},{5,7},{6,4},{7,5},{8,10},{9,11},{10,... | collective-permute-start | bytes 258056 | tf_op jit(solution)/shard_map/ppermute | solution.py:270
  10.7 3.3 %collective-permute-start.3 = (bf16[4,112,128]{2,1,0:T(8,128)(2,1)S(1)}, bf16[4,112,128]{2,1,0:T(8,128)(2,1)S(1)}, u32[]{:S(2)}, u32[]{:S(2)}) collective-permute-start(bf16[4,112,128]{2,1,0:T(8,128)(2,1)S(1)} %pad_maximum_fusion.tiles.own_tiles.part0), channel_id=1, source_target_pairs={{0,1},{1,0},{2,3},{3,2},{4,5},{5,4},{6,7},{7,6},{8,9},{9,8},{10,11... | collective-permute-start | bytes 344072 | tf_op jit(solution)/shard_map/ppermute | solution.py:270
  14.0 1.5 %collective-permute-start.6 = (bf16[4,112,128]{2,1,0:T(8,128)(2,1)S(1)}, bf16[4,112,128]{2,1,0:T(8,128)(2,1)S(1)}, u32[]{:S(2)}, u32[]{:S(2)}) collective-permute-start(bf16[4,112,128]{2,1,0:T(8,128)(2,1)S(1)} %pad_maximum_fusion.1.tiles.part2), channel_id=1, source_target_pairs={{0,1},{1,0},{2,3},{3,2},{4,5},{5,4},{6,7},{7,6},{8,9},{9,8},{10,11... | collective-permute-start | bytes 344072 | tf_op jit(solution)/shard_map/ppermute | solution.py:270

commit v5 on v4

--- a/solution.py
+++ b/solution.py
@@ -68,12 +68,22 @@
     return finish(middle, inner, gate2, in_final)
 
 
-def sigmoid(value):
-    return 0.5 * jnp.tanh(0.5 * value) + 0.5
+def gated(half_gate, half_value):
+    return (jnp.tanh(half_gate) + 1.0) * half_value
+
+
+def halved(weight):
+    return (0.5 * weight).astype(jnp.bfloat16)
 
 
 def dot(value, weight):
     return jnp.dot(value.astype(jnp.bfloat16), weight, preferred_element_type=jnp.float32)
+
+
+def layer_norm_once(value):
+    mean = jnp.mean(value, axis=-1, keepdims=True)
+    variance = jnp.maximum(jnp.mean(value * value, axis=-1, keepdims=True) - mean * mean, 0.0)
+    return (value - mean) * lax.rsqrt(variance + 1e-05)
 
 
 def scaled(centred):
@@ -115,7 +125,7 @@
     start = 0
     for weight_ref in refs[:-1]:
         width = weight_ref.shape[1]
-        refs[-1][:, pl.ds(start, width)] = weight_ref[...].astype(refs[-1].dtype)
+        refs[-1][:, pl.ds(start, width)] = halved(weight_ref[...])
         start += width
 
 
@@ -141,9 +151,9 @@
     raw = jnp.concatenate([lines_ref[...], right_lines_ref[...]], axis=0)
     normed = scaled(split_lines(raw)[0])
     proj = dot(normed[:LENGTH], proj_weight[:, :256])
-    left_ref[...] = sigmoid(proj[:, :128]) * proj[:, 128:]
+    left_ref[...] = gated(proj[:, :128], proj[:, 128:])
     proj = dot(normed[LENGTH:], proj_weight[:, 256:])
-    right_ref[...] = sigmoid(proj[:, :128]) * proj[:, 128:]
+    right_ref[...] = gated(proj[:, :128], proj[:, 128:])
 
     for g in range(2 * SIDE // GROUP):
         at = [pl.ds((g * GROUP + t) * WIDTH, WIDTH) for t in range(GROUP)]
@@ -176,14 +186,14 @@
 
 
 def first_kernel(tiles, out_proj_ref, outer_ref, *scratch):
-    add_terms(tiles, other_slot(), out_proj_ref[...].astype(jnp.bfloat16), None, outer_ref, *scratch)
+    add_terms(tiles, other_slot(), halved(out_proj_ref[...]), None, outer_ref, *scratch)
 
 
 def next_kernel(tiles, weights_ref, before_ref, outer_ref, *scratch):
     add_terms(tiles, other_slot(), weights_ref[:, pl.ds(OUT_PROJ, 512)], before_ref, outer_ref, *scratch)
 
 
-def gate_kernel(tiles, own_tiles, own_ref, weights_ref, before_ref, outer_ref, centred_ref, gate_ref, valid_ref, *scratch):
+def gate_kernel(tiles, own_tiles, own_ref, weights_ref, before_ref, outer_ref, centred_ref, half_gate_ref, valid_ref, *scratch):
     add_terms(tiles, other_slot(), weights_ref[:, pl.ds(OUT_PROJ, 512)], before_ref, outer_ref, *scratch[:-1])
     lines_ref = scratch[-1]
     for slot in range(SPLIT):
@@ -194,11 +204,11 @@
     own = own_ref[...]
     own = own - jnp.mean(own, axis=-1, keepdims=True)
     to_lines(centred_ref, 0, own, 0, SPLIT, WIDTH)
-    gate_ref[...] = sigmoid(dot(scaled(centred_ref[...]), weights_ref[:, pl.ds(OUT_GATE, 128)]))
+    half_gate_ref[...] = dot(scaled(centred_ref[...]), weights_ref[:, pl.ds(OUT_GATE, 128)])
 
 
 def last_kernel(
-    part0, part1, part2, part3, before_ref, centred0_ref, gate0_ref, valid0_ref, own_ref,
+    part0, part1, part2, part3, before_ref, centred0_ref, half_gate0_ref, valid0_ref, own_ref,
     weights_ref,
     result_ref,
     lines_ref, right_lines_ref, left_ref, right_ref, outer_ref, block_ref, left2_ref, right2_ref, mid_ref, normed_ref,
@@ -222,17 +232,18 @@
         ]
 
     centred1, valid1 = split_lines(block_ref[...])
-    gate1 = sigmoid(dot(scaled(centred1), weights_ref[:, pl.ds(OUT_GATE, 128)]))
-    gate = jnp.concatenate([gate0_ref[...], gate1], axis=0)
+    half_gate1 = dot(scaled(centred1), weights_ref[:, pl.ds(OUT_GATE, 128)])
+    half_gate = jnp.concatenate([half_gate0_ref[...], half_gate1], axis=0)
     centred = jnp.concatenate([centred0_ref[...], centred1], axis=0)
-    change = gate * dot(layer_norm(jnp.concatenate(sums_of(1) + sums_of(0), axis=0)), weights_ref[:, pl.ds(OUT_FINAL, 128)])
+    normed = layer_norm(jnp.concatenate(sums_of(1) + sums_of(0), axis=0))
+    change = gated(half_gate, dot(normed, weights_ref[:, pl.ds(OUT_FINAL, 128)]))
     normed = layer_norm(centred + change)
     mid_ref[...] = change[:LENGTH]
     normed_ref[...] = normed[:LENGTH]
     proj = dot(normed[:LENGTH], weights_ref[:, pl.ds(IN_PROJ + 256, 256)])
-    right2_ref[...] = jnp.where(valid0_ref[...] > 0.5, sigmoid(proj[:, :128]) * proj[:, 128:], 0.0)
+    right2_ref[...] = valid0_ref[...] * gated(proj[:, :128], proj[:, 128:])
     proj = dot(normed[LENGTH:], weights_ref[:, pl.ds(IN_PROJ, 256)])
-    left2_ref[...] = jnp.where(valid1, sigmoid(proj[:, :128]) * proj[:, 128:], 0.0)
+    left2_ref[...] = jnp.where(valid1, gated(proj[:, :128], proj[:, 128:]), 0.0)
 
     for j in range(SIDE):
         right = right2_ref[pl.ds(j * WIDTH, WIDTH), :]
@@ -255,8 +266,8 @@
         return flat_ref[...]
 
     mid = own_ref[...] + own_rows(mid_ref, flat_ref)
-    gate = sigmoid(dot(own_rows(normed_ref, flat2_ref), weights_ref[:, pl.ds(IN_GATE, 128)]))
-    result = mid + gate * dot(layer_norm(inner), weights_ref[:, pl.ds(IN_FINAL, 128)])
+    half_gate = dot(own_rows(normed_ref, flat2_ref), weights_ref[:, pl.ds(IN_GATE, 128)])
+    result = mid + gated(half_gate, dot(layer_norm_once(inner), weights_ref[:, pl.ds(IN_FINAL, 128)]))
     for k in range(SIDE):
         result_ref[pl.ds(0, MAIN), k, :] = result[MAIN * k : MAIN * (k + 1)]
         for e in range(REST):

time: 18.1 us -> 17.9 us (0.989)
  no operation moved by 1% of the time
where the time goes in v5:
time: 17.9 us; the launch traced here: 17.7 us
  starting transfers between devices  9.84 us (55%)
  Pallas kernels  6.32 us (35%)
  waiting for transfers between devices  1.4 us (8%)
    ppermute x4, starting transfers between devices, shifted(): return lax.ppermute(value, ('row', 'col'), pairs)  8.39 us
    pallas_call x6, Pallas kernels, call(): pl.pallas_call(kernel, out_shape=out, scratch_shapes=[pltpu.VMEM(one, jnp...  6.32 us
    ppermute x3, starting transfers between devices, swapped(): return lax.ppermute(value, ('row', 'col'), pairs)  1.45 us
    ppermute x3, waiting for transfers between devices, swapped(): return lax.ppermute(value, ('row', 'col'), pairs)  1.19 us
  transfers between devices with their start and end apart: 7, of which 2 were waited for; matrix products, arithmetic and copies ran while one was open for 0% of the time, Pallas kernels for 17%

profile of v5, /device:TPU:0, one launch (start us, length us, event | category | flops | bytes accessed | tf_op | source)
XLA Modules:
  0.0 17.7 jit_solution(7435712357313827204)
XLA Ops:
  0.0 0.0 copy-start
  0.0 1.0 %pack.1 = (bf16[112,128]{1,0:T(8,128)(2,1)S(1)}, f32[112,128]{1,0:T(8,128)S(1)}) custom-call(f32[10,10,128]{2,1,0:T(8,128)} %pair_ref.1, s32[10,10]{1,0:T(8,128)} %mask_ref.1), custom_call_target="tpu_custom_call" | custom-call | flops 1000 | tf_op jit(solution)/shard_map/pack/pallas_call | solution.py:299
  1.0 3.1 %collective-permute-start = (bf16[112,128]{1,0:T(8,128)(2,1)S(1)}, bf16[112,128]{1,0:T(8,128)(2,1)S(1)}, u32[]{:S(2)}, u32[]{:S(2)}) collective-permute-start(bf16[112,128]{1,0:T(8,128)(2,1)S(1)} %get-tuple-element.25), channel_id=1, source_target_pairs={{0,4},{1,5},{2,6},{3,7},{4,8},{5,9},{6,10},{7,11},{8,12},{9,13},{1... | collective-permute-start | bytes 86024 | tf_op jit(solution)/shard_map/ppermute | solution.py:291
  4.1 2.6 %collective-permute-start.1 = (bf16[112,128]{1,0:T(8,128)(2,1)S(1)}, bf16[112,128]{1,0:T(8,128)(2,1)S(1)}, u32[]{:S(2)}, u32[]{:S(2)}) collective-permute-start(bf16[112,128]{1,0:T(8,128)(2,1)S(1)} %get-tuple-element.25), channel_id=1, source_target_pairs={{0,8},{1,9},{2,10},{3,11},{4,12},{5,13},{6,14},{7,15},{8,0},{9,1},... | collective-permute-start | bytes 86024 | tf_op jit(solution)/shard_map/ppermute | solution.py:291
  6.7 1.3 %collective-permute-start.2 = (bf16[112,128]{1,0:T(8,128)(2,1)S(1)}, bf16[112,128]{1,0:T(8,128)(2,1)S(1)}, u32[]{:S(2)}, u32[]{:S(2)}) collective-permute-start(bf16[112,128]{1,0:T(8,128)(2,1)S(1)} %get-tuple-element.25), channel_id=1, source_target_pairs={{0,12},{1,13},{2,14},{3,15},{4,0},{5,1},{6,2},{7,3},{8,4},{9,5},{1... | collective-permute-start | bytes 86024 | tf_op jit(solution)/shard_map/ppermute | solution.py:291
  8.0 1.4 %collective-permute-start.4 = (bf16[112,128]{1,0:T(8,128)(2,1)S(1)}, bf16[112,128]{1,0:T(8,128)(2,1)S(1)}, u32[]{:S(2)}, u32[]{:S(2)}) collective-permute-start(bf16[112,128]{1,0:T(8,128)(2,1)S(1)} %get-tuple-element.25), channel_id=1, source_target_pairs={{0,14},{1,15},{2,12},{3,13},{4,2},{5,3},{6,0},{7,1},{8,6},{9,7},{1... | collective-permute-start | bytes 86024 | tf_op jit(solution)/shard_map/ppermute | solution.py:291
  9.4 0.0 collective-permute-done
  9.4 0.0 collective-permute-done.1
  9.4 1.3 %collective-permute-start.5 = (bf16[3,112,128]{2,1,0:T(8,128)(2,1)S(1)}, bf16[3,112,128]{2,1,0:T(8,128)(2,1)S(1)}, u32[]{:S(2)}, u32[]{:S(2)}) collective-permute-start(bf16[3,112,128]{2,1,0:T(8,128)(2,1)S(1)} %pad_maximum_fusion.2), channel_id=1, source_target_pairs={{0,2},{1,3},{2,0},{3,1},{4,6},{5,7},{6,4},{7,5},{8,10},{9,11},{10,... | collective-permute-start | bytes 258056 | tf_op jit(solution)/shard_map/ppermute | solution.py:281
  10.7 0.0 collective-permute-done.2
  10.7 0.1 collective-permute-start.3
  10.8 0.0 copy-done
  10.8 0.6 %first.1.before_ref = f32[800,128]{1,0:T(8,128)S(1)} custom-call(bf16[4,112,128]{2,1,0:T(8,128)(2,1)S(1)} %pad_maximum_fusion.tiles.own_tiles.part0, f32[128,512]{1,0:T(8,128)S(1)} %copy-done), custom_call_target="tpu_custom_call" | custom-call | flops 1024 | tf_op jit(solution)/shard_map/first/pallas_call | solution.py:299
  11.4 1.1 %weights.1.weights_ref = bf16[128,1536]{1,0:T(8,128)(2,1)S(1)} custom-call(f32[128,512]{1,0:T(8,128)} %refs_0_, f32[128,128]{1,0:T(8,128)} %refs_1_, f32[128,128]{1,0:T(8,128)} %refs_2_, f32[128,512]{1,0:T(8,128)} %refs_3_, f32[128,128]{1,0:T(8,128)} %refs_4_, f32[128,128]{1,0:T(8,128)} %refs_5_), custom_call_target="tpu_custom_call" | custom-call | flops 1000 | tf_op jit(solution)/shard_map/weights/pallas_call | solution.py:299
  12.6 0.2 %collective-permute-done.4 = bf16[112,128]{1,0:T(8,128)(2,1)S(1)} collective-permute-done((bf16[112,128]{1,0:T(8,128)(2,1)S(1)}, bf16[112,128]{1,0:T(8,128)(2,1)S(1)}, u32[]{:S(2)}, u32[]{:S(2)}) %collective-permute-start.4) | collective-permute-done | bytes 28704 | tf_op jit(solution)/shard_map/ppermute | solution.py:291
  12.8 1.2 %collective-permute-done.5 = bf16[3,112,128]{2,1,0:T(8,128)(2,1)S(1)} collective-permute-done((bf16[3,112,128]{2,1,0:T(8,128)(2,1)S(1)}, bf16[3,112,128]{2,1,0:T(8,128)(2,1)S(1)}, u32[]{:S(2)}, u32[]{:S(2)}) %collective-permute-start.5) | collective-permute-done | bytes 86048 | tf_op jit(solution)/shard_map/ppermute | solution.py:281
  14.0 0.1 collective-permute-start.6
  14.0 0.0 collective-permute-done.3.tiles.part1
  14.1 0.7 %second.1 = (f32[800,128]{1,0:T(8,128)S(1)}, f32[400,128]{1,0:T(8,128)S(1)}, f32[400,128]{1,0:T(8,128)S(1)}, f32[400,128]{1,0:T(8,128)S(1)}) custom-call(bf16[4,112,128]{2,1,0:T(8,128)(2,1)S(1)} %collective-permute-done.3.tiles.part1, bf16[4,112,128]{2,1,0:T(8,128)(2,1)S(1)} %pad_maximum_fusion.tiles.own_tiles.part0, ...), custom_call_target="tpu_custom_call" | custom-call | flops 1024 | tf_op jit(solution)/shard_map/second/pallas_call | solution.py:299
  14.8 0.6 %third.1.before_ref = f32[800,128]{1,0:T(8,128)S(1)} custom-call(bf16[4,112,128]{2,1,0:T(8,128)(2,1)S(1)} %pad_maximum_fusion.1.tiles.part2, bf16[128,1536]{1,0:T(8,128)(2,1)S(1)} %weights.1.weights_ref, f32[800,128]{1,0:T(8,128)S(1)} %get-tuple-element.39.before_ref), custom_call_target="tpu_custom_call" | custom-call | flops 1024 | tf_op jit(solution)/shard_map/third/pallas_call | solution.py:299
  15.4 0.0 collective-permute-done.6.part3
  15.4 2.3 %last.1 = f32[10,10,128]{2,1,0:T(8,128)} custom-call(bf16[4,112,128]{2,1,0:T(8,128)(2,1)S(1)} %pad_maximum_fusion.tiles.own_tiles.part0, bf16[4,112,128]{2,1,0:T(8,128)(2,1)S(1)} %collective-permute-done.3.tiles.part1, bf16[4,112,128]{2,1,0:T(8,128)(2,1)S(1)} %pad_maximum_fusion.1.tiles.part2, bf16[4,112,128]{2,1,0:T(8,128)(2,1)S(1)} %collective-permute-done.6.part3, ...), custom_call_target="tpu_custom_call" | custom-call | flops 1024 | tf_op jit(solution)/shard_map/last/pallas_call | solution.py:299
  (3 shorter events, 0.0 us)
Async XLA Ops:
  0.0 10.8 %copy-start = (f32[128,512]{1,0:T(8,128)S(1)}, f32[128,512]{1,0:T(8,128)}, u32[]{:S(2)}) copy-start(f32[128,512]{1,0:T(8,128)} %refs_0_) | copy-start | bytes 786436
  1.0 8.4 %collective-permute-start = (bf16[112,128]{1,0:T(8,128)(2,1)S(1)}, bf16[112,128]{1,0:T(8,128)(2,1)S(1)}, u32[]{:S(2)}, u32[]{:S(2)}) collective-permute-start(bf16[112,128]{1,0:T(8,128)(2,1)S(1)} %get-tuple-element.25), channel_id=1, source_target_pairs={{0,4},{1,5},{2,6},{3,7},{4,8},{5,9},{6,10},{7,11},{8,12},{9,13},{1... | collective-permute-start | bytes 86024 | tf_op jit(solution)/shard_map/ppermute | solution.py:291
  4.1 5.3 %collective-permute-start.1 = (bf16[112,128]{1,0:T(8,128)(2,1)S(1)}, bf16[112,128]{1,0:T(8,128)(2,1)S(1)}, u32[]{:S(2)}, u32[]{:S(2)}) collective-permute-start(bf16[112,128]{1,0:T(8,128)(2,1)S(1)} %get-tuple-element.25), channel_id=1, source_target_pairs={{0,8},{1,9},{2,10},{3,11},{4,12},{5,13},{6,14},{7,15},{8,0},{9,1},... | collective-permute-start | bytes 86024 | tf_op jit(solution)/shard_map/ppermute | solution.py:291
  6.7 4.1 %collective-permute-start.2 = (bf16[112,128]{1,0:T(8,128)(2,1)S(1)}, bf16[112,128]{1,0:T(8,128)(2,1)S(1)}, u32[]{:S(2)}, u32[]{:S(2)}) collective-permute-start(bf16[112,128]{1,0:T(8,128)(2,1)S(1)} %get-tuple-element.25), channel_id=1, source_target_pairs={{0,12},{1,13},{2,14},{3,15},{4,0},{5,1},{6,2},{7,3},{8,4},{9,5},{1... | collective-permute-start | bytes 86024 | tf_op jit(solution)/shard_map/ppermute | solution.py:291
  8.0 4.8 %collective-permute-start.4 = (bf16[112,128]{1,0:T(8,128)(2,1)S(1)}, bf16[112,128]{1,0:T(8,128)(2,1)S(1)}, u32[]{:S(2)}, u32[]{:S(2)}) collective-permute-start(bf16[112,128]{1,0:T(8,128)(2,1)S(1)} %get-tuple-element.25), channel_id=1, source_target_pairs={{0,14},{1,15},{2,12},{3,13},{4,2},{5,3},{6,0},{7,1},{8,6},{9,7},{1... | collective-permute-start | bytes 86024 | tf_op jit(solution)/shard_map/ppermute | solution.py:291
  9.4 4.6 %collective-permute-start.5 = (bf16[3,112,128]{2,1,0:T(8,128)(2,1)S(1)}, bf16[3,112,128]{2,1,0:T(8,128)(2,1)S(1)}, u32[]{:S(2)}, u32[]{:S(2)}) collective-permute-start(bf16[3,112,128]{2,1,0:T(8,128)(2,1)S(1)} %pad_maximum_fusion.2), channel_id=1, source_target_pairs={{0,2},{1,3},{2,0},{3,1},{4,6},{5,7},{6,4},{7,5},{8,10},{9,11},{10,... | collective-permute-start | bytes 258056 | tf_op jit(solution)/shard_map/ppermute | solution.py:281
  10.7 3.3 %collective-permute-start.3 = (bf16[4,112,128]{2,1,0:T(8,128)(2,1)S(1)}, bf16[4,112,128]{2,1,0:T(8,128)(2,1)S(1)}, u32[]{:S(2)}, u32[]{:S(2)}) collective-permute-start(bf16[4,112,128]{2,1,0:T(8,128)(2,1)S(1)} %pad_maximum_fusion.tiles.own_tiles.part0), channel_id=1, source_target_pairs={{0,1},{1,0},{2,3},{3,2},{4,5},{5,4},{6,7},{7,6},{8,9},{9,8},{10,11... | collective-permute-start | bytes 344072 | tf_op jit(solution)/shard_map/ppermute | solution.py:281
  14.0 1.4 %collective-permute-start.6 = (bf16[4,112,128]{2,1,0:T(8,128)(2,1)S(1)}, bf16[4,112,128]{2,1,0:T(8,128)(2,1)S(1)}, u32[]{:S(2)}, u32[]{:S(2)}) collective-permute-start(bf16[4,112,128]{2,1,0:T(8,128)(2,1)S(1)} %pad_maximum_fusion.1.tiles.part2), channel_id=1, source_target_pairs={{0,1},{1,0},{2,3},{3,2},{4,5},{5,4},{6,7},{7,6},{8,9},{9,8},{10,11... | collective-permute-start | bytes 344072 | tf_op jit(solution)/shard_map/ppermute | solution.py:281

commit v6 on v5

--- a/solution.py
+++ b/solution.py
@@ -73,21 +73,23 @@
 
 
 def halved(weight):
-    return (0.5 * weight).astype(jnp.bfloat16)
-
-
-def dot(value, weight):
-    return jnp.dot(value.astype(jnp.bfloat16), weight, preferred_element_type=jnp.float32)
-
-
-def layer_norm_once(value):
-    mean = jnp.mean(value, axis=-1, keepdims=True)
-    variance = jnp.maximum(jnp.mean(value * value, axis=-1, keepdims=True) - mean * mean, 0.0)
-    return (value - mean) * lax.rsqrt(variance + 1e-05)
-
-
-def scaled(centred):
-    return centred * lax.rsqrt(jnp.mean(centred * centred, axis=-1, keepdims=True) + 1e-05)
+    half = 0.5 * weight
+    high = half.astype(jnp.bfloat16)
+    low = (half - high.astype(jnp.float32)).astype(jnp.bfloat16)
+    return jnp.concatenate([high, low], axis=0)
+
+
+def dot(value, terms):
+    value = value.astype(jnp.bfloat16)
+    return jnp.dot(jnp.concatenate([value, value], axis=1), terms, preferred_element_type=jnp.float32)
+
+
+def centre(value):
+    return value - jnp.mean(value, axis=-1, keepdims=True)
+
+
+def scale_of(centred):
+    return lax.rsqrt(jnp.mean(centred * centred, axis=-1, keepdims=True) + 1e-05)
 
 
 def rest_rows(k):
@@ -149,10 +151,11 @@
     to_lines(right_lines_ref, 0, tiles[0].astype(jnp.float32), 0, 2, RIGHT_LINE)
     to_lines(right_lines_ref, 0, tiles[other].astype(jnp.float32), 1, 2, RIGHT_LINE)
     raw = jnp.concatenate([lines_ref[...], right_lines_ref[...]], axis=0)
-    normed = scaled(split_lines(raw)[0])
-    proj = dot(normed[:LENGTH], proj_weight[:, :256])
+    centred = split_lines(raw)[0]
+    scale = scale_of(centred)
+    proj = dot(centred[:LENGTH], proj_weight[:, :256]) * scale[:LENGTH]
     left_ref[...] = gated(proj[:, :128], proj[:, 128:])
-    proj = dot(normed[LENGTH:], proj_weight[:, 256:])
+    proj = dot(centred[LENGTH:], proj_weight[:, 256:]) * scale[LENGTH:]
     right_ref[...] = gated(proj[:, :128], proj[:, 128:])
 
     for g in range(2 * SIDE // GROUP):
@@ -204,14 +207,15 @@
     own = own_ref[...]
     own = own - jnp.mean(own, axis=-1, keepdims=True)
     to_lines(centred_ref, 0, own, 0, SPLIT, WIDTH)
-    half_gate_ref[...] = dot(scaled(centred_ref[...]), weights_ref[:, pl.ds(OUT_GATE, 128)])
+    centred = centred_ref[...]
+    half_gate_ref[...] = dot(centred, weights_ref[:, pl.ds(OUT_GATE, 128)]) * scale_of(centred)
 
 
 def last_kernel(
     part0, part1, part2, part3, before_ref, centred0_ref, half_gate0_ref, valid0_ref, own_ref,
     weights_ref,
     result_ref,
-    lines_ref, right_lines_ref, left_ref, right_ref, outer_ref, block_ref, left2_ref, right2_ref, mid_ref, normed_ref,
+    lines_ref, right_lines_ref, left_ref, right_ref, outer_ref, block_ref, left2_ref, right2_ref, change_ref, normed_ref,
     pieces_ref, flat_ref, flat2_ref,
 ):
     for number, tiles in enumerate((part0, part1, part2, part3)):
@@ -232,17 +236,18 @@
         ]
 
     centred1, valid1 = split_lines(block_ref[...])
-    half_gate1 = dot(scaled(centred1), weights_ref[:, pl.ds(OUT_GATE, 128)])
+    half_gate1 = dot(centred1, weights_ref[:, pl.ds(OUT_GATE, 128)]) * scale_of(centred1)
     half_gate = jnp.concatenate([half_gate0_ref[...], half_gate1], axis=0)
     centred = jnp.concatenate([centred0_ref[...], centred1], axis=0)
-    normed = layer_norm(jnp.concatenate(sums_of(1) + sums_of(0), axis=0))
-    change = gated(half_gate, dot(normed, weights_ref[:, pl.ds(OUT_FINAL, 128)]))
-    normed = layer_norm(centred + change)
-    mid_ref[...] = change[:LENGTH]
-    normed_ref[...] = normed[:LENGTH]
-    proj = dot(normed[:LENGTH], weights_ref[:, pl.ds(IN_PROJ + 256, 256)])
+    sums = centre(jnp.concatenate(sums_of(1) + sums_of(0), axis=0))
+    change = gated(half_gate, dot(sums, weights_ref[:, pl.ds(OUT_FINAL, 128)]) * scale_of(sums))
+    mid = centre(centred + change)
+    scale = scale_of(mid)
+    change_ref[...] = change[:LENGTH]
+    normed_ref[...] = mid[:LENGTH] * scale[:LENGTH]
+    proj = dot(mid[:LENGTH], weights_ref[:, pl.ds(IN_PROJ + 256, 256)]) * scale[:LENGTH]
     right2_ref[...] = valid0_ref[...] * gated(proj[:, :128], proj[:, 128:])
-    proj = dot(normed[LENGTH:], weights_ref[:, pl.ds(IN_PROJ, 256)])
+    proj = dot(mid[LENGTH:], weights_ref[:, pl.ds(IN_PROJ, 256)]) * scale[LENGTH:]
     left2_ref[...] = jnp.where(valid1, gated(proj[:, :128], proj[:, 128:]), 0.0)
 
     for j in range(SIDE):
@@ -265,9 +270,10 @@
             flat_ref[pl.ds(rest_rows(e), SIDE), :] = source_ref[pl.ds(MAIN * SPLIT + e, SIDE, stride=WIDTH), :]
         return flat_ref[...]
 
-    mid = own_ref[...] + own_rows(mid_ref, flat_ref)
+    mid = own_ref[...] + own_rows(change_ref, flat_ref)
     half_gate = dot(own_rows(normed_ref, flat2_ref), weights_ref[:, pl.ds(IN_GATE, 128)])
-    result = mid + gated(half_gate, dot(layer_norm_once(inner), weights_ref[:, pl.ds(IN_FINAL, 128)]))
+    inner = centre(inner)
+    result = mid + gated(half_gate, dot(inner, weights_ref[:, pl.ds(IN_FINAL, 128)]) * scale_of(inner))
     for k in range(SIDE):
         result_ref[pl.ds(0, MAIN), k, :] = result[MAIN * k : MAIN * (k + 1)]
         for e in range(REST):
@@ -327,7 +333,7 @@
     outer = call(first_kernel, "first", cost, sums, work, in_vmem(part0), in_vmem(weights[0]))
     outer, *weights = lax.optimization_barrier((outer, *weights))
     weights = call(
-        weights_kernel, "weights", 1000, pltpu.VMEM((128, WEIGHTS), jnp.bfloat16), [], *weights, grant=None
+        weights_kernel, "weights", 1000, pltpu.VMEM((2 * 128, WEIGHTS), jnp.bfloat16), [], *weights, grant=None
     )
     aslant, swapped_early, outer, weights = lax.optimization_barrier((aslant, swapped_early, outer, weights))
     part2 = jnp.concatenate([swapped_early, aslant[None]])

time: 17.9 us -> 17.8 us (level)
  no operation moved by 1% of the time
where the time goes in v6:
time: 17.8 us; the launch traced here: 17.6 us
  starting transfers between devices  9.84 us (55%)
  Pallas kernels  6.26 us (35%)
  waiting for transfers between devices  1.34 us (8%)
    ppermute x4, starting transfers between devices, shifted(): return lax.ppermute(value, ('row', 'col'), pairs)  8.39 us
    pallas_call x6, Pallas kernels, call(): pl.pallas_call(kernel, out_shape=out, scratch_shapes=[pltpu.VMEM(one, jnp...  6.26 us
    ppermute x3, starting transfers between devices, swapped(): return lax.ppermute(value, ('row', 'col'), pairs)  1.45 us
    ppermute x3, waiting for transfers between devices, swapped(): return lax.ppermute(value, ('row', 'col'), pairs)  1.22 us
  transfers between devices with their start and end apart: 7, of which 2 were waited for; matrix products, arithmetic and copies ran while one was open for 0% of the time, Pallas kernels for 17%

profile of v6, /device:TPU:0, one launch (start us, length us, event | category | flops | bytes accessed | tf_op | source)
XLA Modules:
  0.0 17.6 jit_solution(18117033877637769816)
XLA Ops:
  0.0 0.0 copy-start
  0.0 1.0 %pack.1 = (bf16[112,128]{1,0:T(8,128)(2,1)S(1)}, f32[112,128]{1,0:T(8,128)S(1)}) custom-call(f32[10,10,128]{2,1,0:T(8,128)} %pair_ref.1, s32[10,10]{1,0:T(8,128)} %mask_ref.1), custom_call_target="tpu_custom_call" | custom-call | flops 1000 | tf_op jit(solution)/shard_map/pack/pallas_call | solution.py:305
  1.0 3.1 %collective-permute-start = (bf16[112,128]{1,0:T(8,128)(2,1)S(1)}, bf16[112,128]{1,0:T(8,128)(2,1)S(1)}, u32[]{:S(2)}, u32[]{:S(2)}) collective-permute-start(bf16[112,128]{1,0:T(8,128)(2,1)S(1)} %get-tuple-element.25), channel_id=1, source_target_pairs={{0,4},{1,5},{2,6},{3,7},{4,8},{5,9},{6,10},{7,11},{8,12},{9,13},{1... | collective-permute-start | bytes 86024 | tf_op jit(solution)/shard_map/ppermute | solution.py:297
  4.1 2.6 %collective-permute-start.1 = (bf16[112,128]{1,0:T(8,128)(2,1)S(1)}, bf16[112,128]{1,0:T(8,128)(2,1)S(1)}, u32[]{:S(2)}, u32[]{:S(2)}) collective-permute-start(bf16[112,128]{1,0:T(8,128)(2,1)S(1)} %get-tuple-element.25), channel_id=1, source_target_pairs={{0,8},{1,9},{2,10},{3,11},{4,12},{5,13},{6,14},{7,15},{8,0},{9,1},... | collective-permute-start | bytes 86024 | tf_op jit(solution)/shard_map/ppermute | solution.py:297
  6.7 1.3 %collective-permute-start.2 = (bf16[112,128]{1,0:T(8,128)(2,1)S(1)}, bf16[112,128]{1,0:T(8,128)(2,1)S(1)}, u32[]{:S(2)}, u32[]{:S(2)}) collective-permute-start(bf16[112,128]{1,0:T(8,128)(2,1)S(1)} %get-tuple-element.25), channel_id=1, source_target_pairs={{0,12},{1,13},{2,14},{3,15},{4,0},{5,1},{6,2},{7,3},{8,4},{9,5},{1... | collective-permute-start | bytes 86024 | tf_op jit(solution)/shard_map/ppermute | solution.py:297
  8.0 1.4 %collective-permute-start.4 = (bf16[112,128]{1,0:T(8,128)(2,1)S(1)}, bf16[112,128]{1,0:T(8,128)(2,1)S(1)}, u32[]{:S(2)}, u32[]{:S(2)}) collective-permute-start(bf16[112,128]{1,0:T(8,128)(2,1)S(1)} %get-tuple-element.25), channel_id=1, source_target_pairs={{0,14},{1,15},{2,12},{3,13},{4,2},{5,3},{6,0},{7,1},{8,6},{9,7},{1... | collective-permute-start | bytes 86024 | tf_op jit(solution)/shard_map/ppermute | solution.py:297
  9.4 0.0 collective-permute-done
  9.4 0.0 collective-permute-done.1
  9.4 1.3 %collective-permute-start.5 = (bf16[3,112,128]{2,1,0:T(8,128)(2,1)S(1)}, bf16[3,112,128]{2,1,0:T(8,128)(2,1)S(1)}, u32[]{:S(2)}, u32[]{:S(2)}) collective-permute-start(bf16[3,112,128]{2,1,0:T(8,128)(2,1)S(1)} %pad_maximum_fusion.2), channel_id=1, source_target_pairs={{0,2},{1,3},{2,0},{3,1},{4,6},{5,7},{6,4},{7,5},{8,10},{9,11},{10,... | collective-permute-start | bytes 258056 | tf_op jit(solution)/shard_map/ppermute | solution.py:287
  10.7 0.0 collective-permute-done.2
  10.7 0.1 collective-permute-start.3
  10.8 0.0 copy-done
  10.8 0.6 %first.1.before_ref = f32[800,128]{1,0:T(8,128)S(1)} custom-call(bf16[4,112,128]{2,1,0:T(8,128)(2,1)S(1)} %pad_maximum_fusion.tiles.own_tiles.part0, f32[128,512]{1,0:T(8,128)S(1)} %copy-done), custom_call_target="tpu_custom_call" | custom-call | flops 1024 | tf_op jit(solution)/shard_map/first/pallas_call | solution.py:305
  11.4 1.2 %weights.1.weights_ref = bf16[256,1536]{1,0:T(8,128)(2,1)S(1)} custom-call(f32[128,512]{1,0:T(8,128)} %refs_0_, f32[128,128]{1,0:T(8,128)} %refs_1_, f32[128,128]{1,0:T(8,128)} %refs_2_, f32[128,512]{1,0:T(8,128)} %refs_3_, f32[128,128]{1,0:T(8,128)} %refs_4_, f32[128,128]{1,0:T(8,128)} %refs_5_), custom_call_target="tpu_custom_call" | custom-call | flops 1000 | tf_op jit(solution)/shard_map/weights/pallas_call | solution.py:305
  12.7 0.1 collective-permute-done.4
  12.8 1.2 %collective-permute-done.5 = bf16[3,112,128]{2,1,0:T(8,128)(2,1)S(1)} collective-permute-done((bf16[3,112,128]{2,1,0:T(8,128)(2,1)S(1)}, bf16[3,112,128]{2,1,0:T(8,128)(2,1)S(1)}, u32[]{:S(2)}, u32[]{:S(2)}) %collective-permute-start.5) | collective-permute-done | bytes 86048 | tf_op jit(solution)/shard_map/ppermute | solution.py:287
  14.0 0.1 collective-permute-start.6
  14.0 0.0 collective-permute-done.3.tiles.part1
  14.1 0.7 %second.1 = (f32[800,128]{1,0:T(8,128)S(1)}, f32[400,128]{1,0:T(8,128)S(1)}, f32[400,128]{1,0:T(8,128)S(1)}, f32[400,128]{1,0:T(8,128)S(1)}) custom-call(bf16[4,112,128]{2,1,0:T(8,128)(2,1)S(1)} %collective-permute-done.3.tiles.part1, bf16[4,112,128]{2,1,0:T(8,128)(2,1)S(1)} %pad_maximum_fusion.tiles.own_tiles.part0, ...), custom_call_target="tpu_custom_call" | custom-call | flops 1024 | tf_op jit(solution)/shard_map/second/pallas_call | solution.py:305
  14.7 0.6 %third.1.before_ref = f32[800,128]{1,0:T(8,128)S(1)} custom-call(bf16[4,112,128]{2,1,0:T(8,128)(2,1)S(1)} %pad_maximum_fusion.1.tiles.part2, bf16[256,1536]{1,0:T(8,128)(2,1)S(1)} %weights.1.weights_ref, f32[800,128]{1,0:T(8,128)S(1)} %get-tuple-element.39.before_ref), custom_call_target="tpu_custom_call" | custom-call | flops 1024 | tf_op jit(solution)/shard_map/third/pallas_call | solution.py:305
  15.3 0.0 collective-permute-done.6.part3
  15.4 2.2 %last.1 = f32[10,10,128]{2,1,0:T(8,128)} custom-call(bf16[4,112,128]{2,1,0:T(8,128)(2,1)S(1)} %pad_maximum_fusion.tiles.own_tiles.part0, bf16[4,112,128]{2,1,0:T(8,128)(2,1)S(1)} %collective-permute-done.3.tiles.part1, bf16[4,112,128]{2,1,0:T(8,128)(2,1)S(1)} %pad_maximum_fusion.1.tiles.part2, bf16[4,112,128]{2,1,0:T(8,128)(2,1)S(1)} %collective-permute-done.6.part3, ...), custom_call_target="tpu_custom_call" | custom-call | flops 1024 | tf_op jit(solution)/shard_map/last/pallas_call | solution.py:305
  (3 shorter events, 0.0 us)
Async XLA Ops:
  0.0 10.8 %copy-start = (f32[128,512]{1,0:T(8,128)S(1)}, f32[128,512]{1,0:T(8,128)}, u32[]{:S(2)}) copy-start(f32[128,512]{1,0:T(8,128)} %refs_0_) | copy-start | bytes 786436
  1.0 8.4 %collective-permute-start = (bf16[112,128]{1,0:T(8,128)(2,1)S(1)}, bf16[112,128]{1,0:T(8,128)(2,1)S(1)}, u32[]{:S(2)}, u32[]{:S(2)}) collective-permute-start(bf16[112,128]{1,0:T(8,128)(2,1)S(1)} %get-tuple-element.25), channel_id=1, source_target_pairs={{0,4},{1,5},{2,6},{3,7},{4,8},{5,9},{6,10},{7,11},{8,12},{9,13},{1... | collective-permute-start | bytes 86024 | tf_op jit(solution)/shard_map/ppermute | solution.py:297
  4.1 5.3 %collective-permute-start.1 = (bf16[112,128]{1,0:T(8,128)(2,1)S(1)}, bf16[112,128]{1,0:T(8,128)(2,1)S(1)}, u32[]{:S(2)}, u32[]{:S(2)}) collective-permute-start(bf16[112,128]{1,0:T(8,128)(2,1)S(1)} %get-tuple-element.25), channel_id=1, source_target_pairs={{0,8},{1,9},{2,10},{3,11},{4,12},{5,13},{6,14},{7,15},{8,0},{9,1},... | collective-permute-start | bytes 86024 | tf_op jit(solution)/shard_map/ppermute | solution.py:297
  6.7 4.1 %collective-permute-start.2 = (bf16[112,128]{1,0:T(8,128)(2,1)S(1)}, bf16[112,128]{1,0:T(8,128)(2,1)S(1)}, u32[]{:S(2)}, u32[]{:S(2)}) collective-permute-start(bf16[112,128]{1,0:T(8,128)(2,1)S(1)} %get-tuple-element.25), channel_id=1, source_target_pairs={{0,12},{1,13},{2,14},{3,15},{4,0},{5,1},{6,2},{7,3},{8,4},{9,5},{1... | collective-permute-start | bytes 86024 | tf_op jit(solution)/shard_map/ppermute | solution.py:297
  8.0 4.8 %collective-permute-start.4 = (bf16[112,128]{1,0:T(8,128)(2,1)S(1)}, bf16[112,128]{1,0:T(8,128)(2,1)S(1)}, u32[]{:S(2)}, u32[]{:S(2)}) collective-permute-start(bf16[112,128]{1,0:T(8,128)(2,1)S(1)} %get-tuple-element.25), channel_id=1, source_target_pairs={{0,14},{1,15},{2,12},{3,13},{4,2},{5,3},{6,0},{7,1},{8,6},{9,7},{1... | collective-permute-start | bytes 86024 | tf_op jit(solution)/shard_map/ppermute | solution.py:297
  9.4 4.6 %collective-permute-start.5 = (bf16[3,112,128]{2,1,0:T(8,128)(2,1)S(1)}, bf16[3,112,128]{2,1,0:T(8,128)(2,1)S(1)}, u32[]{:S(2)}, u32[]{:S(2)}) collective-permute-start(bf16[3,112,128]{2,1,0:T(8,128)(2,1)S(1)} %pad_maximum_fusion.2), channel_id=1, source_target_pairs={{0,2},{1,3},{2,0},{3,1},{4,6},{5,7},{6,4},{7,5},{8,10},{9,11},{10,... | collective-permute-start | bytes 258056 | tf_op jit(solution)/shard_map/ppermute | solution.py:287
  10.7 3.3 %collective-permute-start.3 = (bf16[4,112,128]{2,1,0:T(8,128)(2,1)S(1)}, bf16[4,112,128]{2,1,0:T(8,128)(2,1)S(1)}, u32[]{:S(2)}, u32[]{:S(2)}) collective-permute-start(bf16[4,112,128]{2,1,0:T(8,128)(2,1)S(1)} %pad_maximum_fusion.tiles.own_tiles.part0), channel_id=1, source_target_pairs={{0,1},{1,0},{2,3},{3,2},{4,5},{5,4},{6,7},{7,6},{8,9},{9,8},{10,11... | collective-permute-start | bytes 344072 | tf_op jit(solution)/shard_map/ppermute | solution.py:287
  14.0 1.4 %collective-permute-start.6 = (bf16[4,112,128]{2,1,0:T(8,128)(2,1)S(1)}, bf16[4,112,128]{2,1,0:T(8,128)(2,1)S(1)}, u32[]{:S(2)}, u32[]{:S(2)}) collective-permute-start(bf16[4,112,128]{2,1,0:T(8,128)(2,1)S(1)} %pad_maximum_fusion.1.tiles.part2), channel_id=1, source_target_pairs={{0,1},{1,0},{2,3},{3,2},{4,5},{5,4},{6,7},{7,6},{8,9},{9,8},{10,11... | collective-permute-start | bytes 344072 | tf_op jit(solution)/shard_map/ppermute | solution.py:287

commit v7 on v6

--- a/solution.py
+++ b/solution.py
@@ -218,7 +218,7 @@
     lines_ref, right_lines_ref, left_ref, right_ref, outer_ref, block_ref, left2_ref, right2_ref, change_ref, normed_ref,
     pieces_ref, flat_ref, flat2_ref,
 ):
-    for number, tiles in enumerate((part0, part1, part2, part3)):
+    for number, tiles in enumerate((part0, part1, part3, part2)):
         @pl.when(other_part() == number)
         def _():
             for slot in range(SPLIT):
@@ -321,9 +321,9 @@
         pair, pair_mask, grant=None, in_specs=2 * [pl.BlockSpec(memory_space=pl.ANY)],
     )
     around = [tile] + [shifted(tile, step) for step in STEPS]
-    aslant = shifted(tile, STEPS[2], 2)
+    aslant = shifted(tile, STEPS[2], 3)
     early = jnp.stack(around[:3])
-    swapped_early = swapped(early, 0, 2)
+    swapped_early = swapped(early, 0, 3)
     late, _ = lax.optimization_barrier((around[3], early))
     part0 = jnp.concatenate([early, late[None]])
     lines = pltpu.VMEM((LENGTH, 128), f32)

time: 17.8 us -> 17.7 us (level)
  starting transfers between devices: 9.84 us -> 8.31 us
  waiting for transfers between devices: 1.34 us -> 2.77 us
    ppermute x4, waiting for transfers between devices: 0.12 us -> 1.93 us  [shifted(): return lax.ppermute(value, ('row', 'col'), pairs)]
    ppermute x4, starting transfers between devices: 8.39 us -> 7.02 us  [shifted(): return lax.ppermute(value, ('row', 'col'), pairs)]
    ppermute x3, waiting for transfers between devices: 1.22 us -> 0.84 us  [swapped(): return lax.ppermute(value, ('row', 'col'), pairs)]
  transfers between devices with their start and end apart: 7 -> 7, of which waited for: 2 -> 3; matrix products, arithmetic and copies ran while one was open for 0% -> 0% of each run, Pallas kernels for 17% -> 18%
where the time goes in v7:
time: 17.7 us; the launch traced here: 17.5 us
  starting transfers between devices  8.31 us (47%)
  Pallas kernels  6.28 us (35%)
  waiting for transfers between devices  2.77 us (16%)
    ppermute x4, starting transfers between devices, shifted(): return lax.ppermute(value, ('row', 'col'), pairs)  7.02 us
    pallas_call x6, Pallas kernels, call(): pl.pallas_call(kernel, out_shape=out, scratch_shapes=[pltpu.VMEM(one, jnp...  6.28 us
    ppermute x4, waiting for transfers between devices, shifted(): return lax.ppermute(value, ('row', 'col'), pairs)  1.93 us
    ppermute x3, starting transfers between devices, swapped(): return lax.ppermute(value, ('row', 'col'), pairs)  1.29 us
    ppermute x3, waiting for transfers between devices, swapped(): return lax.ppermute(value, ('row', 'col'), pairs)  0.84 us
  transfers between devices with their start and end apart: 7, of which 3 were waited for; matrix products, arithmetic and copies ran while one was open for 0% of the time, Pallas kernels for 18%

profile of v7, /device:TPU:0, one launch (start us, length us, event | category | flops | bytes accessed | tf_op | source)
XLA Modules:
  0.0 17.5 jit_solution(2067486426327540921)
XLA Ops:
  0.0 0.0 copy-start
  0.0 1.0 %pack.1 = (bf16[112,128]{1,0:T(8,128)(2,1)S(1)}, f32[112,128]{1,0:T(8,128)S(1)}) custom-call(f32[10,10,128]{2,1,0:T(8,128)} %pair_ref.1, s32[10,10]{1,0:T(8,128)} %mask_ref.1), custom_call_target="tpu_custom_call" | custom-call | flops 1000 | tf_op jit(solution)/shard_map/pack/pallas_call | solution.py:305
  1.0 3.1 %collective-permute-start = (bf16[112,128]{1,0:T(8,128)(2,1)S(1)}, bf16[112,128]{1,0:T(8,128)(2,1)S(1)}, u32[]{:S(2)}, u32[]{:S(2)}) collective-permute-start(bf16[112,128]{1,0:T(8,128)(2,1)S(1)} %get-tuple-element.25), channel_id=1, source_target_pairs={{0,4},{1,5},{2,6},{3,7},{4,8},{5,9},{6,10},{7,11},{8,12},{9,13},{1... | collective-permute-start | bytes 86024 | tf_op jit(solution)/shard_map/ppermute | solution.py:297
  4.1 2.6 %collective-permute-start.1 = (bf16[112,128]{1,0:T(8,128)(2,1)S(1)}, bf16[112,128]{1,0:T(8,128)(2,1)S(1)}, u32[]{:S(2)}, u32[]{:S(2)}) collective-permute-start(bf16[112,128]{1,0:T(8,128)(2,1)S(1)} %get-tuple-element.25), channel_id=1, source_target_pairs={{0,8},{1,9},{2,10},{3,11},{4,12},{5,13},{6,14},{7,15},{8,0},{9,1},... | collective-permute-start | bytes 86024 | tf_op jit(solution)/shard_map/ppermute | solution.py:297
  6.7 1.3 %collective-permute-start.2 = (bf16[112,128]{1,0:T(8,128)(2,1)S(1)}, bf16[112,128]{1,0:T(8,128)(2,1)S(1)}, u32[]{:S(2)}, u32[]{:S(2)}) collective-permute-start(bf16[112,128]{1,0:T(8,128)(2,1)S(1)} %get-tuple-element.25), channel_id=1, source_target_pairs={{0,12},{1,13},{2,14},{3,15},{4,0},{5,1},{6,2},{7,3},{8,4},{9,5},{1... | collective-permute-start | bytes 86024 | tf_op jit(solution)/shard_map/ppermute | solution.py:297
  8.0 0.0 collective-permute-start.4
  8.0 0.0 collective-permute-done
  8.0 1.1 %collective-permute-done.1 = bf16[112,128]{1,0:T(8,128)(2,1)S(1)} collective-permute-done((bf16[112,128]{1,0:T(8,128)(2,1)S(1)}, bf16[112,128]{1,0:T(8,128)(2,1)S(1)}, u32[]{:S(2)}, u32[]{:S(2)}) %collective-permute-start.1) | collective-permute-done | bytes 28704 | tf_op jit(solution)/shard_map/ppermute | solution.py:297
  9.2 0.6 %collective-permute-start.5 = (bf16[3,112,128]{2,1,0:T(8,128)(2,1)S(1)}, bf16[3,112,128]{2,1,0:T(8,128)(2,1)S(1)}, u32[]{:S(2)}, u32[]{:S(2)}) collective-permute-start(bf16[3,112,128]{2,1,0:T(8,128)(2,1)S(1)} %pad_maximum_fusion.2), channel_id=1, source_target_pairs={{0,3},{1,2},{2,1},{3,0},{4,7},{5,6},{6,5},{7,4},{8,11},{9,10},{10,... | collective-permute-start | bytes 258056 | tf_op jit(solution)/shard_map/ppermute | solution.py:287
  9.7 0.8 %collective-permute-done.2 = bf16[112,128]{1,0:T(8,128)(2,1)S(1)} collective-permute-done((bf16[112,128]{1,0:T(8,128)(2,1)S(1)}, bf16[112,128]{1,0:T(8,128)(2,1)S(1)}, u32[]{:S(2)}, u32[]{:S(2)}) %collective-permute-start.2) | collective-permute-done | bytes 28704 | tf_op jit(solution)/shard_map/ppermute | solution.py:297
  10.5 0.4 %collective-permute-start.3 = (bf16[4,112,128]{2,1,0:T(8,128)(2,1)S(1)}, bf16[4,112,128]{2,1,0:T(8,128)(2,1)S(1)}, u32[]{:S(2)}, u32[]{:S(2)}) collective-permute-start(bf16[4,112,128]{2,1,0:T(8,128)(2,1)S(1)} %pad_maximum_fusion.tiles.own_tiles.part0), channel_id=1, source_target_pairs={{0,1},{1,0},{2,3},{3,2},{4,5},{5,4},{6,7},{7,6},{8,9},{9,8},{10,11... | collective-permute-start | bytes 344072 | tf_op jit(solution)/shard_map/ppermute | solution.py:287
  10.9 0.0 copy-done
  10.9 0.6 %first.1.before_ref = f32[800,128]{1,0:T(8,128)S(1)} custom-call(bf16[4,112,128]{2,1,0:T(8,128)(2,1)S(1)} %pad_maximum_fusion.tiles.own_tiles.part0, f32[128,512]{1,0:T(8,128)S(1)} %copy-done), custom_call_target="tpu_custom_call" | custom-call | flops 1024 | tf_op jit(solution)/shard_map/first/pallas_call | solution.py:305
  11.5 1.2 %weights.1.weights_ref = bf16[256,1536]{1,0:T(8,128)(2,1)S(1)} custom-call(f32[128,512]{1,0:T(8,128)} %refs_0_, f32[128,128]{1,0:T(8,128)} %refs_1_, f32[128,128]{1,0:T(8,128)} %refs_2_, f32[128,512]{1,0:T(8,128)} %refs_3_, f32[128,128]{1,0:T(8,128)} %refs_4_, f32[128,128]{1,0:T(8,128)} %refs_5_), custom_call_target="tpu_custom_call" | custom-call | flops 1000 | tf_op jit(solution)/shard_map/weights/pallas_call | solution.py:305
  12.8 0.0 collective-permute-done.4
  12.8 0.8 %collective-permute-done.5 = bf16[3,112,128]{2,1,0:T(8,128)(2,1)S(1)} collective-permute-done((bf16[3,112,128]{2,1,0:T(8,128)(2,1)S(1)}, bf16[3,112,128]{2,1,0:T(8,128)(2,1)S(1)}, u32[]{:S(2)}, u32[]{:S(2)}) %collective-permute-start.5) | collective-permute-done | bytes 86048 | tf_op jit(solution)/shard_map/ppermute | solution.py:287
  13.6 0.4 %collective-permute-start.6 = (bf16[4,112,128]{2,1,0:T(8,128)(2,1)S(1)}, bf16[4,112,128]{2,1,0:T(8,128)(2,1)S(1)}, u32[]{:S(2)}, u32[]{:S(2)}) collective-permute-start(bf16[4,112,128]{2,1,0:T(8,128)(2,1)S(1)} %pad_maximum_fusion.1.tiles.part2), channel_id=1, source_target_pairs={{0,1},{1,0},{2,3},{3,2},{4,5},{5,4},{6,7},{7,6},{8,9},{9,8},{10,11... | collective-permute-start | bytes 344072 | tf_op jit(solution)/shard_map/ppermute | solution.py:287
  14.0 0.0 collective-permute-done.3.tiles.part1
  14.0 0.7 %second.1 = (f32[800,128]{1,0:T(8,128)S(1)}, f32[400,128]{1,0:T(8,128)S(1)}, f32[400,128]{1,0:T(8,128)S(1)}, f32[400,128]{1,0:T(8,128)S(1)}) custom-call(bf16[4,112,128]{2,1,0:T(8,128)(2,1)S(1)} %collective-permute-done.3.tiles.part1, bf16[4,112,128]{2,1,0:T(8,128)(2,1)S(1)} %pad_maximum_fusion.tiles.own_tiles.part0, ...), custom_call_target="tpu_custom_call" | custom-call | flops 1024 | tf_op jit(solution)/shard_map/second/pallas_call | solution.py:305
  14.6 0.6 %third.1.before_ref = f32[800,128]{1,0:T(8,128)S(1)} custom-call(bf16[4,112,128]{2,1,0:T(8,128)(2,1)S(1)} %pad_maximum_fusion.1.tiles.part2, bf16[256,1536]{1,0:T(8,128)(2,1)S(1)} %weights.1.weights_ref, f32[800,128]{1,0:T(8,128)S(1)} %get-tuple-element.39.before_ref), custom_call_target="tpu_custom_call" | custom-call | flops 1024 | tf_op jit(solution)/shard_map/third/pallas_call | solution.py:305
  15.2 0.0 collective-permute-done.6.part3
  15.2 2.2 %last.1 = f32[10,10,128]{2,1,0:T(8,128)} custom-call(bf16[4,112,128]{2,1,0:T(8,128)(2,1)S(1)} %pad_maximum_fusion.tiles.own_tiles.part0, bf16[4,112,128]{2,1,0:T(8,128)(2,1)S(1)} %collective-permute-done.3.tiles.part1, bf16[4,112,128]{2,1,0:T(8,128)(2,1)S(1)} %pad_maximum_fusion.1.tiles.part2, bf16[4,112,128]{2,1,0:T(8,128)(2,1)S(1)} %collective-permute-done.6.part3, ...), custom_call_target="tpu_custom_call" | custom-call | flops 1024 | tf_op jit(solution)/shard_map/last/pallas_call | solution.py:305
  (3 shorter events, 0.0 us)
Async XLA Ops:
  0.0 10.9 %copy-start = (f32[128,512]{1,0:T(8,128)S(1)}, f32[128,512]{1,0:T(8,128)}, u32[]{:S(2)}) copy-start(f32[128,512]{1,0:T(8,128)} %refs_0_) | copy-start | bytes 786436
  1.0 7.0 %collective-permute-start = (bf16[112,128]{1,0:T(8,128)(2,1)S(1)}, bf16[112,128]{1,0:T(8,128)(2,1)S(1)}, u32[]{:S(2)}, u32[]{:S(2)}) collective-permute-start(bf16[112,128]{1,0:T(8,128)(2,1)S(1)} %get-tuple-element.25), channel_id=1, source_target_pairs={{0,4},{1,5},{2,6},{3,7},{4,8},{5,9},{6,10},{7,11},{8,12},{9,13},{1... | collective-permute-start | bytes 86024 | tf_op jit(solution)/shard_map/ppermute | solution.py:297
  4.1 5.1 %collective-permute-start.1 = (bf16[112,128]{1,0:T(8,128)(2,1)S(1)}, bf16[112,128]{1,0:T(8,128)(2,1)S(1)}, u32[]{:S(2)}, u32[]{:S(2)}) collective-permute-start(bf16[112,128]{1,0:T(8,128)(2,1)S(1)} %get-tuple-element.25), channel_id=1, source_target_pairs={{0,8},{1,9},{2,10},{3,11},{4,12},{5,13},{6,14},{7,15},{8,0},{9,1},... | collective-permute-start | bytes 86024 | tf_op jit(solution)/shard_map/ppermute | solution.py:297
  6.7 3.9 %collective-permute-start.2 = (bf16[112,128]{1,0:T(8,128)(2,1)S(1)}, bf16[112,128]{1,0:T(8,128)(2,1)S(1)}, u32[]{:S(2)}, u32[]{:S(2)}) collective-permute-start(bf16[112,128]{1,0:T(8,128)(2,1)S(1)} %get-tuple-element.25), channel_id=1, source_target_pairs={{0,12},{1,13},{2,14},{3,15},{4,0},{5,1},{6,2},{7,3},{8,4},{9,5},{1... | collective-permute-start | bytes 86024 | tf_op jit(solution)/shard_map/ppermute | solution.py:297
  8.0 4.8 %collective-permute-start.4 = (bf16[112,128]{1,0:T(8,128)(2,1)S(1)}, bf16[112,128]{1,0:T(8,128)(2,1)S(1)}, u32[]{:S(2)}, u32[]{:S(2)}) collective-permute-start(bf16[112,128]{1,0:T(8,128)(2,1)S(1)} %get-tuple-element.25), channel_id=1, source_target_pairs={{0,15},{1,14},{2,13},{3,12},{4,3},{5,2},{6,1},{7,0},{8,7},{9,6},{1... | collective-permute-start | bytes 86024 | tf_op jit(solution)/shard_map/ppermute | solution.py:297
  9.2 4.4 %collective-permute-start.5 = (bf16[3,112,128]{2,1,0:T(8,128)(2,1)S(1)}, bf16[3,112,128]{2,1,0:T(8,128)(2,1)S(1)}, u32[]{:S(2)}, u32[]{:S(2)}) collective-permute-start(bf16[3,112,128]{2,1,0:T(8,128)(2,1)S(1)} %pad_maximum_fusion.2), channel_id=1, source_target_pairs={{0,3},{1,2},{2,1},{3,0},{4,7},{5,6},{6,5},{7,4},{8,11},{9,10},{10,... | collective-permute-start | bytes 258056 | tf_op jit(solution)/shard_map/ppermute | solution.py:287
  10.5 3.4 %collective-permute-start.3 = (bf16[4,112,128]{2,1,0:T(8,128)(2,1)S(1)}, bf16[4,112,128]{2,1,0:T(8,128)(2,1)S(1)}, u32[]{:S(2)}, u32[]{:S(2)}) collective-permute-start(bf16[4,112,128]{2,1,0:T(8,128)(2,1)S(1)} %pad_maximum_fusion.tiles.own_tiles.part0), channel_id=1, source_target_pairs={{0,1},{1,0},{2,3},{3,2},{4,5},{5,4},{6,7},{7,6},{8,9},{9,8},{10,11... | collective-permute-start | bytes 344072 | tf_op jit(solution)/shard_map/ppermute | solution.py:287
  13.6 1.6 %collective-permute-start.6 = (bf16[4,112,128]{2,1,0:T(8,128)(2,1)S(1)}, bf16[4,112,128]{2,1,0:T(8,128)(2,1)S(1)}, u32[]{:S(2)}, u32[]{:S(2)}) collective-permute-start(bf16[4,112,128]{2,1,0:T(8,128)(2,1)S(1)} %pad_maximum_fusion.1.tiles.part2), channel_id=1, source_target_pairs={{0,1},{1,0},{2,3},{3,2},{4,5},{5,4},{6,7},{7,6},{8,9},{9,8},{10,11... | collective-permute-start | bytes 344072 | tf_op jit(solution)/shard_map/ppermute | solution.py:287

commit v8 on v7

--- a/solution.py
+++ b/solution.py
@@ -90,6 +90,12 @@
 
 def scale_of(centred):
     return lax.rsqrt(jnp.mean(centred * centred, axis=-1, keepdims=True) + 1e-05)
+
+
+def scale_of_whole(value):
+    mean = jnp.mean(value, axis=-1, keepdims=True)
+    square = jnp.mean(value * value, axis=-1, keepdims=True)
+    return lax.rsqrt(jnp.maximum(square - mean * mean, 0.0) + 1e-05)
 
 
 def rest_rows(k):
@@ -126,8 +132,10 @@
 def weights_kernel(*refs):
     start = 0
     for weight_ref in refs[:-1]:
-        width = weight_ref.shape[1]
-        refs[-1][:, pl.ds(start, width)] = halved(weight_ref[...])
+        weight, width = weight_ref[...], weight_ref.shape[1]
+        if start in (IN_PROJ, IN_GATE):
+            weight = weight - jnp.mean(weight, axis=0, keepdims=True)
+        refs[-1][:, pl.ds(start, width)] = halved(weight)
         start += width
 
 
@@ -241,8 +249,8 @@
     centred = jnp.concatenate([centred0_ref[...], centred1], axis=0)
     sums = centre(jnp.concatenate(sums_of(1) + sums_of(0), axis=0))
     change = gated(half_gate, dot(sums, weights_ref[:, pl.ds(OUT_FINAL, 128)]) * scale_of(sums))
-    mid = centre(centred + change)
-    scale = scale_of(mid)
+    mid = centred + change
+    scale = scale_of_whole(mid)
     change_ref[...] = change[:LENGTH]
     normed_ref[...] = mid[:LENGTH] * scale[:LENGTH]
     proj = dot(mid[:LENGTH], weights_ref[:, pl.ds(IN_PROJ + 256, 256)]) * scale[:LENGTH]

time: 17.7 us -> 17.6 us (level)
  no operation moved by 1% of the time
where the time goes in v8:
time: 17.6 us; the launch traced here: 17.4 us
  starting transfers between devices  8.31 us (47%)
  Pallas kernels  6.22 us (35%)
  waiting for transfers between devices  2.74 us (16%)
    ppermute x4, starting transfers between devices, shifted(): return lax.ppermute(value, ('row', 'col'), pairs)  7.02 us
    pallas_call x6, Pallas kernels, call(): pl.pallas_call(kernel, out_shape=out, scratch_shapes=[pltpu.VMEM(one, jnp...  6.22 us
    ppermute x4, waiting for transfers between devices, shifted(): return lax.ppermute(value, ('row', 'col'), pairs)  1.93 us
    ppermute x3, starting transfers between devices, swapped(): return lax.ppermute(value, ('row', 'col'), pairs)  1.29 us
    ppermute x3, waiting for transfers between devices, swapped(): return lax.ppermute(value, ('row', 'col'), pairs)  0.8 us
  transfers between devices with their start and end apart: 7, of which 3 were waited for; matrix products, arithmetic and copies ran while one was open for 0% of the time, Pallas kernels for 18%

profile of v8, /device:TPU:0, one launch (start us, length us, event | category | flops | bytes accessed | tf_op | source)
XLA Modules:
  0.0 17.4 jit_solution(8230003926066622426)
XLA Ops:
  0.0 0.0 copy-start
  0.0 1.0 %pack.1 = (bf16[112,128]{1,0:T(8,128)(2,1)S(1)}, f32[112,128]{1,0:T(8,128)S(1)}) custom-call(f32[10,10,128]{2,1,0:T(8,128)} %pair_ref.1, s32[10,10]{1,0:T(8,128)} %mask_ref.1), custom_call_target="tpu_custom_call" | custom-call | flops 1000 | tf_op jit(solution)/shard_map/pack/pallas_call | solution.py:313
  1.0 3.1 %collective-permute-start = (bf16[112,128]{1,0:T(8,128)(2,1)S(1)}, bf16[112,128]{1,0:T(8,128)(2,1)S(1)}, u32[]{:S(2)}, u32[]{:S(2)}) collective-permute-start(bf16[112,128]{1,0:T(8,128)(2,1)S(1)} %get-tuple-element.25), channel_id=1, source_target_pairs={{0,4},{1,5},{2,6},{3,7},{4,8},{5,9},{6,10},{7,11},{8,12},{9,13},{1... | collective-permute-start | bytes 86024 | tf_op jit(solution)/shard_map/ppermute | solution.py:305
  4.1 2.6 %collective-permute-start.1 = (bf16[112,128]{1,0:T(8,128)(2,1)S(1)}, bf16[112,128]{1,0:T(8,128)(2,1)S(1)}, u32[]{:S(2)}, u32[]{:S(2)}) collective-permute-start(bf16[112,128]{1,0:T(8,128)(2,1)S(1)} %get-tuple-element.25), channel_id=1, source_target_pairs={{0,8},{1,9},{2,10},{3,11},{4,12},{5,13},{6,14},{7,15},{8,0},{9,1},... | collective-permute-start | bytes 86024 | tf_op jit(solution)/shard_map/ppermute | solution.py:305
  6.7 1.3 %collective-permute-start.2 = (bf16[112,128]{1,0:T(8,128)(2,1)S(1)}, bf16[112,128]{1,0:T(8,128)(2,1)S(1)}, u32[]{:S(2)}, u32[]{:S(2)}) collective-permute-start(bf16[112,128]{1,0:T(8,128)(2,1)S(1)} %get-tuple-element.25), channel_id=1, source_target_pairs={{0,12},{1,13},{2,14},{3,15},{4,0},{5,1},{6,2},{7,3},{8,4},{9,5},{1... | collective-permute-start | bytes 86024 | tf_op jit(solution)/shard_map/ppermute | solution.py:305
  8.0 0.0 collective-permute-start.4
  8.0 0.0 collective-permute-done
  8.0 1.1 %collective-permute-done.1 = bf16[112,128]{1,0:T(8,128)(2,1)S(1)} collective-permute-done((bf16[112,128]{1,0:T(8,128)(2,1)S(1)}, bf16[112,128]{1,0:T(8,128)(2,1)S(1)}, u32[]{:S(2)}, u32[]{:S(2)}) %collective-permute-start.1) | collective-permute-done | bytes 28704 | tf_op jit(solution)/shard_map/ppermute | solution.py:305
  9.2 0.6 %collective-permute-start.5 = (bf16[3,112,128]{2,1,0:T(8,128)(2,1)S(1)}, bf16[3,112,128]{2,1,0:T(8,128)(2,1)S(1)}, u32[]{:S(2)}, u32[]{:S(2)}) collective-permute-start(bf16[3,112,128]{2,1,0:T(8,128)(2,1)S(1)} %pad_maximum_fusion.2), channel_id=1, source_target_pairs={{0,3},{1,2},{2,1},{3,0},{4,7},{5,6},{6,5},{7,4},{8,11},{9,10},{10,... | collective-permute-start | bytes 258056 | tf_op jit(solution)/shard_map/ppermute | solution.py:295
  9.7 0.8 %collective-permute-done.2 = bf16[112,128]{1,0:T(8,128)(2,1)S(1)} collective-permute-done((bf16[112,128]{1,0:T(8,128)(2,1)S(1)}, bf16[112,128]{1,0:T(8,128)(2,1)S(1)}, u32[]{:S(2)}, u32[]{:S(2)}) %collective-permute-start.2) | collective-permute-done | bytes 28704 | tf_op jit(solution)/shard_map/ppermute | solution.py:305
  10.5 0.4 %collective-permute-start.3 = (bf16[4,112,128]{2,1,0:T(8,128)(2,1)S(1)}, bf16[4,112,128]{2,1,0:T(8,128)(2,1)S(1)}, u32[]{:S(2)}, u32[]{:S(2)}) collective-permute-start(bf16[4,112,128]{2,1,0:T(8,128)(2,1)S(1)} %pad_maximum_fusion.tiles.own_tiles.part0), channel_id=1, source_target_pairs={{0,1},{1,0},{2,3},{3,2},{4,5},{5,4},{6,7},{7,6},{8,9},{9,8},{10,11... | collective-permute-start | bytes 344072 | tf_op jit(solution)/shard_map/ppermute | solution.py:295
  10.9 0.0 copy-done
  10.9 0.6 %first.1.before_ref = f32[800,128]{1,0:T(8,128)S(1)} custom-call(bf16[4,112,128]{2,1,0:T(8,128)(2,1)S(1)} %pad_maximum_fusion.tiles.own_tiles.part0, f32[128,512]{1,0:T(8,128)S(1)} %copy-done), custom_call_target="tpu_custom_call" | custom-call | flops 1024 | tf_op jit(solution)/shard_map/first/pallas_call | solution.py:313
  11.5 1.3 %weights.1.weights_ref = bf16[256,1536]{1,0:T(8,128)(2,1)S(1)} custom-call(f32[128,512]{1,0:T(8,128)} %refs_0_, f32[128,128]{1,0:T(8,128)} %refs_1_, f32[128,128]{1,0:T(8,128)} %refs_2_, f32[128,512]{1,0:T(8,128)} %refs_3_, f32[128,128]{1,0:T(8,128)} %refs_4_, f32[128,128]{1,0:T(8,128)} %refs_5_), custom_call_target="tpu_custom_call" | custom-call | flops 1000 | tf_op jit(solution)/shard_map/weights/pallas_call | solution.py:313
  12.8 0.0 collective-permute-done.4
  12.8 0.8 %collective-permute-done.5 = bf16[3,112,128]{2,1,0:T(8,128)(2,1)S(1)} collective-permute-done((bf16[3,112,128]{2,1,0:T(8,128)(2,1)S(1)}, bf16[3,112,128]{2,1,0:T(8,128)(2,1)S(1)}, u32[]{:S(2)}, u32[]{:S(2)}) %collective-permute-start.5) | collective-permute-done | bytes 86048 | tf_op jit(solution)/shard_map/ppermute | solution.py:295
  13.6 0.4 %collective-permute-start.6 = (bf16[4,112,128]{2,1,0:T(8,128)(2,1)S(1)}, bf16[4,112,128]{2,1,0:T(8,128)(2,1)S(1)}, u32[]{:S(2)}, u32[]{:S(2)}) collective-permute-start(bf16[4,112,128]{2,1,0:T(8,128)(2,1)S(1)} %pad_maximum_fusion.1.tiles.part2), channel_id=1, source_target_pairs={{0,1},{1,0},{2,3},{3,2},{4,5},{5,4},{6,7},{7,6},{8,9},{9,8},{10,11... | collective-permute-start | bytes 344072 | tf_op jit(solution)/shard_map/ppermute | solution.py:295
  14.0 0.0 collective-permute-done.3.tiles.part1
  14.0 0.7 %second.1 = (f32[800,128]{1,0:T(8,128)S(1)}, f32[400,128]{1,0:T(8,128)S(1)}, f32[400,128]{1,0:T(8,128)S(1)}, f32[400,128]{1,0:T(8,128)S(1)}) custom-call(bf16[4,112,128]{2,1,0:T(8,128)(2,1)S(1)} %collective-permute-done.3.tiles.part1, bf16[4,112,128]{2,1,0:T(8,128)(2,1)S(1)} %pad_maximum_fusion.tiles.own_tiles.part0, ...), custom_call_target="tpu_custom_call" | custom-call | flops 1024 | tf_op jit(solution)/shard_map/second/pallas_call | solution.py:313
  14.6 0.6 %third.1.before_ref = f32[800,128]{1,0:T(8,128)S(1)} custom-call(bf16[4,112,128]{2,1,0:T(8,128)(2,1)S(1)} %pad_maximum_fusion.1.tiles.part2, bf16[256,1536]{1,0:T(8,128)(2,1)S(1)} %weights.1.weights_ref, f32[800,128]{1,0:T(8,128)S(1)} %get-tuple-element.39.before_ref), custom_call_target="tpu_custom_call" | custom-call | flops 1024 | tf_op jit(solution)/shard_map/third/pallas_call | solution.py:313
  15.2 0.0 collective-permute-done.6.part3
  15.2 2.1 %last.1 = f32[10,10,128]{2,1,0:T(8,128)} custom-call(bf16[4,112,128]{2,1,0:T(8,128)(2,1)S(1)} %pad_maximum_fusion.tiles.own_tiles.part0, bf16[4,112,128]{2,1,0:T(8,128)(2,1)S(1)} %collective-permute-done.3.tiles.part1, bf16[4,112,128]{2,1,0:T(8,128)(2,1)S(1)} %pad_maximum_fusion.1.tiles.part2, bf16[4,112,128]{2,1,0:T(8,128)(2,1)S(1)} %collective-permute-done.6.part3, ...), custom_call_target="tpu_custom_call" | custom-call | flops 1024 | tf_op jit(solution)/shard_map/last/pallas_call | solution.py:313
  (3 shorter events, 0.0 us)
Async XLA Ops:
  0.0 10.9 %copy-start = (f32[128,512]{1,0:T(8,128)S(1)}, f32[128,512]{1,0:T(8,128)}, u32[]{:S(2)}) copy-start(f32[128,512]{1,0:T(8,128)} %refs_0_) | copy-start | bytes 786436
  1.0 7.0 %collective-permute-start = (bf16[112,128]{1,0:T(8,128)(2,1)S(1)}, bf16[112,128]{1,0:T(8,128)(2,1)S(1)}, u32[]{:S(2)}, u32[]{:S(2)}) collective-permute-start(bf16[112,128]{1,0:T(8,128)(2,1)S(1)} %get-tuple-element.25), channel_id=1, source_target_pairs={{0,4},{1,5},{2,6},{3,7},{4,8},{5,9},{6,10},{7,11},{8,12},{9,13},{1... | collective-permute-start | bytes 86024 | tf_op jit(solution)/shard_map/ppermute | solution.py:305
  4.1 5.1 %collective-permute-start.1 = (bf16[112,128]{1,0:T(8,128)(2,1)S(1)}, bf16[112,128]{1,0:T(8,128)(2,1)S(1)}, u32[]{:S(2)}, u32[]{:S(2)}) collective-permute-start(bf16[112,128]{1,0:T(8,128)(2,1)S(1)} %get-tuple-element.25), channel_id=1, source_target_pairs={{0,8},{1,9},{2,10},{3,11},{4,12},{5,13},{6,14},{7,15},{8,0},{9,1},... | collective-permute-start | bytes 86024 | tf_op jit(solution)/shard_map/ppermute | solution.py:305
  6.7 3.9 %collective-permute-start.2 = (bf16[112,128]{1,0:T(8,128)(2,1)S(1)}, bf16[112,128]{1,0:T(8,128)(2,1)S(1)}, u32[]{:S(2)}, u32[]{:S(2)}) collective-permute-start(bf16[112,128]{1,0:T(8,128)(2,1)S(1)} %get-tuple-element.25), channel_id=1, source_target_pairs={{0,12},{1,13},{2,14},{3,15},{4,0},{5,1},{6,2},{7,3},{8,4},{9,5},{1... | collective-permute-start | bytes 86024 | tf_op jit(solution)/shard_map/ppermute | solution.py:305
  8.0 4.8 %collective-permute-start.4 = (bf16[112,128]{1,0:T(8,128)(2,1)S(1)}, bf16[112,128]{1,0:T(8,128)(2,1)S(1)}, u32[]{:S(2)}, u32[]{:S(2)}) collective-permute-start(bf16[112,128]{1,0:T(8,128)(2,1)S(1)} %get-tuple-element.25), channel_id=1, source_target_pairs={{0,15},{1,14},{2,13},{3,12},{4,3},{5,2},{6,1},{7,0},{8,7},{9,6},{1... | collective-permute-start | bytes 86024 | tf_op jit(solution)/shard_map/ppermute | solution.py:305
  9.2 4.4 %collective-permute-start.5 = (bf16[3,112,128]{2,1,0:T(8,128)(2,1)S(1)}, bf16[3,112,128]{2,1,0:T(8,128)(2,1)S(1)}, u32[]{:S(2)}, u32[]{:S(2)}) collective-permute-start(bf16[3,112,128]{2,1,0:T(8,128)(2,1)S(1)} %pad_maximum_fusion.2), channel_id=1, source_target_pairs={{0,3},{1,2},{2,1},{3,0},{4,7},{5,6},{6,5},{7,4},{8,11},{9,10},{10,... | collective-permute-start | bytes 258056 | tf_op jit(solution)/shard_map/ppermute | solution.py:295
  10.5 3.4 %collective-permute-start.3 = (bf16[4,112,128]{2,1,0:T(8,128)(2,1)S(1)}, bf16[4,112,128]{2,1,0:T(8,128)(2,1)S(1)}, u32[]{:S(2)}, u32[]{:S(2)}) collective-permute-start(bf16[4,112,128]{2,1,0:T(8,128)(2,1)S(1)} %pad_maximum_fusion.tiles.own_tiles.part0), channel_id=1, source_target_pairs={{0,1},{1,0},{2,3},{3,2},{4,5},{5,4},{6,7},{7,6},{8,9},{9,8},{10,11... | collective-permute-start | bytes 344072 | tf_op jit(solution)/shard_map/ppermute | solution.py:295
  13.6 1.6 %collective-permute-start.6 = (bf16[4,112,128]{2,1,0:T(8,128)(2,1)S(1)}, bf16[4,112,128]{2,1,0:T(8,128)(2,1)S(1)}, u32[]{:S(2)}, u32[]{:S(2)}) collective-permute-start(bf16[4,112,128]{2,1,0:T(8,128)(2,1)S(1)} %pad_maximum_fusion.1.tiles.part2), channel_id=1, source_target_pairs={{0,1},{1,0},{2,3},{3,2},{4,5},{5,4},{6,7},{7,6},{8,9},{9,8},{10,11... | collective-permute-start | bytes 344072 | tf_op jit(solution)/shard_map/ppermute | solution.py:295

commit v9 on v8

--- a/solution.py
+++ b/solution.py
@@ -204,11 +204,9 @@
     add_terms(tiles, other_slot(), weights_ref[:, pl.ds(OUT_PROJ, 512)], before_ref, outer_ref, *scratch)
 
 
-def gate_kernel(tiles, own_tiles, own_ref, weights_ref, before_ref, outer_ref, centred_ref, half_gate_ref, valid_ref, *scratch):
-    add_terms(tiles, other_slot(), weights_ref[:, pl.ds(OUT_PROJ, 512)], before_ref, outer_ref, *scratch[:-1])
-    lines_ref = scratch[-1]
+def gate_kernel(tiles, own_ref, weights_ref, centred_ref, half_gate_ref, valid_ref, lines_ref):
     for slot in range(SPLIT):
-        to_lines(lines_ref, 0, own_tiles[slot].astype(jnp.float32), slot, SPLIT, WIDTH)
+        to_lines(lines_ref, 0, tiles[slot].astype(jnp.float32), slot, SPLIT, WIDTH)
     centred, valid = split_lines(lines_ref[...])
     centred_ref[...] = centred
     valid_ref[...] = jnp.where(valid, 1.0, 0.0)
@@ -343,14 +341,14 @@
     weights = call(
         weights_kernel, "weights", 1000, pltpu.VMEM((2 * 128, WEIGHTS), jnp.bfloat16), [], *weights, grant=None
     )
-    aslant, swapped_early, outer, weights = lax.optimization_barrier((aslant, swapped_early, outer, weights))
+    weights = in_vmem(weights)
+    centred0, gate0, valid0 = call(
+        gate_kernel, "gate", cost, (lines, lines, lines), [(LENGTH, 128)], in_vmem(part0), in_vmem(own), weights
+    )
+    aslant, swapped_early, outer, gate0 = lax.optimization_barrier((aslant, swapped_early, outer, gate0))
     part2 = jnp.concatenate([swapped_early, aslant[None]])
-    weights = in_vmem(weights)
     part1 = swapped(part0, 0, 1)
-    outer, centred0, gate0, valid0 = call(
-        gate_kernel, "second", cost, (sums, lines, lines, lines), work + [(LENGTH, 128)],
-        *map(in_vmem, (part1, part0, own)), weights, in_vmem(outer),
-    )
+    outer = call(next_kernel, "second", cost, sums, work, in_vmem(part1), weights, in_vmem(outer))
     part3 = swapped(part2, 0, 1)
     outer = call(next_kernel, "third", cost, sums, work, in_vmem(part2), weights, in_vmem(outer))
     part3, outer = lax.optimization_barrier((part3, outer))

time: 17.6 us -> 17.5 us (level)
  waiting for transfers between devices: 2.74 us -> 2.47 us
  Pallas kernels: 6.22 us -> 6.42 us
    ppermute x3, waiting for transfers between devices: 0.8 us -> 0.54 us  [swapped(): return lax.ppermute(value, ('row', 'col'), pairs)]
    pallas_call x6 -> x7, Pallas kernels: 6.22 us -> 6.42 us  [call(): pl.pallas_call(kernel, out_shape=out, scratch_shapes=[pltpu.VMEM(one, jnp...]
  transfers between devices with their start and end apart: 7 -> 7, of which waited for: 3 -> 3; matrix products, arithmetic and copies ran while one was open for 0% -> 0% of each run, Pallas kernels for 18% -> 19%
where the time goes in v9:
time: 17.5 us; the launch traced here: 17.3 us
  starting transfers between devices  8.31 us (47%)
  Pallas kernels  6.42 us (37%)
  waiting for transfers between devices  2.47 us (14%)
    ppermute x4, starting transfers between devices, shifted(): return lax.ppermute(value, ('row', 'col'), pairs)  7.02 us
    pallas_call x7, Pallas kernels, call(): pl.pallas_call(kernel, out_shape=out, scratch_shapes=[pltpu.VMEM(one, jnp...  6.42 us
    ppermute x4, waiting for transfers between devices, shifted(): return lax.ppermute(value, ('row', 'col'), pairs)  1.93 us
    ppermute x3, starting transfers between devices, swapped(): return lax.ppermute(value, ('row', 'col'), pairs)  1.29 us
    ppermute x3, waiting for transfers between devices, swapped(): return lax.ppermute(value, ('row', 'col'), pairs)  0.54 us
  transfers between devices with their start and end apart: 7, of which 3 were waited for; matrix products, arithmetic and copies ran while one was open for 0% of the time, Pallas kernels for 19%

profile of v9, /device:TPU:0, one launch (start us, length us, event | category | flops | bytes accessed | tf_op | source)
XLA Modules:
  0.0 17.3 jit_solution(7512315833204796374)
XLA Ops:
  0.0 0.0 copy-start
  0.0 1.0 %pack.1 = (bf16[112,128]{1,0:T(8,128)(2,1)S(1)}, f32[112,128]{1,0:T(8,128)S(1)}) custom-call(f32[10,10,128]{2,1,0:T(8,128)} %pair_ref.1, s32[10,10]{1,0:T(8,128)} %mask_ref.1), custom_call_target="tpu_custom_call" | custom-call | flops 1000 | tf_op jit(solution)/shard_map/pack/pallas_call | solution.py:311
  1.0 3.1 %collective-permute-start = (bf16[112,128]{1,0:T(8,128)(2,1)S(1)}, bf16[112,128]{1,0:T(8,128)(2,1)S(1)}, u32[]{:S(2)}, u32[]{:S(2)}) collective-permute-start(bf16[112,128]{1,0:T(8,128)(2,1)S(1)} %get-tuple-element.24), channel_id=1, source_target_pairs={{0,4},{1,5},{2,6},{3,7},{4,8},{5,9},{6,10},{7,11},{8,12},{9,13},{1... | collective-permute-start | bytes 86024 | tf_op jit(solution)/shard_map/ppermute | solution.py:303
  4.1 2.6 %collective-permute-start.1 = (bf16[112,128]{1,0:T(8,128)(2,1)S(1)}, bf16[112,128]{1,0:T(8,128)(2,1)S(1)}, u32[]{:S(2)}, u32[]{:S(2)}) collective-permute-start(bf16[112,128]{1,0:T(8,128)(2,1)S(1)} %get-tuple-element.24), channel_id=1, source_target_pairs={{0,8},{1,9},{2,10},{3,11},{4,12},{5,13},{6,14},{7,15},{8,0},{9,1},... | collective-permute-start | bytes 86024 | tf_op jit(solution)/shard_map/ppermute | solution.py:303
  6.7 1.3 %collective-permute-start.2 = (bf16[112,128]{1,0:T(8,128)(2,1)S(1)}, bf16[112,128]{1,0:T(8,128)(2,1)S(1)}, u32[]{:S(2)}, u32[]{:S(2)}) collective-permute-start(bf16[112,128]{1,0:T(8,128)(2,1)S(1)} %get-tuple-element.24), channel_id=1, source_target_pairs={{0,12},{1,13},{2,14},{3,15},{4,0},{5,1},{6,2},{7,3},{8,4},{9,5},{1... | collective-permute-start | bytes 86024 | tf_op jit(solution)/shard_map/ppermute | solution.py:303
  8.0 0.0 collective-permute-start.4
  8.0 0.0 collective-permute-done
  8.0 1.1 %collective-permute-done.1 = bf16[112,128]{1,0:T(8,128)(2,1)S(1)} collective-permute-done((bf16[112,128]{1,0:T(8,128)(2,1)S(1)}, bf16[112,128]{1,0:T(8,128)(2,1)S(1)}, u32[]{:S(2)}, u32[]{:S(2)}) %collective-permute-start.1) | collective-permute-done | bytes 28704 | tf_op jit(solution)/shard_map/ppermute | solution.py:303
  9.2 0.6 %collective-permute-start.5 = (bf16[3,112,128]{2,1,0:T(8,128)(2,1)S(1)}, bf16[3,112,128]{2,1,0:T(8,128)(2,1)S(1)}, u32[]{:S(2)}, u32[]{:S(2)}) collective-permute-start(bf16[3,112,128]{2,1,0:T(8,128)(2,1)S(1)} %pad_maximum_fusion.2), channel_id=1, source_target_pairs={{0,3},{1,2},{2,1},{3,0},{4,7},{5,6},{6,5},{7,4},{8,11},{9,10},{10,... | collective-permute-start | bytes 258056 | tf_op jit(solution)/shard_map/ppermute | solution.py:293
  9.7 0.8 %collective-permute-done.2 = bf16[112,128]{1,0:T(8,128)(2,1)S(1)} collective-permute-done((bf16[112,128]{1,0:T(8,128)(2,1)S(1)}, bf16[112,128]{1,0:T(8,128)(2,1)S(1)}, u32[]{:S(2)}, u32[]{:S(2)}) %collective-permute-start.2) | collective-permute-done | bytes 28704 | tf_op jit(solution)/shard_map/ppermute | solution.py:303
  10.5 0.4 %collective-permute-start.3 = (bf16[4,112,128]{2,1,0:T(8,128)(2,1)S(1)}, bf16[4,112,128]{2,1,0:T(8,128)(2,1)S(1)}, u32[]{:S(2)}, u32[]{:S(2)}) collective-permute-start(bf16[4,112,128]{2,1,0:T(8,128)(2,1)S(1)} %pad_maximum_fusion.tiles.part0), channel_id=1, source_target_pairs={{0,1},{1,0},{2,3},{3,2},{4,5},{5,4},{6,7},{7,6},{8,9},{9,8},{10,11... | collective-permute-start | bytes 344072 | tf_op jit(solution)/shard_map/ppermute | solution.py:293
  10.9 0.0 copy-done
  10.9 0.6 %first.1.before_ref = f32[800,128]{1,0:T(8,128)S(1)} custom-call(bf16[4,112,128]{2,1,0:T(8,128)(2,1)S(1)} %pad_maximum_fusion.tiles.part0, f32[128,512]{1,0:T(8,128)S(1)} %copy-done), custom_call_target="tpu_custom_call" | custom-call | flops 1024 | tf_op jit(solution)/shard_map/first/pallas_call | solution.py:311
  11.5 1.3 %weights.1.weights_ref = bf16[256,1536]{1,0:T(8,128)(2,1)S(1)} custom-call(f32[128,512]{1,0:T(8,128)} %refs_0_, f32[128,128]{1,0:T(8,128)} %refs_1_, f32[128,128]{1,0:T(8,128)} %refs_2_, f32[128,512]{1,0:T(8,128)} %refs_3_, f32[128,128]{1,0:T(8,128)} %refs_4_, f32[128,128]{1,0:T(8,128)} %refs_5_), custom_call_target="tpu_custom_call" | custom-call | flops 1000 | tf_op jit(solution)/shard_map/weights/pallas_call | solution.py:311
  12.8 0.3 %gate.1 = (f32[400,128]{1,0:T(8,128)S(1)}, f32[400,128]{1,0:T(8,128)S(1)}, f32[400,128]{1,0:T(8,128)S(1)}) custom-call(bf16[4,112,128]{2,1,0:T(8,128)(2,1)S(1)} %pad_maximum_fusion.tiles.part0, f32[112,128]{1,0:T(8,128)S(1)} %get-tuple-element.27.own_ref, bf16[256,1536]{1,0:T(8,128)(2,1)S(1)} %weights.1.weights_ref), custom_call_target="tpu_custom_call" | custom-call | flops 1024 | tf_op jit(solution)/shard_map/gate/pallas_call | solution.py:311
  13.1 0.0 collective-permute-done.4
  13.1 0.5 %collective-permute-done.5 = bf16[3,112,128]{2,1,0:T(8,128)(2,1)S(1)} collective-permute-done((bf16[3,112,128]{2,1,0:T(8,128)(2,1)S(1)}, bf16[3,112,128]{2,1,0:T(8,128)(2,1)S(1)}, u32[]{:S(2)}, u32[]{:S(2)}) %collective-permute-start.5) | collective-permute-done | bytes 86048 | tf_op jit(solution)/shard_map/ppermute | solution.py:293
  13.6 0.4 %collective-permute-start.6 = (bf16[4,112,128]{2,1,0:T(8,128)(2,1)S(1)}, bf16[4,112,128]{2,1,0:T(8,128)(2,1)S(1)}, u32[]{:S(2)}, u32[]{:S(2)}) collective-permute-start(bf16[4,112,128]{2,1,0:T(8,128)(2,1)S(1)} %pad_maximum_fusion.1.tiles.part2), channel_id=1, source_target_pairs={{0,1},{1,0},{2,3},{3,2},{4,5},{5,4},{6,7},{7,6},{8,9},{9,8},{10,11... | collective-permute-start | bytes 344072 | tf_op jit(solution)/shard_map/ppermute | solution.py:293
  14.0 0.0 collective-permute-done.3.tiles.part1
  14.0 0.6 %second.1.before_ref = f32[800,128]{1,0:T(8,128)S(1)} custom-call(bf16[4,112,128]{2,1,0:T(8,128)(2,1)S(1)} %collective-permute-done.3.tiles.part1, bf16[256,1536]{1,0:T(8,128)(2,1)S(1)} %weights.1.weights_ref, f32[800,128]{1,0:T(8,128)S(1)} %first.1.before_ref), custom_call_target="tpu_custom_call" | custom-call | flops 1024 | tf_op jit(solution)/shard_map/second/pallas_call | solution.py:311
  14.6 0.6 %third.1.before_ref = f32[800,128]{1,0:T(8,128)S(1)} custom-call(bf16[4,112,128]{2,1,0:T(8,128)(2,1)S(1)} %pad_maximum_fusion.1.tiles.part2, bf16[256,1536]{1,0:T(8,128)(2,1)S(1)} %weights.1.weights_ref, f32[800,128]{1,0:T(8,128)S(1)} %second.1.before_ref), custom_call_target="tpu_custom_call" | custom-call | flops 1024 | tf_op jit(solution)/shard_map/third/pallas_call | solution.py:311
  15.2 0.0 collective-permute-done.6.part3
  15.2 2.2 %last.1 = f32[10,10,128]{2,1,0:T(8,128)} custom-call(bf16[4,112,128]{2,1,0:T(8,128)(2,1)S(1)} %pad_maximum_fusion.tiles.part0, bf16[4,112,128]{2,1,0:T(8,128)(2,1)S(1)} %collective-permute-done.3.tiles.part1, bf16[4,112,128]{2,1,0:T(8,128)(2,1)S(1)} %pad_maximum_fusion.1.tiles.part2, bf16[4,112,128]{2,1,0:T(8,128)(2,1)S(1)} %collective-permute-done.6.part3, ...), custom_call_target="tpu_custom_call" | custom-call | flops 1024 | tf_op jit(solution)/shard_map/last/pallas_call | solution.py:311
  (3 shorter events, 0.0 us)
Async XLA Ops:
  0.0 10.9 %copy-start = (f32[128,512]{1,0:T(8,128)S(1)}, f32[128,512]{1,0:T(8,128)}, u32[]{:S(2)}) copy-start(f32[128,512]{1,0:T(8,128)} %refs_0_) | copy-start | bytes 786436
  1.0 7.0 %collective-permute-start = (bf16[112,128]{1,0:T(8,128)(2,1)S(1)}, bf16[112,128]{1,0:T(8,128)(2,1)S(1)}, u32[]{:S(2)}, u32[]{:S(2)}) collective-permute-start(bf16[112,128]{1,0:T(8,128)(2,1)S(1)} %get-tuple-element.24), channel_id=1, source_target_pairs={{0,4},{1,5},{2,6},{3,7},{4,8},{5,9},{6,10},{7,11},{8,12},{9,13},{1... | collective-permute-start | bytes 86024 | tf_op jit(solution)/shard_map/ppermute | solution.py:303
  4.1 5.1 %collective-permute-start.1 = (bf16[112,128]{1,0:T(8,128)(2,1)S(1)}, bf16[112,128]{1,0:T(8,128)(2,1)S(1)}, u32[]{:S(2)}, u32[]{:S(2)}) collective-permute-start(bf16[112,128]{1,0:T(8,128)(2,1)S(1)} %get-tuple-element.24), channel_id=1, source_target_pairs={{0,8},{1,9},{2,10},{3,11},{4,12},{5,13},{6,14},{7,15},{8,0},{9,1},... | collective-permute-start | bytes 86024 | tf_op jit(solution)/shard_map/ppermute | solution.py:303
  6.7 3.9 %collective-permute-start.2 = (bf16[112,128]{1,0:T(8,128)(2,1)S(1)}, bf16[112,128]{1,0:T(8,128)(2,1)S(1)}, u32[]{:S(2)}, u32[]{:S(2)}) collective-permute-start(bf16[112,128]{1,0:T(8,128)(2,1)S(1)} %get-tuple-element.24), channel_id=1, source_target_pairs={{0,12},{1,13},{2,14},{3,15},{4,0},{5,1},{6,2},{7,3},{8,4},{9,5},{1... | collective-permute-start | bytes 86024 | tf_op jit(solution)/shard_map/ppermute | solution.py:303
  8.0 5.1 %collective-permute-start.4 = (bf16[112,128]{1,0:T(8,128)(2,1)S(1)}, bf16[112,128]{1,0:T(8,128)(2,1)S(1)}, u32[]{:S(2)}, u32[]{:S(2)}) collective-permute-start(bf16[112,128]{1,0:T(8,128)(2,1)S(1)} %get-tuple-element.24), channel_id=1, source_target_pairs={{0,15},{1,14},{2,13},{3,12},{4,3},{5,2},{6,1},{7,0},{8,7},{9,6},{1... | collective-permute-start | bytes 86024 | tf_op jit(solution)/shard_map/ppermute | solution.py:303
  9.2 4.4 %collective-permute-start.5 = (bf16[3,112,128]{2,1,0:T(8,128)(2,1)S(1)}, bf16[3,112,128]{2,1,0:T(8,128)(2,1)S(1)}, u32[]{:S(2)}, u32[]{:S(2)}) collective-permute-start(bf16[3,112,128]{2,1,0:T(8,128)(2,1)S(1)} %pad_maximum_fusion.2), channel_id=1, source_target_pairs={{0,3},{1,2},{2,1},{3,0},{4,7},{5,6},{6,5},{7,4},{8,11},{9,10},{10,... | collective-permute-start | bytes 258056 | tf_op jit(solution)/shard_map/ppermute | solution.py:293
  10.5 3.4 %collective-permute-start.3 = (bf16[4,112,128]{2,1,0:T(8,128)(2,1)S(1)}, bf16[4,112,128]{2,1,0:T(8,128)(2,1)S(1)}, u32[]{:S(2)}, u32[]{:S(2)}) collective-permute-start(bf16[4,112,128]{2,1,0:T(8,128)(2,1)S(1)} %pad_maximum_fusion.tiles.part0), channel_id=1, source_target_pairs={{0,1},{1,0},{2,3},{3,2},{4,5},{5,4},{6,7},{7,6},{8,9},{9,8},{10,11... | collective-permute-start | bytes 344072 | tf_op jit(solution)/shard_map/ppermute | solution.py:293
  13.6 1.6 %collective-permute-start.6 = (bf16[4,112,128]{2,1,0:T(8,128)(2,1)S(1)}, bf16[4,112,128]{2,1,0:T(8,128)(2,1)S(1)}, u32[]{:S(2)}, u32[]{:S(2)}) collective-permute-start(bf16[4,112,128]{2,1,0:T(8,128)(2,1)S(1)} %pad_maximum_fusion.1.tiles.part2), channel_id=1, source_target_pairs={{0,1},{1,0},{2,3},{3,2},{4,5},{5,4},{6,7},{7,6},{8,9},{9,8},{10,11... | collective-permute-start | bytes 344072 | tf_op jit(solution)/shard_map/ppermute | solution.py:293
